TPU v7x, 32 devices: a whole 2x2x4 slice. The times are simulated.
32 devices in a mesh: bins: 8 (over z, x), xy: 4 (over y, core).
Axes of the slice: x: 2, y: 2, z: 4, core: 2. Of those that a mesh axis runs over, the one named last changes fastest.
Arguments:
- conc: float32 [8, 128, 16, 256], P('bins', None, 'xy'), may hold values from 0.05 to 2
- vel_x: float32 [8, 16, 256], P('bins', 'xy'), may hold values from -0.3 to 0.3
- vel_y: float32 [8, 16, 256], P('bins', 'xy'), may hold values from -0.3 to 0.3
- sea_mask: int32 [16, 256], P('xy'), may hold values 0 or 1
- settle: float32 [128], replicated, may hold values from 0.05 to 0.6
- size_bin_kernel_class: int32 [128], replicated, may hold values from 0 to 7
- aggregate_upward_factor: float32 [8], replicated, may hold values from 0.25 to 2
- agg_down: float32 [8], replicated, may hold values from 0.25 to 2
- break_rate: float32 [8], replicated, may hold values from 0.05 to 0.5
Outputs:
- conc_next: float32 [8, 128, 16, 256], P('bins', None, 'xy')
All inputs are finite; a program needn't handle non-finite values. No bound on the sum of `sea_mask` on one device may be relied on, other than what follows from the above.
Results may differ from a plain program's by a relative error of at most 0.00007.
Values sent between devices are 32-bit elements; how exact they have to be, the bound alone decides.
No kernel may reach another device: no remote copies, remote signals or barrier semaphores. Data moves between devices by JAX's collectives and lax.ppermute only.
A program may use at most 64 MiB of HBM per device.

v0:
```python
import jax
import jax.numpy as jnp
from jax import lax
from jax.sharding import PartitionSpec as P

NB = 128
NCLS = 8
HSUB = 2
VERTICAL_SUBSTEP = 2


h_diffusion = 0.2
v_diffusion = 0.2
step_duration = 0.5
collide_scale = 2.0


def extended(cells, sides, width):
    for axis, dim in sides:
        count = lax.axis_size(axis)
        ends = count - 1
        head = lax.slice_in_dim(cells, 0, width, axis=dim)
        tail = lax.slice_in_dim(cells, cells.shape[dim] - width, cells.shape[dim], axis=dim)
        cells = jnp.concatenate(
            [
                lax.ppermute(tail, axis, [(i, (i + 1) % count) for i in range(ends)]),
                cells,
                lax.ppermute(head, axis, [((i + 1) % count, i) for i in range(ends)]),
            ],
            axis=dim,
        )
    return cells


def prefix(value, axis, join, neutral, backward):
    count, mine = (lax.axis_size(axis), lax.axis_index(axis))
    pieces = jax.tree.map(lambda part: lax.all_gather(part, axis), value)
    if backward:
        pieces = jax.tree.map(lambda part: part[::-1], pieces)
        mine = count - 1 - mine
    running = jax.tree.map(
        lambda part, zero: jnp.full_like(part, 0) + jnp.asarray(zero, part.dtype), value, neutral
    )

    def lap(position, running):
        longer = join(running, jax.tree.map(lambda part: part[position], pieces))
        return jax.tree.map(lambda new, old: jnp.where(position < mine, new, old), longer, running)

    return lax.fori_loop(0, count - 1, lap, running)


def add_parts(earlier, later):
    return jax.tree.map(jnp.add, earlier, later)


def settle_mix(column, sink):
    flux = sink * column
    above = jnp.concatenate([jnp.zeros_like(flux[:1]), flux[:-1]], 0)
    upper = jnp.concatenate([column[:1], column[:-1]], 0)
    lower = jnp.concatenate([column[1:], column[-1:]], 0)
    return column - flux + above + v_diffusion * (upper + lower - 2.0 * column)


def lookup(table, onehot):
    return jnp.dot(onehot, table, precision=lax.Precision.HIGHEST)[:, None, None]


def local(
    conc,
    vel_x,
    vel_y,
    sea_mask,
    settle,
    size_bin_kernel_class,
    aggregate_upward_factor,
    agg_down,
    break_rate,
):
    water = sea_mask.astype(jnp.float32)
    speed_x = vel_x[:, None]
    speed_y = vel_y[:, None]
    level = conc
    for unused_item in range(HSUB):
        padded = extended(level, (("xy", 2),), 1)
        east = padded[:, :, 2:, :]
        west = padded[:, :, :-2, :]
        side = jnp.pad(level, ((0, 0), (0, 0), (0, 0), (1, 1)))
        north = side[:, :, :, 2:]
        south = side[:, :, :, :-2]
        level = water * (
            level
            - 0.5 * speed_x * (east - west)
            - 0.5 * speed_y * (north - south)
            + h_diffusion * (east + west + north + south - 4.0 * level)
        )
    classes = jnp.arange(NCLS)
    count_bins = lax.axis_size("bins")
    local_size_bins = NB // count_bins
    first_bin = lax.axis_index("bins") * local_size_bins
    own_class = lax.dynamic_slice_in_dim(size_bin_kernel_class, first_bin, local_size_bins)
    onehot = (own_class[:, None] == classes[None, :]).astype(jnp.float32)
    sink = lax.dynamic_slice_in_dim(settle, first_bin, local_size_bins)[:, None, None]
    bin_index = first_bin + jnp.arange(local_size_bins)
    block = lax.all_to_all(level, "bins", split_axis=1, concat_axis=0, tiled=True)
    for unused_item in range(VERTICAL_SUBSTEP):
        block = settle_mix(block, sink)
    up_rate = lookup(aggregate_upward_factor, onehot)
    down_rate = lookup(agg_down, onehot)
    brk_rate = lookup(break_rate, onehot)
    weight = (1.0 / jnp.maximum(bin_index, 1).astype(jnp.float32))[:, None, None]
    broken = (bin_index >= 1).astype(jnp.float32)[:, None, None]
    up_terms = up_rate * block
    down_terms = down_rate * block
    fragmentation_terms = brk_rate * block * weight
    up_own = jnp.sum(up_terms, 1)
    down_own = jnp.sum(down_terms, 1)
    frag_own = jnp.sum(fragmentation_terms, 1)
    empty = jnp.zeros_like(up_own)
    up_lower = prefix(up_own, "bins", add_parts, empty, False)
    down_higher, frag_higher = prefix((down_own, frag_own), "bins", add_parts, (empty, empty), True)
    lower_sum = up_lower[:, None] + jnp.cumsum(up_terms, 1) - up_terms
    higher_sum = down_higher[:, None] + down_own[:, None] - jnp.cumsum(down_terms, 1)
    frag_sum = frag_higher[:, None] + frag_own[:, None] - jnp.cumsum(fragmentation_terms, 1)
    concentration_change = (
        collide_scale / NB * (down_rate * block * lower_sum - up_rate * block * higher_sum)
    )
    result = block + step_duration * (concentration_change + frag_sum - brk_rate * broken * block)
    result = lax.all_to_all(result, "bins", split_axis=0, concat_axis=1, tiled=True)
    return result


def solution(mesh):
    placed = (
        P("bins", None, "xy", None),
        P("bins", "xy", None),
        P("bins", "xy", None),
        P("xy", None),
        P(),
        P(),
        P(),
        P(),
        P(),
    )
    return jax.shard_map(
        local, mesh=mesh, in_specs=placed, out_specs=P("bins", None, "xy", None), check_vma=False
    )
```

profile of v0, /device:TPU:0, one launch (start us, length us, event | category | flops | bytes accessed | tf_op | source)
XLA Modules:
  0.0 150.3 jit_solution(8229547005319806867)
XLA Ops:
  0.0 1.2 copy.94
  1.2 1.3 collective-permute-start
  2.5 3.0 %collective-permute-start.1 = (f32[1,128,1,256]{3,1,2,0:T(8,128)S(1)}, f32[1,128,1,256]{3,1,2,0:T(8,128)S(1)}, u32[]{:S(2)}, u32[]{:S(2)}) collective-permute-start(f32[1,128,1,256]{3,1,2,0:T(8,128)S(1)} %get-tuple-element.271), channel_id=1, source_target_pairs={{0,1},{1,2},{2,3},{4,5},{5,6},{6,7},{8,9},{9,10},{10,11},{12,13},{... | collective-permute-start | bytes 393224 | tf_op jit(solution)/shard_map/ppermute | solution.py:26
  5.6 0.9 collective-permute-done.1
  6.5 0.4 add_multiply_fusion.1
  6.9 1.3 collective-permute-start.2
  8.2 6.1 %collective-permute-start.3 = (f32[1,128,1,256]{3,1,2,0:T(8,128)S(1)}, f32[1,128,1,256]{3,1,2,0:T(8,128)S(1)}, u32[]{:S(2)}, u32[]{:S(2)}) collective-permute-start(f32[1,128,1,256]{3,1,2,0:T(8,128)S(1)} %get-tuple-element.269), channel_id=1, source_target_pairs={{0,1},{1,2},{2,3},{4,5},{5,6},{6,7},{8,9},{9,10},{10,11},{12,13},{... | collective-permute-start | bytes 393224 | tf_op jit(solution)/shard_map/ppermute | solution.py:26
  14.3 1.0 collective-permute-done.3
  15.3 0.4 add_multiply_fusion
  15.7 1.3 copy.97
  17.0 5.8 %all-to-all-start = ((f32[1,128,4,256]{3,0,2,1:T(1,128)}), f32[1,128,4,256]{3,0,2,1:T(1,128)S(1)}, u32[]{:S(2)}, u32[]{:S(2)}) async-start(f32[1,128,4,256]{3,0,2,1:T(1,128)} %copy.97), calls=%async_computation | async-start | bytes 1048576 | tf_op jit(solution)/shard_map/all_to_all | solution.py:104
  22.8 0.6 copy-done.4
  23.6 0.6 copy-done.5
  24.2 0.6 copy-done.6
  25.1 0.5 copy-done.7
  25.9 11.1 %all-to-all-done = f32[1,128,4,256]{3,0,2,1:T(1,128)S(1)} async-done(((f32[1,128,4,256]{3,0,2,1:T(1,128)}), f32[1,128,4,256]{3,0,2,1:T(1,128)S(1)}, u32[]{:S(2)}, u32[]{:S(2)}) %all-to-all-start) | async-done | bytes 524320 | tf_op jit(solution)/shard_map/all_to_all | solution.py:104
  38.1 0.6 broadcast_multiply_fusion
  38.9 0.5 fusion.15
  39.4 30.7 %all-gather.1 = f32[64,4,256]{2,1,0:T(4,128)S(1)} all-gather(f32[8,4,256]{2,1,0:T(4,128)S(1)} %copy.110), channel_id=3, replica_groups=mesh['bins'=8,'xy'=4] {'bins'}, dimensions={0}, use_global_device_ids=true | all-gather | bytes 294912 | tf_op jit(solution)/shard_map/all_gather | solution.py:37
  70.2 30.9 %all-gather.2 = f32[64,4,256]{2,1,0:T(4,128)S(1)} all-gather(f32[8,4,256]{2,1,0:T(4,128)S(1)} %copy.111), channel_id=4, replica_groups=mesh['bins'=8,'xy'=4] {'bins'}, dimensions={0}, use_global_device_ids=true | all-gather | bytes 294912 | tf_op jit(solution)/shard_map/all_gather | solution.py:37
  101.2 0.4 while.31
  101.7 31.0 %all-gather = f32[64,4,256]{2,1,0:T(4,128)S(1)} all-gather(f32[8,4,256]{2,1,0:T(4,128)S(1)} %copy.108), channel_id=2, replica_groups=mesh['bins'=8,'xy'=4] {'bins'}, dimensions={0}, use_global_device_ids=true | all-gather | bytes 294912 | tf_op jit(solution)/shard_map/all_gather | solution.py:37
  134.0 15.2 %all_to_all.24 = f32[8,16,4,256]{3,1,2,0:T(8,128)S(1)} all-to-all(f32[8,16,4,256]{3,1,2,0:T(8,128)S(1)} %copy.114), channel_id=1, replica_groups=mesh['bins'=8,'xy'=4] {'bins'}, dimensions={0} | all-to-all | bytes 1048576 | tf_op jit(solution)/shard_map/all_to_all | solution.py:128
  149.2 1.1 copy.116
  (63 shorter events, 3.8 us)
Async XLA Ops:
  0.0 25.7 %copy-start = (f32[8]{0:T(128)S(1)}, f32[8]{0:T(128)}, u32[]{:S(2)}) copy-start(f32[8]{0:T(128)} %param.21) | copy-start | bytes 100
  1.2 4.4 %copy-start.1 = (s32[4,256]{1,0:T(4,128)S(1)}, s32[4,256]{1,0:T(4,128)}, u32[]{:S(2)}) copy-start(s32[4,256]{1,0:T(4,128)} %param.16) | copy-start | bytes 12292
  1.2 4.4 %collective-permute-start = (f32[1,128,1,256]{3,1,2,0:T(8,128)S(1)}, f32[1,128,1,256]{3,1,2,0:T(8,128)S(1)}, u32[]{:S(2)}, u32[]{:S(2)}) collective-permute-start(f32[1,128,1,256]{3,1,2,0:T(8,128)S(1)} %get-tuple-element.272), channel_id=1, source_target_pairs={{1,0},{2,1},{3,2},{5,4},{6,5},{7,6},{9,8},{10,9},{11,10},{13,12},{... | collective-permute-start | bytes 393224 | tf_op jit(solution)/shard_map/ppermute | solution.py:28
  2.5 3.1 %copy-start.2 = (f32[1,4,256]{2,1,0:T(4,128)S(1)}, f32[1,4,256]{2,1,0:T(4,128)}, u32[]{:S(2)}) copy-start(f32[1,4,256]{2,1,0:T(4,128)} %param.15) | copy-start | bytes 12292
  2.5 3.1 %copy-start.3 = (f32[1,4,256]{2,1,0:T(4,128)S(1)}, f32[1,4,256]{2,1,0:T(4,128)}, u32[]{:S(2)}) copy-start(f32[1,4,256]{2,1,0:T(4,128)} %param.14) | copy-start | bytes 12292
  2.5 4.0 %collective-permute-start.1 = (f32[1,128,1,256]{3,1,2,0:T(8,128)S(1)}, f32[1,128,1,256]{3,1,2,0:T(8,128)S(1)}, u32[]{:S(2)}, u32[]{:S(2)}) collective-permute-start(f32[1,128,1,256]{3,1,2,0:T(8,128)S(1)} %get-tuple-element.271), channel_id=1, source_target_pairs={{0,1},{1,2},{2,3},{4,5},{5,6},{6,7},{8,9},{9,10},{10,11},{12,13},{... | collective-permute-start | bytes 393224 | tf_op jit(solution)/shard_map/ppermute | solution.py:26
  6.9 7.4 %collective-permute-start.2 = (f32[1,128,1,256]{3,1,2,0:T(8,128)S(1)}, f32[1,128,1,256]{3,1,2,0:T(8,128)S(1)}, u32[]{:S(2)}, u32[]{:S(2)}) collective-permute-start(f32[1,128,1,256]{3,1,2,0:T(8,128)S(1)} %get-tuple-element.270), channel_id=1, source_target_pairs={{1,0},{2,1},{3,2},{5,4},{6,5},{7,6},{9,8},{10,9},{11,10},{13,12},{... | collective-permute-start | bytes 393224 | tf_op jit(solution)/shard_map/ppermute | solution.py:28
  8.2 7.1 %collective-permute-start.3 = (f32[1,128,1,256]{3,1,2,0:T(8,128)S(1)}, f32[1,128,1,256]{3,1,2,0:T(8,128)S(1)}, u32[]{:S(2)}, u32[]{:S(2)}) collective-permute-start(f32[1,128,1,256]{3,1,2,0:T(8,128)S(1)} %get-tuple-element.269), channel_id=1, source_target_pairs={{0,1},{1,2},{2,3},{4,5},{5,6},{6,7},{8,9},{9,10},{10,11},{12,13},{... | collective-permute-start | bytes 393224 | tf_op jit(solution)/shard_map/ppermute | solution.py:26
  17.0 20.0 %all-to-all-start = ((f32[1,128,4,256]{3,0,2,1:T(1,128)}), f32[1,128,4,256]{3,0,2,1:T(1,128)S(1)}, u32[]{:S(2)}, u32[]{:S(2)}) async-start(f32[1,128,4,256]{3,0,2,1:T(1,128)} %copy.97), calls=%async_computation | async-start | bytes 1048576 | tf_op jit(solution)/shard_map/all_to_all | solution.py:104
  22.8 0.7 copy-start.4
  23.5 0.7 copy-start.5
  24.2 0.7 copy-start.6
  24.9 0.7 copy-start.7
where the time goes:
time: 151 us; the launch traced here: 150 us
  blocking collectives  108 us (72%)
  starting transfers between devices  17.5 us (12%)
  waiting for transfers between devices  12.9 us (9%)
  local copies, waits for them, and re-layouts  7.37 us (5%)
  other arithmetic  3.41 us (2%)
    all_gather x3, blocking collectives, prefix(): pieces = jax.tree.map(lambda part: lax.all_gather(part, axis), value)  92.7 us
    all_to_all x1, blocking collectives, local(): lax.all_to_all(result, 'bins', split_axis=0, concat_axis=1, tiled=True)  15.2 us
    all_to_all x1, waiting for transfers between devices, local(): lax.all_to_all(level, 'bins', split_axis=1, concat_axis=0, tiled=True)  11.1 us
    ppermute x2, starting transfers between devices, extended(): lax.ppermute(tail, axis, [(i, (i + 1) % count) for i in range(ends)])  9.12 us
    all_to_all x1, starting transfers between devices, local(): lax.all_to_all(level, 'bins', split_axis=1, concat_axis=0, tiled=True)  5.81 us
    unnamed x17, local copies, waits for them, and re-layouts  3.53 us
  transfers between devices with their start and end apart: 5, of which 3 were waited for; matrix products, arithmetic and copies ran while one was open for 0% of the time, Pallas kernels for 0%

commit v1 on v0

v1 whole, which is shorter than its diff:
```python
import jax
import jax.numpy as jnp
from jax import lax
from jax.sharding import PartitionSpec as P

NB = 128
NCLS = 8

h_diffusion = 0.2
v_diffusion = 0.2
step_duration = 0.5
collide_scale = 2.0


def swap(value, axis, reach, parity):
    count = lax.axis_size(axis)
    pairs = []
    for low in range(count - reach):
        if (low // reach) % 2 == parity:
            pairs += [(low, low + reach), (low + reach, low)]
    return lax.ppermute(value, axis, pairs)


def substep(padded, speed_x, speed_y, water):
    level = padded[1:-1]
    east = padded[2:]
    west = padded[:-2]
    side = jnp.pad(level, ((0, 0), (0, 0), (1, 1)))
    north = side[:, :, 2:]
    south = side[:, :, :-2]
    return water * (
        level
        - 0.5 * speed_x * (east - west)
        - 0.5 * speed_y * (north - south)
        + h_diffusion * (east + west + north + south - 4.0 * level)
    )


def horizontal(rows, speed_x, speed_y, water):
    count, bins, cols = rows.shape
    odd = lax.axis_index("xy") % 2 == 1

    def message(low, high):
        edge = rows[:2] if low else rows[count - 2 :]
        at = 0 if low else count - 1
        aux = jnp.stack([speed_x[at], speed_y[at], water[at]])
        return jnp.concatenate([edge.reshape(2 * bins, cols), jnp.pad(aux, ((0, 5), (0, 0)))], 0)

    low, high = message(True, False), message(False, True)
    got_a = swap(jnp.where(odd, low, high), "xy", 1, 0)
    got_b = swap(jnp.where(odd, high, low), "xy", 1, 1)
    above = jnp.where(odd, got_a, got_b)
    below = jnp.where(odd, got_b, got_a)

    def split(got):
        return got[: 2 * bins].reshape(2, bins, cols), got[2 * bins : 2 * bins + 3]

    top, top_aux = split(above)
    bottom, bottom_aux = split(below)
    ext = jnp.concatenate([top, rows, bottom], 0)
    aux = [
        jnp.concatenate([top_aux[i : i + 1], own, bottom_aux[i : i + 1]], 0)[:, None]
        for i, own in enumerate((speed_x, speed_y, water))
    ]
    once = substep(ext, *aux)
    return substep(once, *[part[1:-1] for part in aux])


def local(
    conc,
    vel_x,
    vel_y,
    sea_mask,
    settle,
    size_bin_kernel_class,
    aggregate_upward_factor,
    agg_down,
    break_rate,
):
    rows = jnp.transpose(conc[0], (1, 0, 2))
    water = sea_mask.astype(jnp.float32)
    moved = horizontal(rows, vel_x[0], vel_y[0], water)

    levels = lax.axis_size("bins")
    k = lax.axis_index("bins")
    odd = k % 2 == 1
    high_z = (k // 2) % 2 == 1
    fall = settle + v_diffusion
    rise = v_diffusion

    def keep(level):
        inner = (level > 0).astype(jnp.float32) + (level < levels - 1).astype(jnp.float32)
        return 1.0 - settle - v_diffusion * inner

    inner = (k > 0).astype(jnp.float32) + (k < levels - 1).astype(jnp.float32)
    on_self = keep(k) * keep(k) + inner * fall * rise
    on_up2 = fall * fall
    on_down2 = jnp.full_like(settle, rise * rise)
    on_up1 = fall * (keep(k + 1) + keep(k))
    on_down1 = rise * (keep(k - 1) + keep(k))

    def col(vector):
        return vector[None, :, None]

    half = NB // 2
    c_a, c_b = moved[:, :half], moved[:, half:]

    a0 = swap(c_a, "bins", 2, 0)
    a1 = swap(c_a, "bins", 2, 1)
    b_pair = swap(c_b, "bins", 1, 0)

    pair_own = jnp.where(odd, on_down1, on_up1)
    pair_far = jnp.where(odd, fall * (keep(k - 1) + keep(k - 2)), rise * (keep(k + 1) + keep(k + 2)))
    zero = jnp.zeros_like(settle)
    in_first = odd == high_z
    pair_0 = jnp.where(in_first, pair_far, zero)
    pair_1 = jnp.where(in_first, zero, pair_far)
    send_pair = (
        col(pair_own[:half]) * c_a + col(pair_0[:half]) * a0 + col(pair_1[:half]) * a1
    )
    up_pair = jnp.where(odd, zero, fall * (keep(k + 2) + keep(k + 1)))
    down_pair = jnp.where(odd, rise * (keep(k - 2) + keep(k - 1)), zero)
    send0 = col(jnp.where(high_z, on_down2, on_up2)[half:]) * c_b + col(jnp.where(high_z, down_pair, up_pair)[half:]) * b_pair
    send1 = col(jnp.where(high_z, on_up2, on_down2)[half:]) * c_b + col(jnp.where(high_z, up_pair, down_pair)[half:]) * b_pair

    b0 = swap(send0, "bins", 2, 0)
    b1 = swap(send1, "bins", 2, 1)
    a_pair = swap(send_pair, "bins", 1, 0)

    far_0 = jnp.where(high_z, on_up2, on_down2)
    far_1 = jnp.where(high_z, on_down2, on_up2)
    sunk_a = col(on_self[:half]) * c_a + col(far_0[:half]) * a0 + col(far_1[:half]) * a1 + a_pair
    from_pair = jnp.where(odd, fall * (keep(k) + keep(k - 1)), rise * (keep(k) + keep(k + 1)))
    sunk_b = col(on_self[half:]) * c_b + col(from_pair[half:]) * b_pair + b0 + b1
    sunk = jnp.concatenate([sunk_a, sunk_b], 1)

    onehot = (size_bin_kernel_class[:, None] == jnp.arange(NCLS)[None, :]).astype(jnp.float32)

    def lookup(table):
        return jnp.sum(onehot * table[None, :], 1)

    up_rate = lookup(aggregate_upward_factor)
    down_rate = lookup(agg_down)
    brk_rate = lookup(break_rate)
    index = jnp.arange(NB)
    i, j = index[None, :], index[:, None]
    weight = 1.0 / jnp.maximum(index, 1).astype(jnp.float32)
    pairs = jnp.where(i < j, down_rate[:, None] * up_rate[None, :], 0.0) - jnp.where(
        i > j, up_rate[:, None] * down_rate[None, :], 0.0
    )
    pieces = jnp.where(i > j, (brk_rate * weight)[None, :], 0.0) - jnp.where(
        (i == j) & (j >= 1), brk_rate[:, None], 0.0
    )
    both = jnp.concatenate([pairs * (step_duration * collide_scale / NB), pieces * step_duration], 0)
    sums = jnp.einsum("ji,ric->rjc", both, sunk, precision=lax.Precision.HIGHEST)
    result = sunk + sunk * sums[:, :NB] + sums[:, NB:]
    return jnp.transpose(result, (1, 0, 2))[None]


def solution(mesh):
    placed = (
        P("bins", None, "xy", None),
        P("bins", "xy", None),
        P("bins", "xy", None),
        P("xy", None),
        P(),
        P(),
        P(),
        P(),
        P(),
    )
    return jax.shard_map(
        local, mesh=mesh, in_specs=placed, out_specs=P("bins", None, "xy", None), check_vma=False
    )
```

time: 151 us -> 46.5 us (0.31)
  the two profiles are of different devices: /device:TPU:0 before, /device:TPU:12 now
where the time goes in v1:
time: 46.5 us; the launch traced here: 46.2 us
  waiting for transfers between devices  23.3 us (50%)
  starting transfers between devices  12.7 us (27%)
  local copies, waits for them, and re-layouts  6.14 us (13%)
  other arithmetic  2.67 us (6%)
  matrix products  1.02 us (2%)
    ppermute x8, waiting for transfers between devices, swap(): return lax.ppermute(value, axis, pairs)  23.3 us
    ppermute x8, starting transfers between devices, swap(): return lax.ppermute(value, axis, pairs)  12.7 us
    unnamed x17, local copies, waits for them, and re-layouts  3.95 us
    mul x2, other arithmetic, substep(): water * (level - 0.5 * speed_x * (east - west) - 0.5 * speed_y * (north -...  1.37 us
    dot_general x1, matrix products, local(): jnp.einsum('ji,ric->rjc', both, sunk, precision=lax.Precision.HIGHEST)  1.02 us
    broadcast_in_dim x1, local copies, waits for them, and re-layouts, local(): return jnp.transpose(result, (1, 0, 2))[None]  1 us
  transfers between devices with their start and end apart: 8, of which 7 were waited for; matrix products, arithmetic and copies ran while one was open for 1% of the time, Pallas kernels for 0%

profile of v1, /device:TPU:12, one launch (start us, length us, event | category | flops | bytes accessed | tf_op | source)
XLA Modules:
  0.0 46.2 jit_solution(4223854684926991125)
XLA Ops:
  0.0 0.7 %copy-done.2 = s32[4,256]{1,0:T(4,128)S(1)} copy-done((s32[4,256]{1,0:T(4,128)S(1)}, s32[4,256]{1,0:T(4,128)}, u32[]{:S(2)}) %copy-start.2) | copy-done | bytes 4120
  0.7 0.7 %copy-done = f32[1,4,256]{2,1,0:T(4,128)S(1)} copy-done((f32[1,4,256]{2,1,0:T(4,128)S(1)}, f32[1,4,256]{2,1,0:T(4,128)}, u32[]{:S(2)}) %copy-start) | copy-done | bytes 4120
  1.4 1.2 %copy.20 = f32[1,128,4,256]{1,3,2,0:T(8,128)S(1)} copy(f32[1,128,4,256]{3,2,1,0:T(4,128)} %param.9) | data formatting | bytes 1048576 | tf_op args[0]
  3.1 2.5 %collective-permute-start.1 = (f32[264,256]{1,0:T(8,128)S(1)}, f32[264,256]{1,0:T(8,128)S(1)}, u32[]{:S(2)}, u32[]{:S(2)}) collective-permute-start(f32[264,256]{1,0:T(8,128)S(1)} %get-tuple-element.17), channel_id=1, source_target_pairs={{1,2},{2,1},{5,6},{6,5},{9,10},{10,9},{13,14},{14,13},{17,18},{18,... | collective-permute-start | bytes 811016 | tf_op jit(solution)/shard_map/ppermute | solution.py:21
  5.7 0.6 %copy-done.3 = f32[128]{0:T(128)S(1)} copy-done((f32[128]{0:T(128)S(1)}, f32[128]{0:T(128)}, u32[]{:S(2)}) %copy-start.3) | copy-done | bytes 536
  6.5 0.6 %copy-done.4 = f32[8]{0:T(128)S(1)} copy-done((f32[8]{0:T(128)S(1)}, f32[8]{0:T(128)}, u32[]{:S(2)}) %copy-start.4) | copy-done | bytes 56
  7.3 3.6 %collective-permute-done.1 = f32[264,256]{1,0:T(8,128)S(1)} collective-permute-done((f32[264,256]{1,0:T(8,128)S(1)}, f32[264,256]{1,0:T(8,128)S(1)}, u32[]{:S(2)}, u32[]{:S(2)}) %collective-permute-start.1) | collective-permute-done | bytes 270368 | tf_op jit(solution)/shard_map/ppermute | solution.py:21
  11.4 0.8 %add_multiply_fusion = f32[6,128,256]{1,2,0:T(8,128)S(1)} fusion(f32[6,128,256]{1,2,0:T(8,128)S(1)} %pad_maximum_fusion, f32[4,128,256]{1,2,0:T(8,128)S(1)} %bitcast.33, f32[2,128,256]{1,2,0:T(8,128)S(1)} %copy.23, f32[2,128,256]{1,2,0:T(8,128)S(1)} %copy.24, f32[6,256]{1,0:T(8,128)S(1)} %maximum_multiply_fusion.1, f32[6,256]{1,0:T(8,128)S(1)} %maximum_multiply_fusion, ...), kind=kLoop, calls=%fused_computation.6 | loop fusion | flops 3145728 | bytes 2639872 | tf_op jit(solution)/shard_map/mul | solution.py:31
  12.3 0.5 %add_multiply_fusion.1 = f32[4,128,256]{1,2,0:T(8,128)S(1)} fusion(f32[4,128,256]{1,2,0:T(8,128)S(1)} %slice.206, f32[6,128,256]{1,2,0:T(8,128)S(1)} %add_multiply_fusion, f32[4,256]{1,0:T(4,128)S(1)} %get-tuple-element.58, f32[4,256]{1,0:T(4,128)S(1)} %get-tuple-element.59, f32[4,256]{1,0:T(4,128)S(1)} %convert_element_type.37), kind=kLoop, calls=%fused_computation.15 | loop fusion | flops 1835008 | bytes 2109440 | tf_op jit(solution)/shard_map/mul | solution.py:31
  13.0 0.5 %collective-permute-start.2 = (f32[4,64,256]{1,2,0:T(8,128)S(1)}, f32[4,64,256]{1,2,0:T(8,128)S(1)}, u32[]{:S(2)}, u32[]{:S(2)}) collective-permute-start(f32[4,64,256]{1,2,0:T(8,128)S(1)} %get-tuple-element.21), channel_id=1, source_target_pairs={{0,8},{8,0},{4,12},{12,4},{16,24},{24,16},{20,28},{28,20},{1,9},{9... | collective-permute-start | bytes 786440 | tf_op jit(solution)/shard_map/ppermute | solution.py:21
  13.5 4.6 %collective-permute-start.3 = (f32[4,64,256]{1,2,0:T(8,128)S(1)}, f32[4,64,256]{1,2,0:T(8,128)S(1)}, u32[]{:S(2)}, u32[]{:S(2)}) collective-permute-start(f32[4,64,256]{1,2,0:T(8,128)S(1)} %get-tuple-element.21), channel_id=1, source_target_pairs={{8,16},{16,8},{12,20},{20,12},{9,17},{17,9},{13,21},{21,13},{10,18... | collective-permute-start | bytes 786440 | tf_op jit(solution)/shard_map/ppermute | solution.py:21
  18.1 1.6 %collective-permute-start.5 = (f32[4,64,256]{1,2,0:T(8,128)S(1)}, f32[4,64,256]{1,2,0:T(8,128)S(1)}, u32[]{:S(2)}, u32[]{:S(2)}) collective-permute-start(f32[4,64,256]{1,2,0:T(8,128)S(1)} %get-tuple-element.22), channel_id=1, source_target_pairs={{0,4},{4,0},{8,12},{12,8},{16,20},{20,16},{24,28},{28,24},{1,5},{5... | collective-permute-start | bytes 786440 | tf_op jit(solution)/shard_map/ppermute | solution.py:21
  19.9 2.3 %collective-permute-done.2 = f32[4,64,256]{1,2,0:T(8,128)S(1)} collective-permute-done((f32[4,64,256]{1,2,0:T(8,128)S(1)}, f32[4,64,256]{1,2,0:T(8,128)S(1)}, u32[]{:S(2)}, u32[]{:S(2)}) %collective-permute-start.2) | collective-permute-done | bytes 262176 | tf_op jit(solution)/shard_map/ppermute | solution.py:21
  22.3 3.0 %collective-permute-done.3 = f32[4,64,256]{1,2,0:T(8,128)S(1)} collective-permute-done((f32[4,64,256]{1,2,0:T(8,128)S(1)}, f32[4,64,256]{1,2,0:T(8,128)S(1)}, u32[]{:S(2)}, u32[]{:S(2)}) %collective-permute-start.3) | collective-permute-done | bytes 262176 | tf_op jit(solution)/shard_map/ppermute | solution.py:21
  25.3 5.4 %collective-permute-done.5 = f32[4,64,256]{1,2,0:T(8,128)S(1)} collective-permute-done((f32[4,64,256]{1,2,0:T(8,128)S(1)}, f32[4,64,256]{1,2,0:T(8,128)S(1)}, u32[]{:S(2)}, u32[]{:S(2)}) %collective-permute-start.5) | collective-permute-done | bytes 262176 | tf_op jit(solution)/shard_map/ppermute | solution.py:21
  30.7 0.3 multiply_add_fusion.2
  31.0 1.6 %collective-permute-start.4 = (f32[4,64,256]{1,2,0:T(8,128)S(1)}, f32[4,64,256]{1,2,0:T(8,128)S(1)}, u32[]{:S(2)}, u32[]{:S(2)}) collective-permute-start(f32[4,64,256]{1,2,0:T(8,128)S(1)} %get-tuple-element.20), channel_id=1, source_target_pairs={{0,4},{4,0},{8,12},{12,8},{16,20},{20,16},{24,28},{28,24},{1,5},{5... | collective-permute-start | bytes 786440 | tf_op jit(solution)/shard_map/ppermute | solution.py:21
  32.6 1.9 %collective-permute-start.7 = (f32[4,64,256]{1,2,0:T(8,128)S(1)}, f32[4,64,256]{1,2,0:T(8,128)S(1)}, u32[]{:S(2)}, u32[]{:S(2)}) collective-permute-start(f32[4,64,256]{1,2,0:T(8,128)S(1)} %get-tuple-element.13), channel_id=1, source_target_pairs={{8,16},{16,8},{12,20},{20,12},{9,17},{17,9},{13,21},{21,13},{10,18... | collective-permute-start | bytes 786440 | tf_op jit(solution)/shard_map/ppermute | solution.py:21
  34.7 5.5 %collective-permute-done.4 = f32[4,64,256]{1,2,0:T(8,128)S(1)} collective-permute-done((f32[4,64,256]{1,2,0:T(8,128)S(1)}, f32[4,64,256]{1,2,0:T(8,128)S(1)}, u32[]{:S(2)}, u32[]{:S(2)}) %collective-permute-start.4) | collective-permute-done | bytes 262176 | tf_op jit(solution)/shard_map/ppermute | solution.py:21
  40.3 1.5 %collective-permute-done.6 = f32[4,64,256]{1,2,0:T(8,128)S(1)} collective-permute-done((f32[4,64,256]{1,2,0:T(8,128)S(1)}, f32[4,64,256]{1,2,0:T(8,128)S(1)}, u32[]{:S(2)}, u32[]{:S(2)}) %collective-permute-start.6) | collective-permute-done | bytes 262176 | tf_op jit(solution)/shard_map/ppermute | solution.py:21
  41.8 1.9 %collective-permute-done.7 = f32[4,64,256]{1,2,0:T(8,128)S(1)} collective-permute-done((f32[4,64,256]{1,2,0:T(8,128)S(1)}, f32[4,64,256]{1,2,0:T(8,128)S(1)}, u32[]{:S(2)}, u32[]{:S(2)}) %collective-permute-start.7) | collective-permute-done | bytes 262176 | tf_op jit(solution)/shard_map/ppermute | solution.py:21
  43.6 0.3 add_add_fusion.1
  44.0 1.0 %convolution_bitcast_fusion = f32[4,256,256]{1,2,0:T(8,128)S(1)} fusion(f32[4,64,256]{1,2,0:T(8,128)S(1)} %get-tuple-element.19, f32[4,64,256]{1,2,0:T(8,128)S(1)} %get-tuple-element.18, f32[128,128]{1,0:T(8,128)S(1)} %get-tuple-element.60, f32[128,128]{1,0:T(8,128)S(1)} %get-tuple-element.61), kind=kOutput, calls=%fused_computation | convolution fusion | flops 402817024 | bytes 1703936 | tf_op jit(solution)/shard_map/ji,ric->rjc/dot_general | solution.py:155
  45.2 1.0 %copy.27 = f32[1,128,4,256]{3,2,1,0:T(4,128)} copy(f32[1,128,4,256]{1,3,2,0:T(8,128)S(1)} %fusion.1) | data formatting | bytes 1048576 | tf_op jit(solution)/shard_map/broadcast_in_dim | solution.py:157
  (51 shorter events, 2.0 us)
Async XLA Ops:
  0.0 0.7 %copy-start.2 = (s32[4,256]{1,0:T(4,128)S(1)}, s32[4,256]{1,0:T(4,128)}, u32[]{:S(2)}) copy-start(s32[4,256]{1,0:T(4,128)} %param.12) | copy-start | bytes 12292
  0.7 0.7 %copy-start = (f32[1,4,256]{2,1,0:T(4,128)S(1)}, f32[1,4,256]{2,1,0:T(4,128)}, u32[]{:S(2)}) copy-start(f32[1,4,256]{2,1,0:T(4,128)} %param.10) | copy-start | bytes 12292
  0.7 0.7 %copy-start.1 = (f32[1,4,256]{2,1,0:T(4,128)S(1)}, f32[1,4,256]{2,1,0:T(4,128)}, u32[]{:S(2)}) copy-start(f32[1,4,256]{2,1,0:T(4,128)} %param.11) | copy-start | bytes 12292
  3.0 4.2 %collective-permute-start = (f32[264,256]{1,0:T(8,128)S(1)}, f32[264,256]{1,0:T(8,128)S(1)}, u32[]{:S(2)}, u32[]{:S(2)}) collective-permute-start(f32[264,256]{1,0:T(8,128)S(1)} %get-tuple-element.16), channel_id=1, source_target_pairs={{0,1},{1,0},{2,3},{3,2},{4,5},{5,4},{6,7},{7,6},{8,9},{9,8},{10,11... | collective-permute-start | bytes 811016 | tf_op jit(solution)/shard_map/ppermute | solution.py:21
  3.1 7.8 %collective-permute-start.1 = (f32[264,256]{1,0:T(8,128)S(1)}, f32[264,256]{1,0:T(8,128)S(1)}, u32[]{:S(2)}, u32[]{:S(2)}) collective-permute-start(f32[264,256]{1,0:T(8,128)S(1)} %get-tuple-element.17), channel_id=1, source_target_pairs={{1,2},{2,1},{5,6},{6,5},{9,10},{10,9},{13,14},{14,13},{17,18},{18,... | collective-permute-start | bytes 811016 | tf_op jit(solution)/shard_map/ppermute | solution.py:21
  5.7 0.7 %copy-start.3 = (f32[128]{0:T(128)S(1)}, f32[128]{0:T(128)}, u32[]{:S(2)}) copy-start(f32[128]{0:T(128)} %param.13) | copy-start | bytes 1540
  6.4 0.7 %copy-start.4 = (f32[8]{0:T(128)S(1)}, f32[8]{0:T(128)}, u32[]{:S(2)}) copy-start(f32[8]{0:T(128)} %param.15) | copy-start | bytes 100
  6.4 0.7 %copy-start.5 = (s32[128]{0:T(128)S(1)}, s32[128]{0:T(128)}, u32[]{:S(2)}) copy-start(s32[128]{0:T(128)} %param.14) | copy-start | bytes 1540
  6.4 0.7 %copy-start.6 = (f32[8]{0:T(128)S(1)}, f32[8]{0:T(128)}, u32[]{:S(2)}) copy-start(f32[8]{0:T(128)} %param.17) | copy-start | bytes 100
  6.5 0.7 %copy-start.7 = (f32[8]{0:T(128)S(1)}, f32[8]{0:T(128)}, u32[]{:S(2)}) copy-start(f32[8]{0:T(128)} %param.16) | copy-start | bytes 100
  13.0 9.2 %collective-permute-start.2 = (f32[4,64,256]{1,2,0:T(8,128)S(1)}, f32[4,64,256]{1,2,0:T(8,128)S(1)}, u32[]{:S(2)}, u32[]{:S(2)}) collective-permute-start(f32[4,64,256]{1,2,0:T(8,128)S(1)} %get-tuple-element.21), channel_id=1, source_target_pairs={{0,8},{8,0},{4,12},{12,4},{16,24},{24,16},{20,28},{28,20},{1,9},{9... | collective-permute-start | bytes 786440 | tf_op jit(solution)/shard_map/ppermute | solution.py:21
  13.5 11.8 %collective-permute-start.3 = (f32[4,64,256]{1,2,0:T(8,128)S(1)}, f32[4,64,256]{1,2,0:T(8,128)S(1)}, u32[]{:S(2)}, u32[]{:S(2)}) collective-permute-start(f32[4,64,256]{1,2,0:T(8,128)S(1)} %get-tuple-element.21), channel_id=1, source_target_pairs={{8,16},{16,8},{12,20},{20,12},{9,17},{17,9},{13,21},{21,13},{10,18... | collective-permute-start | bytes 786440 | tf_op jit(solution)/shard_map/ppermute | solution.py:21
  18.1 12.5 %collective-permute-start.5 = (f32[4,64,256]{1,2,0:T(8,128)S(1)}, f32[4,64,256]{1,2,0:T(8,128)S(1)}, u32[]{:S(2)}, u32[]{:S(2)}) collective-permute-start(f32[4,64,256]{1,2,0:T(8,128)S(1)} %get-tuple-element.22), channel_id=1, source_target_pairs={{0,4},{4,0},{8,12},{12,8},{16,20},{20,16},{24,28},{28,24},{1,5},{5... | collective-permute-start | bytes 786440 | tf_op jit(solution)/shard_map/ppermute | solution.py:21
  31.0 9.2 %collective-permute-start.4 = (f32[4,64,256]{1,2,0:T(8,128)S(1)}, f32[4,64,256]{1,2,0:T(8,128)S(1)}, u32[]{:S(2)}, u32[]{:S(2)}) collective-permute-start(f32[4,64,256]{1,2,0:T(8,128)S(1)} %get-tuple-element.20), channel_id=1, source_target_pairs={{0,4},{4,0},{8,12},{12,8},{16,20},{20,16},{24,28},{28,24},{1,5},{5... | collective-permute-start | bytes 786440 | tf_op jit(solution)/shard_map/ppermute | solution.py:21
  32.6 9.2 %collective-permute-start.6 = (f32[4,64,256]{1,2,0:T(8,128)S(1)}, f32[4,64,256]{1,2,0:T(8,128)S(1)}, u32[]{:S(2)}, u32[]{:S(2)}) collective-permute-start(f32[4,64,256]{1,2,0:T(8,128)S(1)} %get-tuple-element.12), channel_id=1, source_target_pairs={{0,8},{8,0},{4,12},{12,4},{16,24},{24,16},{20,28},{28,20},{1,9},{9... | collective-permute-start | bytes 786440 | tf_op jit(solution)/shard_map/ppermute | solution.py:21
  32.6 11.1 %collective-permute-start.7 = (f32[4,64,256]{1,2,0:T(8,128)S(1)}, f32[4,64,256]{1,2,0:T(8,128)S(1)}, u32[]{:S(2)}, u32[]{:S(2)}) collective-permute-start(f32[4,64,256]{1,2,0:T(8,128)S(1)} %get-tuple-element.13), channel_id=1, source_target_pairs={{8,16},{16,8},{12,20},{20,12},{9,17},{17,9},{13,21},{21,13},{10,18... | collective-permute-start | bytes 786440 | tf_op jit(solution)/shard_map/ppermute | solution.py:21

commit v2 on v1

v2 whole, which is shorter than its diff:
```python
import functools

import jax
import jax.numpy as jnp
from jax import lax
from jax.experimental import pallas as pl
from jax.experimental.pallas import tpu as pltpu
from jax.sharding import PartitionSpec as P

NB = 128
NCLS = 8

h_diffusion = 0.2
v_diffusion = 0.2
step_duration = 0.5
collide_scale = 2.0
SUBLANES = 8
EDGE = 2
CHUNKS = ((0, 0, 128, True), (1, 0, 128, False))
VMEM = pl.BlockSpec(memory_space=pltpu.VMEM)
HBM = pl.BlockSpec(memory_space=pltpu.HBM)
PARAMS = pltpu.CompilerParams(vmem_limit_bytes=8 << 20)


def in_vmem(*values):
    return [pltpu.with_memory_space_constraint(value, pltpu.VMEM) for value in values]


def in_hbm(*values):
    return [pltpu.with_memory_space_constraint(value, pltpu.HBM) for value in values]


def odd_core():
    return lax.axis_index("xy") % 2 == 1


def by_parity(body):
    odd = odd_core()
    pl.when(odd)(functools.partial(body, True))
    pl.when(jnp.logical_not(odd))(functools.partial(body, False))


def swap(value, axis, reach, parity):
    count = lax.axis_size(axis)
    pairs = []
    for low in range(count - reach):
        if (low // reach) % 2 == parity:
            pairs += [(low, low + reach), (low + reach, low)]
    return lax.ppermute(value, axis, pairs)


def load_kernel(conc, vel_x, vel_y, mask, rows, near, far, flow, mask_rows, sems):
    count, bins, _ = rows.shape

    def body(odd):
        near_at, far_at = (0, count - EDGE) if odd else (count - EDGE, 0)
        copies = [pltpu.make_async_copy(mask, mask_rows, sems.at[0])]
        copies.append(pltpu.make_async_copy(vel_x.at[0], flow.at[0], sems.at[1]))
        copies.append(pltpu.make_async_copy(vel_y.at[0], flow.at[1], sems.at[2]))
        for target, at in ((near, near_at), (far, far_at)):
            for r in range(EDGE):
                copies.append(
                    pltpu.make_async_copy(
                        conc.at[0, :, at + r, :], target.at[r, pl.ds(0, bins)], sems.at[len(copies)]
                    )
                )
        for r in range(count):
            copies.append(pltpu.make_async_copy(conc.at[0, :, r, :], rows.at[r], sems.at[len(copies)]))
        for copy in copies:
            copy.start()
        for copy in copies[:3]:
            copy.wait()
        flow[2] = mask_rows[...].astype(jnp.float32)
        for target, end in ((near, 0 if odd else count - 1), (far, count - 1 if odd else 0)):
            for r in range(EDGE):
                target[r, bins:, :] = jnp.zeros_like(target[r, bins:, :])
            for i in range(3):
                target[0, bins + i : bins + i + 1, :] = flow[i, end : end + 1, :]
        for copy in copies[3:]:
            copy.wait()

    by_parity(body)


def load(conc, vel_x, vel_y, mask):
    _, bins, count, cols = conc.shape
    edge = pltpu.VMEM((EDGE, bins + SUBLANES, cols), jnp.float32)
    return pl.pallas_call(
        load_kernel,
        out_shape=(
            pltpu.VMEM((count, bins, cols), jnp.float32),
            edge,
            edge,
            pltpu.VMEM((3, count, cols), jnp.float32),
        ),
        in_specs=[HBM] * 4,
        out_specs=(VMEM,) * 4,
        scratch_shapes=[pltpu.VMEM((count, cols), jnp.int32), pltpu.SemaphoreType.DMA((3 + 2 * EDGE + count,))],
        compiler_params=PARAMS,
    )(*in_hbm(conc, vel_x, vel_y, mask))


def horizontal_kernel(near, rows_ref, halo_ref, flow_ref, out_ref, scale_ref):
    count, bins, cols = rows_ref.shape
    column = lax.broadcasted_iota(jnp.int32, (1, cols), 1)
    block = 4 * SUBLANES

    def body(odd):
        first = odd == near
        base = 0 if first else count - 4

        def row(i):
            if first:
                return (halo_ref, i) if i < EDGE else (rows_ref, i - EDGE)
            return (rows_ref, base + i) if i < 4 else (halo_ref, i - 4)

        for i in range(1, 5):
            ref, at = row(i)
            if ref is halo_ref:
                aux = halo_ref[0, bins : bins + SUBLANES, :]
                x, y, water = aux[0:1], aux[1:2], aux[2:3]
            else:
                x, y, water = (flow_ref[part, at : at + 1, :] for part in range(3))
            x, y = 0.5 * x, 0.5 * y
            parts = (
                water * (1.0 - 4.0 * h_diffusion),
                water * (h_diffusion - x),
                water * (h_diffusion + x),
                jnp.where(column == cols - 1, 0.0, water * (h_diffusion - y)),
                jnp.where(column == 0, 0.0, water * (h_diffusion + y)),
            )
            for number, part in enumerate(parts):
                scale_ref[i - 1, number] = jnp.broadcast_to(part, (SUBLANES, cols))

        def step(cells, i):
            own, east, west, north, south = (
                jnp.concatenate([scale_ref[i - 1, number]] * (block // SUBLANES), 0) for number in range(5)
            )
            here = cells[i]
            return (
                own * here
                + east * cells[i + 1]
                + west * cells[i - 1]
                + north * pltpu.roll(here, cols - 1, 1)
                + south * pltpu.roll(here, 1, 1)
            )

        for at in range(0, bins, block):
            at = pl.ds(at, block)
            cells = {}
            for i in range(6):
                ref, place = row(i)
                cells[i] = ref[place, at, :]
            once = {i: step(cells, i) for i in range(1, 5)}
            for i in range(EDGE):
                out_ref[i, at, :] = step(once, EDGE + i)

    by_parity(body)


def horizontal(near, rows, halo, flow):
    _, bins, cols = rows.shape
    return pl.pallas_call(
        functools.partial(horizontal_kernel, near),
        out_shape=pltpu.VMEM((EDGE, bins, cols), jnp.float32),
        in_specs=[VMEM] * 3,
        out_specs=VMEM,
        scratch_shapes=[pltpu.VMEM((4, 5, SUBLANES, cols), jnp.float32)],
        cost_estimate=pl.CostEstimate(flops=6 * 9 * bins * cols, bytes_accessed=32 * bins * cols, transcendentals=0),
        compiler_params=PARAMS,
    )(*in_vmem(rows, halo, flow))


def split(value):
    high = value.astype(jnp.bfloat16)
    return high, (value - high.astype(jnp.float32)).astype(jnp.bfloat16)


def collide_kernel(near, cells_ref, both_ref, *refs):
    out_ref, done_ref, sems = refs[-3:]
    count = out_ref.shape[2]

    def body(odd):
        at = 0 if odd == near else count - EDGE
        copies = []
        for r in range(EDGE):
            cells = cells_ref[r]
            high, low = split(cells)
            sums = jnp.dot(
                both_ref[...], jnp.concatenate([high, low, high], 0), preferred_element_type=jnp.float32
            )
            done_ref[r] = cells + cells * sums[:NB] + sums[NB:]
            copies.append(pltpu.make_async_copy(done_ref.at[r], out_ref.at[0, :, at + r, :], sems.at[r]))
            copies[-1].start()
        for copy in copies:
            copy.wait()

    by_parity(body)


def collide(near, cells, both, shape, before=None):
    rest = () if before is None else (before,)
    return pl.pallas_call(
        functools.partial(collide_kernel, near),
        out_shape=pltpu.HBM(shape, jnp.float32),
        in_specs=[VMEM] * 2 + [HBM] * len(rest),
        out_specs=HBM,
        input_output_aliases={2: 0} if rest else {},
        scratch_shapes=[pltpu.VMEM(cells.shape, jnp.float32), pltpu.SemaphoreType.DMA((EDGE,))],
        cost_estimate=pl.CostEstimate(flops=4 * 3 * NB * cells.size, bytes_accessed=12 * cells.size, transcendentals=0),
        compiler_params=PARAMS,
    )(*in_vmem(cells, both), *in_hbm(*rest))


def after(value, done):
    return lax.optimization_barrier((value, done))[0]


def local(
    conc,
    vel_x,
    vel_y,
    sea_mask,
    settle,
    size_bin_kernel_class,
    aggregate_upward_factor,
    agg_down,
    break_rate,
):
    rows, near_edge, far_edge, flow = load(conc, vel_x, vel_y, sea_mask)
    halo_core = swap(near_edge, "xy", 1, 0)
    halo_chip = swap(far_edge, "xy", 1, 1)
    near = horizontal(True, rows, halo_core, flow)
    halo_chip = after(halo_chip, near)
    settle, size_bin_kernel_class, aggregate_upward_factor, agg_down, break_rate, _ = lax.optimization_barrier(
        (settle, size_bin_kernel_class, aggregate_upward_factor, agg_down, break_rate, near)
    )
    moved = [near, horizontal(False, rows, halo_chip, flow)]

    levels = lax.axis_size("bins")
    k = lax.axis_index("bins")
    odd = k % 2 == 1
    high_z = (k // 2) % 2 == 1
    fall = settle + v_diffusion
    rise = jnp.full_like(settle, v_diffusion)

    def keep(level):
        inner = (level > 0).astype(jnp.float32) + (level < levels - 1).astype(jnp.float32)
        return 1.0 - settle - v_diffusion * inner

    inner = (k > 0).astype(jnp.float32) + (k < levels - 1).astype(jnp.float32)
    on_self = keep(k) * keep(k) + inner * fall * rise
    up2, down2 = fall * fall, rise * rise
    zero = jnp.zeros_like(settle)
    up_pair = jnp.where(odd, zero, fall * (keep(k + 2) + keep(k + 1)))
    down_pair = jnp.where(odd, rise * (keep(k - 2) + keep(k - 1)), zero)
    send_0 = (jnp.where(high_z, down2, up2), jnp.where(high_z, down_pair, up_pair))
    send_1 = (jnp.where(high_z, up2, down2), jnp.where(high_z, up_pair, down_pair))
    from_pair = jnp.where(odd, fall * (keep(k) + keep(k - 1)), rise * (keep(k) + keep(k + 1)))
    pair_own = jnp.where(odd, rise * (keep(k - 1) + keep(k)), fall * (keep(k + 1) + keep(k)))
    pair_far = jnp.where(odd, fall * (keep(k - 1) + keep(k - 2)), rise * (keep(k + 1) + keep(k + 2)))
    far_0 = jnp.where(high_z, up2, down2)
    far_1 = jnp.where(high_z, down2, up2)
    uses_0 = odd == high_z

    def total(low, high, *terms):
        out = None
        for scale, cells in terms:
            part = cells if scale is None else scale[low:high][None, :, None] * cells
            out = part if out is None else out + part
        return out

    onehot = (size_bin_kernel_class[:, None] == jnp.arange(NCLS)[None, :]).astype(jnp.float32)

    def lookup(table):
        return jnp.sum(onehot * table[None, :], 1)

    up_rate = lookup(aggregate_upward_factor)
    down_rate = lookup(agg_down)
    brk_rate = lookup(break_rate)
    index = jnp.arange(NB)
    i, j = index[None, :], index[:, None]
    weight = 1.0 / jnp.maximum(index, 1).astype(jnp.float32)
    pairs = jnp.where(i < j, down_rate[:, None] * up_rate[None, :], 0.0) - jnp.where(
        i > j, up_rate[:, None] * down_rate[None, :], 0.0
    )
    pieces = jnp.where(i > j, (brk_rate * weight)[None, :], 0.0) - jnp.where(
        (i == j) & (j >= 1), brk_rate[:, None], 0.0
    )
    both = jnp.concatenate([pairs * (step_duration * collide_scale / NB), pieces * step_duration], 0)

    high = lax.reduce_precision(both, 8, 7)
    low = both - high
    both = jnp.concatenate([high, high, low], 1).astype(jnp.bfloat16)

    first = []
    for far, low, high, x_first in CHUNKS:
        cells = moved[far][:, low:high]
        if x_first:
            first.append((cells, swap(cells, "bins", 1, 0)))
        else:
            first.append((cells, swap(cells, "bins", 2, 0), swap(cells, "bins", 2, 1)))
    done = moved[1]
    sums = [[], []]
    for (far, low, high, x_first), got in zip(CHUNKS, first):
        cells = got[0]
        if x_first:
            pair = after(got[1], done)
            done = total(low, high, (send_0[0], cells), (send_0[1], pair))
            r0 = swap(done, "bins", 2, 0)
            r1 = swap(total(low, high, (send_1[0], cells), (send_1[1], pair)), "bins", 2, 1)
            terms = ((on_self, cells), (from_pair, pair), (None, r0), (None, r1))
        else:
            z0, z1 = got[1:]
            z0 = after(z0, done)
            used = jnp.where(uses_0, z0, z1)
            done = total(low, high, (pair_own, cells), (pair_far, used))
            pair = swap(done, "bins", 1, 0)
            terms = ((on_self, cells), (far_0, z0), (far_1, z1), (None, pair))
        sums[far].append((low, high, terms))

    result = None
    for far in (0, 1):
        parts = []
        for low, high, terms in sorted(sums[far], key=lambda item: item[0]):
            terms = terms[:-1] + ((None, after(terms[-1][1], done)),)
            parts.append(total(low, high, *terms))
        result = done = collide(far == 0, jnp.concatenate(parts, 1), both, conc.shape, result)
    return result


def solution(mesh):
    placed = (
        P("bins", None, "xy", None),
        P("bins", "xy", None),
        P("bins", "xy", None),
        P("xy", None),
        P(),
        P(),
        P(),
        P(),
        P(),
    )
    return jax.shard_map(
        local, mesh=mesh, in_specs=placed, out_specs=P("bins", None, "xy", None), check_vma=False
    )
```

time: 46.5 us -> 29.6 us (0.64)
  waiting for transfers between devices: 23.3 us -> 10.7 us
  local copies, waits for them, and re-layouts: 6.14 us -> 0.53 us
  Pallas kernels: 0 us -> 5.19 us
  other arithmetic: 2.67 us -> 0.79 us
  matrix products: 1.02 us -> 0 us
  starting transfers between devices: 12.7 us -> 11.9 us
    ppermute x8, waiting for transfers between devices: 23.3 us -> 10.7 us  [swap(): return lax.ppermute(value, axis, pairs)]
    pallas_call x0 -> x5, Pallas kernels: none -> 5.19 us  [the longest x2 2.52 us: collide(): pl.pallas_call(functools.partial(collide_kernel, near), out_shape=pltpu.H...]
    unnamed x17 -> x10, local copies, waits for them, and re-layouts: 3.95 us -> 0.53 us
    mul x5 -> x0, other arithmetic: 1.4 us -> none  [the longest x2 1.37 us: substep(): water * (level - 0.5 * speed_x * (east - west) - 0.5 * speed_y * (north -...]
    dot_general x1 -> x0, matrix products: 1.02 us -> none  [local(): jnp.einsum('ji,ric->rjc', both, sunk, precision=lax.Precision.HIGHEST)]
    broadcast_in_dim x1 -> x0, local copies, waits for them, and re-layouts: 1 us -> none  [local(): return jnp.transpose(result, (1, 0, 2))[None]]
    slice x17 -> x0, local copies, waits for them, and re-layouts: 0.95 us -> none  [the longest x3 0.29 us: message(): edge = rows[:2] if low else rows[count - 2:]]
    ppermute x8, starting transfers between devices: 12.7 us -> 11.9 us  [swap(): return lax.ppermute(value, axis, pairs)]
  transfers between devices with their start and end apart: 8 -> 8, of which waited for: 7 -> 5; matrix products, arithmetic and copies ran while one was open for 1% -> 2% of each run, Pallas kernels for 0% -> 9%
where the time goes in v2:
time: 29.6 us; the launch traced here: 29.4 us
  starting transfers between devices  11.9 us (40%)
  waiting for transfers between devices  10.7 us (36%)
  Pallas kernels  5.19 us (18%)
  other arithmetic  0.79 us (3%)
  local copies, waits for them, and re-layouts  0.53 us (2%)
  between operations  0.32 us (1%)
    ppermute x8, starting transfers between devices, swap(): return lax.ppermute(value, axis, pairs)  11.9 us
    ppermute x8, waiting for transfers between devices, swap(): return lax.ppermute(value, axis, pairs)  10.7 us
    pallas_call x2, Pallas kernels, collide(): pl.pallas_call(functools.partial(collide_kernel, near), out_shape=pltpu.H...  2.52 us
    pallas_call x1, Pallas kernels, load(): pl.pallas_call(load_kernel, out_shape=(pltpu.VMEM((count, bins, cols), jn...  1.43 us
    pallas_call x2, Pallas kernels, horizontal(): pl.pallas_call(functools.partial(horizontal_kernel, near), out_shape=pltp...  1.24 us
  transfers between devices with their start and end apart: 8, of which 5 were waited for; matrix products, arithmetic and copies ran while one was open for 2% of the time, Pallas kernels for 9%

profile of v2, /device:TPU:12, one launch (start us, length us, event | category | flops | bytes accessed | tf_op | source)
XLA Modules:
  0.0 29.4 jit_solution(8814790197712227464)
XLA Ops:
  0.0 1.4 %shard_map.91 = (f32[4,128,256]{2,1,0:T(8,128)S(1)}, f32[2,136,256]{2,1,0:T(8,128)S(1)}, f32[2,136,256]{2,1,0:T(8,128)S(1)}, f32[3,4,256]{2,1,0:T(4,128)S(1)}) custom-call(f32[1,128,4,256]{3,2,1,0:T(4,128)} %conc.1, f32[1,4,256]{2,1,0:T(4,128)} %vel_x.1, f32[1,4,256]{2,1,0:T(4,128)} %vel_y.1, s32[4,256]{1,0:T(4,128)} %mask.1), custom_call_target="tpu_custom_call" | custom-call | tf_op jit(solution)/shard_map/pallas_call | solution.py:88
  1.5 2.5 %collective-permute-start.1 = (f32[2,136,256]{2,1,0:T(8,128)S(1)}, f32[2,136,256]{2,1,0:T(8,128)S(1)}, u32[]{:S(2)}, u32[]{:S(2)}) collective-permute-start(f32[2,136,256]{2,1,0:T(8,128)S(1)} %get-tuple-element.23), channel_id=1, source_target_pairs={{1,2},{2,1},{5,6},{6,5},{9,10},{10,9},{13,14},{14,13},{17,18},{18,... | collective-permute-start | bytes 835592 | tf_op jit(solution)/shard_map/ppermute | solution.py:49
  4.1 0.6 %shard_map.92 = f32[2,128,256]{2,1,0:T(8,128)S(1)} custom-call(f32[4,128,256]{2,1,0:T(8,128)S(1)} %get-tuple-element.19.rows_ref, f32[2,136,256]{2,1,0:T(8,128)S(1)} %collective-permute-done.halo_ref, f32[3,4,256]{2,1,0:T(4,128)S(1)} %get-tuple-element.21.flow_ref), custom_call_target="tpu_custom_call" | custom-call | flops 1769472 | bytes 1048576 | tf_op jit(solution)/shard_map/pallas_call | solution.py:163
  4.8 1.6 %collective-permute-start.3 = (f32[2,128,256]{2,1,0:T(8,128)S(1)}, f32[2,128,256]{2,1,0:T(8,128)S(1)}, u32[]{:S(2)}, u32[]{:S(2)}) collective-permute-start(f32[2,128,256]{2,1,0:T(8,128)S(1)} %shard_map.92), channel_id=1, source_target_pairs={{0,4},{4,0},{8,12},{12,8},{16,20},{20,16},{24,28},{28,24},{1,5},{5... | collective-permute-start | bytes 786440 | tf_op jit(solution)/shard_map/ppermute | solution.py:49
  6.4 3.0 %collective-permute-done.1.halo_ref = f32[2,136,256]{2,1,0:T(8,128)S(1)} collective-permute-done((f32[2,136,256]{2,1,0:T(8,128)S(1)}, f32[2,136,256]{2,1,0:T(8,128)S(1)}, u32[]{:S(2)}, u32[]{:S(2)}) %collective-permute-start.1) | collective-permute-done | bytes 278560 | tf_op jit(solution)/shard_map/ppermute | solution.py:49
  9.4 0.6 %shard_map.93 = f32[2,128,256]{2,1,0:T(8,128)S(1)} custom-call(f32[4,128,256]{2,1,0:T(8,128)S(1)} %get-tuple-element.19.rows_ref, f32[2,136,256]{2,1,0:T(8,128)S(1)} %collective-permute-done.1.halo_ref, f32[3,4,256]{2,1,0:T(4,128)S(1)} %get-tuple-element.21.flow_ref), custom_call_target="tpu_custom_call" | custom-call | flops 1769472 | bytes 1048576 | tf_op jit(solution)/shard_map/pallas_call | solution.py:163
  10.0 0.5 %collective-permute-start.2 = (f32[2,128,256]{2,1,0:T(8,128)S(1)}, f32[2,128,256]{2,1,0:T(8,128)S(1)}, u32[]{:S(2)}, u32[]{:S(2)}) collective-permute-start(f32[2,128,256]{2,1,0:T(8,128)S(1)} %shard_map.93), channel_id=1, source_target_pairs={{0,8},{8,0},{4,12},{12,4},{16,24},{24,16},{20,28},{28,20},{1,9},{9... | collective-permute-start | bytes 786440 | tf_op jit(solution)/shard_map/ppermute | solution.py:49
  10.5 4.6 %collective-permute-start.4 = (f32[2,128,256]{2,1,0:T(8,128)S(1)}, f32[2,128,256]{2,1,0:T(8,128)S(1)}, u32[]{:S(2)}, u32[]{:S(2)}) collective-permute-start(f32[2,128,256]{2,1,0:T(8,128)S(1)} %shard_map.93), channel_id=1, source_target_pairs={{8,16},{16,8},{12,20},{20,12},{9,17},{17,9},{13,21},{21,13},{10,18... | collective-permute-start | bytes 786440 | tf_op jit(solution)/shard_map/ppermute | solution.py:49
  15.2 0.1 select_reduce_fusion.1
  15.3 0.1 subtract_multiply_fusion
  15.4 0.5 %copy-done = f32[128]{0:T(128)S(1)} copy-done((f32[128]{0:T(128)S(1)}, f32[128]{0:T(128)}, u32[]{:S(2)}) %copy-start) | copy-done | bytes 536
  16.0 0.1 multiply_add_fusion
  16.1 1.9 %collective-permute-start.7 = (f32[2,128,256]{2,1,0:T(8,128)S(1)}, f32[2,128,256]{2,1,0:T(8,128)S(1)}, u32[]{:S(2)}, u32[]{:S(2)}) collective-permute-start(f32[2,128,256]{2,1,0:T(8,128)S(1)} %get-tuple-element.39), channel_id=1, source_target_pairs={{8,16},{16,8},{12,20},{20,12},{9,17},{17,9},{13,21},{21,13},{10,18... | collective-permute-start | bytes 786440 | tf_op jit(solution)/shard_map/ppermute | solution.py:49
  18.1 0.1 collective-permute-start.6
  18.2 3.3 %collective-permute-done.4 = f32[2,128,256]{2,1,0:T(8,128)S(1)} collective-permute-done((f32[2,128,256]{2,1,0:T(8,128)S(1)}, f32[2,128,256]{2,1,0:T(8,128)S(1)}, u32[]{:S(2)}, u32[]{:S(2)}) %collective-permute-start.4) | collective-permute-done | bytes 262176 | tf_op jit(solution)/shard_map/ppermute | solution.py:49
  21.5 0.1 multiply_add_fusion.1
  21.6 0.6 %collective-permute-start.5 = (f32[2,128,256]{2,1,0:T(8,128)S(1)}, f32[2,128,256]{2,1,0:T(8,128)S(1)}, u32[]{:S(2)}, u32[]{:S(2)}) collective-permute-start(f32[2,128,256]{2,1,0:T(8,128)S(1)} %multiply_add_fusion.1), channel_id=1, source_target_pairs={{0,4},{4,0},{8,12},{12,8},{16,20},{20,16},{24,28},{28,24},{1,5},{5... | collective-permute-start | bytes 786440 | tf_op jit(solution)/shard_map/ppermute | solution.py:49
  22.2 2.2 %collective-permute-done.7 = f32[2,128,256]{2,1,0:T(8,128)S(1)} collective-permute-done((f32[2,128,256]{2,1,0:T(8,128)S(1)}, f32[2,128,256]{2,1,0:T(8,128)S(1)}, u32[]{:S(2)}, u32[]{:S(2)}) %collective-permute-start.7) | collective-permute-done | bytes 262176 | tf_op jit(solution)/shard_map/ppermute | solution.py:49
  24.4 0.1 collective-permute-done.6
  24.5 0.1 add_add_fusion.cells_ref
  24.6 1.3 %shard_map.94.refs_0_ = f32[1,128,4,256]{3,2,1,0:T(4,128)} custom-call(f32[2,128,256]{2,1,0:T(8,128)S(1)} %add_add_fusion.cells_ref, bf16[256,384]{1,0:T(8,128)(2,1)S(1)} %pad_maximum_fusion.both_ref), custom_call_target="tpu_custom_call" | custom-call | flops 100663296 | bytes 786432 | tf_op jit(solution)/shard_map/pallas_call | solution.py:203
  25.9 2.1 %collective-permute-done.5 = f32[2,128,256]{2,1,0:T(8,128)S(1)} collective-permute-done((f32[2,128,256]{2,1,0:T(8,128)S(1)}, f32[2,128,256]{2,1,0:T(8,128)S(1)}, u32[]{:S(2)}, u32[]{:S(2)}) %collective-permute-start.5) | collective-permute-done | bytes 262176 | tf_op jit(solution)/shard_map/ppermute | solution.py:49
  28.0 0.1 add_add_fusion.1.cells_ref
  28.2 1.3 %shard_map.95 = f32[1,128,4,256]{3,2,1,0:T(4,128)} custom-call(f32[2,128,256]{2,1,0:T(8,128)S(1)} %add_add_fusion.1.cells_ref, bf16[256,384]{1,0:T(8,128)(2,1)S(1)} %pad_maximum_fusion.both_ref, f32[1,128,4,256]{3,2,1,0:T(4,128)} %shard_map.94.refs_0_), custom_call_target="tpu_custom_call", output_to_operand_aliasing={{}: (2, {})} | custom-call | flops 100663296 | bytes 786432 | tf_op jit(solution)/shard_map/pallas_call | solution.py:203
  (19 shorter events, 0.2 us)
Async XLA Ops:
  1.4 2.7 %collective-permute-start = (f32[2,136,256]{2,1,0:T(8,128)S(1)}, f32[2,136,256]{2,1,0:T(8,128)S(1)}, u32[]{:S(2)}, u32[]{:S(2)}) collective-permute-start(f32[2,136,256]{2,1,0:T(8,128)S(1)} %get-tuple-element.20), channel_id=1, source_target_pairs={{0,1},{1,0},{2,3},{3,2},{4,5},{5,4},{6,7},{7,6},{8,9},{9,8},{10,11... | collective-permute-start | bytes 835592 | tf_op jit(solution)/shard_map/ppermute | solution.py:49
  1.5 7.9 %collective-permute-start.1 = (f32[2,136,256]{2,1,0:T(8,128)S(1)}, f32[2,136,256]{2,1,0:T(8,128)S(1)}, u32[]{:S(2)}, u32[]{:S(2)}) collective-permute-start(f32[2,136,256]{2,1,0:T(8,128)S(1)} %get-tuple-element.23), channel_id=1, source_target_pairs={{1,2},{2,1},{5,6},{6,5},{9,10},{10,9},{13,14},{14,13},{17,18},{18,... | collective-permute-start | bytes 835592 | tf_op jit(solution)/shard_map/ppermute | solution.py:49
  4.8 10.4 %copy-start.1 = (f32[8]{0:T(128)S(1)}, f32[8]{0:T(128)}, u32[]{:S(2)}) copy-start(f32[8]{0:T(128)} %param.15) | copy-start | bytes 100
  4.8 10.4 %copy-start.2 = (s32[128]{0:T(128)S(1)}, s32[128]{0:T(128)}, u32[]{:S(2)}) copy-start(s32[128]{0:T(128)} %param.14) | copy-start | bytes 1540
  4.8 10.4 %copy-start.3 = (f32[8]{0:T(128)S(1)}, f32[8]{0:T(128)}, u32[]{:S(2)}) copy-start(f32[8]{0:T(128)} %param.17) | copy-start | bytes 100
  4.8 10.4 %copy-start.4 = (f32[8]{0:T(128)S(1)}, f32[8]{0:T(128)}, u32[]{:S(2)}) copy-start(f32[8]{0:T(128)} %param.16) | copy-start | bytes 100
  4.8 11.2 %collective-permute-start.3 = (f32[2,128,256]{2,1,0:T(8,128)S(1)}, f32[2,128,256]{2,1,0:T(8,128)S(1)}, u32[]{:S(2)}, u32[]{:S(2)}) collective-permute-start(f32[2,128,256]{2,1,0:T(8,128)S(1)} %shard_map.92), channel_id=1, source_target_pairs={{0,4},{4,0},{8,12},{12,8},{16,20},{20,16},{24,28},{28,24},{1,5},{5... | collective-permute-start | bytes 786440 | tf_op jit(solution)/shard_map/ppermute | solution.py:49
  10.0 8.2 %collective-permute-start.2 = (f32[2,128,256]{2,1,0:T(8,128)S(1)}, f32[2,128,256]{2,1,0:T(8,128)S(1)}, u32[]{:S(2)}, u32[]{:S(2)}) collective-permute-start(f32[2,128,256]{2,1,0:T(8,128)S(1)} %shard_map.93), channel_id=1, source_target_pairs={{0,8},{8,0},{4,12},{12,4},{16,24},{24,16},{20,28},{28,20},{1,9},{9... | collective-permute-start | bytes 786440 | tf_op jit(solution)/shard_map/ppermute | solution.py:49
  10.5 11.0 %collective-permute-start.4 = (f32[2,128,256]{2,1,0:T(8,128)S(1)}, f32[2,128,256]{2,1,0:T(8,128)S(1)}, u32[]{:S(2)}, u32[]{:S(2)}) collective-permute-start(f32[2,128,256]{2,1,0:T(8,128)S(1)} %shard_map.93), channel_id=1, source_target_pairs={{8,16},{16,8},{12,20},{20,12},{9,17},{17,9},{13,21},{21,13},{10,18... | collective-permute-start | bytes 786440 | tf_op jit(solution)/shard_map/ppermute | solution.py:49
  15.3 0.7 %copy-start = (f32[128]{0:T(128)S(1)}, f32[128]{0:T(128)}, u32[]{:S(2)}) copy-start(f32[128]{0:T(128)} %param.13) | copy-start | bytes 1540
  16.1 8.3 %collective-permute-start.7 = (f32[2,128,256]{2,1,0:T(8,128)S(1)}, f32[2,128,256]{2,1,0:T(8,128)S(1)}, u32[]{:S(2)}, u32[]{:S(2)}) collective-permute-start(f32[2,128,256]{2,1,0:T(8,128)S(1)} %get-tuple-element.39), channel_id=1, source_target_pairs={{8,16},{16,8},{12,20},{20,12},{9,17},{17,9},{13,21},{21,13},{10,18... | collective-permute-start | bytes 786440 | tf_op jit(solution)/shard_map/ppermute | solution.py:49
  18.1 6.4 %collective-permute-start.6 = (f32[2,128,256]{2,1,0:T(8,128)S(1)}, f32[2,128,256]{2,1,0:T(8,128)S(1)}, u32[]{:S(2)}, u32[]{:S(2)}) collective-permute-start(f32[2,128,256]{2,1,0:T(8,128)S(1)} %get-tuple-element.40), channel_id=1, source_target_pairs={{0,8},{8,0},{4,12},{12,4},{16,24},{24,16},{20,28},{28,20},{1,9},{9... | collective-permute-start | bytes 786440 | tf_op jit(solution)/shard_map/ppermute | solution.py:49
  21.6 6.4 %collective-permute-start.5 = (f32[2,128,256]{2,1,0:T(8,128)S(1)}, f32[2,128,256]{2,1,0:T(8,128)S(1)}, u32[]{:S(2)}, u32[]{:S(2)}) collective-permute-start(f32[2,128,256]{2,1,0:T(8,128)S(1)} %multiply_add_fusion.1), channel_id=1, source_target_pairs={{0,4},{4,0},{8,12},{12,8},{16,20},{20,16},{24,28},{28,24},{1,5},{5... | collective-permute-start | bytes 786440 | tf_op jit(solution)/shard_map/ppermute | solution.py:49

commit v3 on v2

v3 whole, which is shorter than its diff:
```python
import functools

import jax
import jax.numpy as jnp
from jax import lax
from jax.experimental import pallas as pl
from jax.experimental.pallas import tpu as pltpu
from jax.sharding import PartitionSpec as P

NB = 128
NCLS = 8

h_diffusion = 0.2
v_diffusion = 0.2
step_duration = 0.5
collide_scale = 2.0
SUBLANES = 8
EDGE = 2
CHUNKS = (((0, 0, 128, False),), ((1, 0, 128, True),))
VMEM = pl.BlockSpec(memory_space=pltpu.VMEM)
HBM = pl.BlockSpec(memory_space=pltpu.HBM)
ANY = pl.BlockSpec(memory_space=pl.ANY)
PARAMS = pltpu.CompilerParams(vmem_limit_bytes=8 << 20)


def in_vmem(*values):
    return [pltpu.with_memory_space_constraint(value, pltpu.VMEM) for value in values]


def in_hbm(*values):
    return [pltpu.with_memory_space_constraint(value, pltpu.HBM) for value in values]


def odd_core():
    return lax.axis_index("xy") % 2 == 1


def by_parity(body):
    odd = odd_core()
    pl.when(odd)(functools.partial(body, True))
    pl.when(jnp.logical_not(odd))(functools.partial(body, False))


def exchange(value, partner):
    bands = lax.axis_size("xy")
    pairs = []
    for level in range(lax.axis_size("bins")):
        for band in range(bands):
            to_level, to_band = partner(level, band)
            pairs.append((level * bands + band, to_level * bands + to_band))
    return lax.ppermute(value, ("bins", "xy"), pairs)


def swap_core(value):
    return exchange(value, lambda level, band: (level, band ^ 1))


def swap_chip(value):
    bands = lax.axis_size("xy")

    def partner(level, band):
        to = band + 1 if band % 2 else band - 1
        return (level, to) if 0 <= to < bands else (level ^ 1, band)

    return exchange(value, partner)


def swap_pair(value):
    return exchange(value, lambda level, band: (level ^ 1, band))


def swap_far(value, parity):
    levels = lax.axis_size("bins")

    def partner(level, band):
        to = level + 2 if level // 2 % 2 == parity else level - 2
        return (to, band) if 0 <= to < levels else (level, band ^ 1)

    return exchange(value, partner)


def load_kernel(conc, vel_x, vel_y, mask, rows, near, *refs):
    far, (flow, mask_rows, sems) = refs[:-3], refs[-3:]
    count, bins, _ = rows.shape
    part = bins // len(far)

    def body(odd):
        near_at, far_at = (0, count - EDGE) if odd else (count - EDGE, 0)
        copies = [pltpu.make_async_copy(mask, mask_rows, sems.at[0])]
        copies.append(pltpu.make_async_copy(vel_x.at[0], flow.at[0], sems.at[1]))
        copies.append(pltpu.make_async_copy(vel_y.at[0], flow.at[1], sems.at[2]))
        edges = [(near, near_at, 0, bins)] + [(ref, far_at, i * part, part) for i, ref in enumerate(far)]
        for target, at, low, size in edges:
            for r in range(EDGE):
                copies.append(
                    pltpu.make_async_copy(
                        conc.at[0, pl.ds(low, size), at + r, :], target.at[r, pl.ds(0, size)], sems.at[len(copies)]
                    )
                )
        for r in range(count):
            copies.append(pltpu.make_async_copy(conc.at[0, :, r, :], rows.at[r], sems.at[len(copies)]))
        for copy in copies:
            copy.start()
        for copy in copies[:3]:
            copy.wait()
        flow[2] = mask_rows[...].astype(jnp.float32)
        for target, at, _, size in edges:
            end = at if at == 0 else count - 1
            for r in range(EDGE):
                target[r, size:, :] = jnp.zeros_like(target[r, size:, :])
            for i in range(3):
                target[0, size + i : size + i + 1, :] = flow[i, end : end + 1, :]
        for copy in copies[3:]:
            copy.wait()

    by_parity(body)


def load(conc, vel_x, vel_y, mask, parts):
    _, bins, count, cols = conc.shape

    def edge(size):
        return pltpu.VMEM((EDGE, size + SUBLANES, cols), jnp.float32)

    rows, near, *far, flow = pl.pallas_call(
        load_kernel,
        out_shape=(
            pltpu.VMEM((count, bins, cols), jnp.float32),
            edge(bins),
            *[edge(bins // parts)] * parts,
            pltpu.VMEM((3, count, cols), jnp.float32),
        ),
        in_specs=[HBM] * 4,
        out_specs=(VMEM,) * (3 + parts),
        scratch_shapes=[
            pltpu.VMEM((count, cols), jnp.int32),
            pltpu.SemaphoreType.DMA((3 + EDGE * (1 + parts) + count,)),
        ],
        compiler_params=PARAMS,
    )(*in_hbm(conc, vel_x, vel_y, mask))
    return rows, near, far, flow


def horizontal_kernel(near, low, rows_ref, halo_ref, flow_ref, *refs):
    out_ref, scale_ref = refs[-2:]
    count, _, cols = rows_ref.shape
    bins = out_ref.shape[1]
    column = lax.broadcasted_iota(jnp.int32, (1, cols), 1)
    block = 4 * SUBLANES

    def body(odd):
        first = odd == near
        base = 0 if first else count - 4

        def row(i):
            if first:
                return (halo_ref, i) if i < EDGE else (rows_ref, i - EDGE)
            return (rows_ref, base + i) if i < 4 else (halo_ref, i - 4)

        band = lax.axis_index("xy")
        outside = jnp.logical_and(not near, jnp.logical_or(band == 0, band == lax.axis_size("xy") - 1))
        inside = jnp.where(outside, 0.0, 1.0)
        for i in range(1, 5):
            ref, at = row(i)
            if ref is halo_ref:
                aux = halo_ref[0, bins : bins + SUBLANES, :]
                x, y, water = aux[0:1], aux[1:2], aux[2:3] * inside
            else:
                x, y, water = (flow_ref[part, at : at + 1, :] for part in range(3))
            x, y = 0.5 * x, 0.5 * y
            east = inside if i == 3 and not first else 1.0
            west = inside if i == 2 and first else 1.0
            parts = (
                water * (1.0 - 4.0 * h_diffusion),
                water * (h_diffusion - x) * east,
                water * (h_diffusion + x) * west,
                jnp.where(column == cols - 1, 0.0, water * (h_diffusion - y)),
                jnp.where(column == 0, 0.0, water * (h_diffusion + y)),
            )
            for number, part in enumerate(parts):
                scale_ref[i - 1, number] = jnp.broadcast_to(part, (SUBLANES, cols))

        def step(cells, i):
            own, east, west, north, south = (
                jnp.concatenate([scale_ref[i - 1, number]] * (block // SUBLANES), 0) for number in range(5)
            )
            here = cells[i]
            return (
                own * here
                + east * cells[i + 1]
                + west * cells[i - 1]
                + north * pltpu.roll(here, cols - 1, 1)
                + south * pltpu.roll(here, 1, 1)
            )

        for at in range(0, bins, block):
            cells = {}
            for i in range(6):
                ref, place = row(i)
                cells[i] = ref[place, pl.ds(at if ref is halo_ref else low + at, block), :]
            once = {i: step(cells, i) for i in range(1, 5)}
            for i in range(EDGE):
                out_ref[i, pl.ds(at, block), :] = step(once, EDGE + i)

    by_parity(body)


def horizontal(near, rows, halo, flow, low, size, before=()):
    cols = rows.shape[2]
    return pl.pallas_call(
        functools.partial(horizontal_kernel, near, low),
        out_shape=pltpu.VMEM((EDGE, size, cols), jnp.float32),
        in_specs=[VMEM] * 3 + [ANY] * len(before),
        out_specs=VMEM,
        scratch_shapes=[pltpu.VMEM((4, 5, SUBLANES, cols), jnp.float32)],
        cost_estimate=pl.CostEstimate(flops=6 * 9 * size * cols, bytes_accessed=32 * size * cols, transcendentals=0),
        compiler_params=PARAMS,
    )(*in_vmem(rows, halo, flow, *before))


def weigh(table_ref, low, terms):
    out = None
    for column, cells in terms:
        part = table_ref[low : low + cells.shape[0], column : column + 1] * cells
        out = part if out is None else out + part
    return out


def combine_kernel(low, sums, width, table_ref, *refs):
    cells, outs = refs[:width], refs[len(refs) - len(sums) :]
    for r in range(EDGE):
        for terms, out in zip(sums, outs):
            out[r] = weigh(table_ref, low, [(column, cells[i][r]) for i, column in enumerate(terms)])


def combine(table, low, cells, sums, before=()):
    outs = pl.pallas_call(
        functools.partial(combine_kernel, low, sums, len(cells)),
        out_shape=(pltpu.VMEM(cells[0].shape, jnp.float32),) * len(sums),
        in_specs=[VMEM] * (1 + len(cells)) + [ANY] * len(before),
        out_specs=(VMEM,) * len(sums),
        cost_estimate=pl.CostEstimate(flops=6 * cells[0].size, bytes_accessed=20 * cells[0].size, transcendentals=0),
        compiler_params=PARAMS,
    )(*in_vmem(table, *cells, *before))
    return list(outs)


def split(value):
    high = value.astype(jnp.bfloat16)
    return high, (value - high.astype(jnp.float32)).astype(jnp.bfloat16)


def collide_kernel(near, parts, table_ref, both_ref, *refs):
    out_ref, done_ref, sems = refs[-3:]
    count = out_ref.shape[2]

    def body(odd):
        at = 0 if odd == near else count - EDGE
        copies = []
        for r in range(EDGE):
            first, pieces = 0, []
            for low, columns in parts:
                cells = refs[first : first + len(columns)]
                first += len(columns)
                pieces.append(weigh(table_ref, low, [(column, ref[r]) for column, ref in zip(columns, cells)]))
            cells = jnp.concatenate(pieces, 0)
            high, low = split(cells)
            sums = jnp.dot(
                both_ref[...], jnp.concatenate([high, low, high], 0), preferred_element_type=jnp.float32
            )
            done_ref[r] = cells + cells * sums[:NB] + sums[NB:]
            copies.append(pltpu.make_async_copy(done_ref.at[r], out_ref.at[0, :, at + r, :], sems.at[r]))
            copies[-1].start()
        for copy in copies:
            copy.wait()

    by_parity(body)


def collide(near, table, both, parts, shape, before=None):
    rest = () if before is None else (before,)
    cells = [value for _, terms in parts for _, value in terms]
    parts = [(low, [column for column, _ in terms]) for low, terms in parts]
    cols = shape[3]
    return pl.pallas_call(
        functools.partial(collide_kernel, near, parts),
        out_shape=pltpu.HBM(shape, jnp.float32),
        in_specs=[VMEM] * (2 + len(cells)) + [HBM] * len(rest),
        out_specs=HBM,
        input_output_aliases={2 + len(cells): 0} if rest else {},
        scratch_shapes=[pltpu.VMEM((EDGE, NB, cols), jnp.float32), pltpu.SemaphoreType.DMA((EDGE,))],
        cost_estimate=pl.CostEstimate(
            flops=12 * NB * NB * EDGE * cols, bytes_accessed=24 * EDGE * NB * cols, transcendentals=0
        ),
        compiler_params=PARAMS,
    )(*in_vmem(table, both, *cells), *in_hbm(*rest))


def local(
    conc,
    vel_x,
    vel_y,
    sea_mask,
    settle,
    size_bin_kernel_class,
    aggregate_upward_factor,
    agg_down,
    break_rate,
):
    rows, near_edge, far_edges, flow = load(conc, vel_x, vel_y, sea_mask, 1)
    halo_core = swap_core(near_edge)
    halo_chip = [swap_chip(edge) for edge in far_edges]
    part = NB // 1
    near = horizontal(True, rows, halo_core, flow, 0, NB)
    far = []
    for i in reversed(range(1)):
        far.insert(0, horizontal(False, rows, halo_chip[i], flow, i * part, part, (far or [near])[:1]))

    def transported(is_far, low, high):
        if not is_far:
            return near[:, low:high]
        if high - low > part:
            return jnp.concatenate(far, 1)
        return far[low // part][:, low % part : low % part + high - low]

    levels = lax.axis_size("bins")
    k = lax.axis_index("bins")
    odd = k % 2 == 1
    high_z = (k // 2) % 2 == 1
    fall = settle + v_diffusion
    rise = jnp.full_like(settle, v_diffusion)

    def keep(level):
        inner = (level > 0).astype(jnp.float32) + (level < levels - 1).astype(jnp.float32)
        return 1.0 - settle - v_diffusion * inner

    inner = (k > 0).astype(jnp.float32) + (k < levels - 1).astype(jnp.float32)
    on_self = keep(k) * keep(k) + inner * fall * rise
    up2, down2 = fall * fall, rise * rise
    zero = jnp.zeros_like(settle)
    up_pair = jnp.where(odd, zero, fall * (keep(k + 2) + keep(k + 1)))
    down_pair = jnp.where(odd, rise * (keep(k - 2) + keep(k - 1)), zero)
    send_0 = (jnp.where(high_z, down2, up2), jnp.where(high_z, down_pair, up_pair))
    send_1 = (jnp.where(high_z, up2, down2), jnp.where(high_z, up_pair, down_pair))
    from_pair = jnp.where(odd, fall * (keep(k) + keep(k - 1)), rise * (keep(k) + keep(k + 1)))
    pair_own = jnp.where(odd, rise * (keep(k - 1) + keep(k)), fall * (keep(k + 1) + keep(k)))
    pair_far = jnp.where(odd, fall * (keep(k - 1) + keep(k - 2)), rise * (keep(k + 1) + keep(k + 2)))
    below, above = (k >= 2).astype(jnp.float32), (k + 2 < levels).astype(jnp.float32)
    there_0, there_1 = jnp.where(high_z, below, above), jnp.where(high_z, above, below)
    far_0 = jnp.where(high_z, up2, down2) * there_0
    far_1 = jnp.where(high_z, down2, up2) * there_1
    pair_far = pair_far * jnp.where(odd, below, above)
    uses_0 = odd == high_z

    onehot = (size_bin_kernel_class[:, None] == jnp.arange(NCLS)[None, :]).astype(jnp.float32)

    def lookup(table):
        return jnp.sum(onehot * table[None, :], 1)

    up_rate = lookup(aggregate_upward_factor)
    down_rate = lookup(agg_down)
    brk_rate = lookup(break_rate)
    index = jnp.arange(NB)
    i, j = index[None, :], index[:, None]
    weight = 1.0 / jnp.maximum(index, 1).astype(jnp.float32)
    pairs = jnp.where(i < j, down_rate[:, None] * up_rate[None, :], 0.0) - jnp.where(
        i > j, up_rate[:, None] * down_rate[None, :], 0.0
    )
    pieces = jnp.where(i > j, (brk_rate * weight)[None, :], 0.0) - jnp.where(
        (i == j) & (j >= 1), brk_rate[:, None], 0.0
    )
    both = jnp.concatenate([pairs * (step_duration * collide_scale / NB), pieces * step_duration], 0)

    high = lax.reduce_precision(both, 8, 7)
    low = both - high
    both = jnp.concatenate([high, high, low], 1).astype(jnp.bfloat16)

    columns = [
        send_0[0], send_0[1], send_1[0], send_1[1], on_self, from_pair, there_0 + zero, there_1 + zero,
        pair_own, jnp.where(uses_0, pair_far, zero), jnp.where(uses_0, zero, pair_far), far_0, far_1, zero + 1.0,
    ]
    table = jnp.pad(jnp.stack(columns, 1), ((0, 0), (0, 128 - len(columns))))

    first = []
    for group in CHUNKS:
        for is_far, low, high, x_first in group:
            cells = transported(is_far, low, high)
            if x_first:
                first.append((cells, swap_pair(cells)))
            elif True:
                z1 = swap_far(cells, 1)
                first.append((cells, swap_far(cells, 0), z1))
            else:
                first.append((cells, swap_far(cells, 0), swap_far(cells, 1)))
    parts = [[], []]
    before = ()
    for group in CHUNKS:
        came = [first.pop(0) for _ in group]
        if len(group) > 1:
            came = lax.optimization_barrier(came)
        for (is_far, low, high, x_first), cells in zip(group, came):
            if x_first:
                sends = combine(table, low, cells, ((0, 1), (2, 3)), before)
                if True:
                    r1 = swap_far(sends[1], 1)
                    r0 = swap_far(sends[0], 0)
                else:
                    r0 = swap_far(sends[0], 0)
                    r1 = swap_far(sends[1], 1)
                terms = [(4, cells[0]), (5, cells[1]), (6, r0), (7, r1)]
            else:
                sends = combine(table, low, cells, ((8, 9, 10),), before)
                terms = [(4, cells[0]), (11, cells[1]), (12, cells[2]), (13, swap_pair(sends[0]))]
            before = tuple(sends[:1])
            parts[is_far].append((low, terms))
    result = None
    for is_far in (0, 1):
        result = collide(
            not is_far, table, both, sorted(parts[is_far], key=lambda item: item[0]), conc.shape, result
        )
    return result


def solution(mesh):
    placed = (
        P("bins", None, "xy", None),
        P("bins", "xy", None),
        P("bins", "xy", None),
        P("xy", None),
        P(),
        P(),
        P(),
        P(),
        P(),
    )
    return jax.shard_map(
        local, mesh=mesh, in_specs=placed, out_specs=P("bins", None, "xy", None), check_vma=False
    )
```

time: 29.6 us -> 27.8 us (0.939)
  the two profiles are of different devices: /device:TPU:12 before, /device:TPU:0 now
where the time goes in v3:
time: 27.8 us; the launch traced here: 27.6 us
  starting transfers between devices  10.3 us (37%)
  waiting for transfers between devices  9.2 us (33%)
  Pallas kernels  6.19 us (22%)
  local copies, waits for them, and re-layouts  1.51 us (5%)
  other arithmetic  0.3 us (1%)
    ppermute x8, starting transfers between devices, exchange(): return lax.ppermute(value, ('bins', 'xy'), pairs)  10.3 us
    ppermute x8, waiting for transfers between devices, exchange(): return lax.ppermute(value, ('bins', 'xy'), pairs)  9.2 us
    pallas_call x2, Pallas kernels, collide(): pl.pallas_call(functools.partial(collide_kernel, near, parts), out_shape=...  3.14 us
    pallas_call x1, Pallas kernels, load(): pl.pallas_call(load_kernel, out_shape=(pltpu.VMEM((count, bins, cols), jn...  1.43 us
    unnamed x10, local copies, waits for them, and re-layouts  1.33 us
    pallas_call x2, Pallas kernels, horizontal(): pl.pallas_call(functools.partial(horizontal_kernel, near, low), out_shape...  1.24 us
  transfers between devices with their start and end apart: 8, of which 3 were waited for; matrix products, arithmetic and copies ran while one was open for 2% of the time, Pallas kernels for 12%

profile of v3, /device:TPU:0, one launch (start us, length us, event | category | flops | bytes accessed | tf_op | source)
XLA Modules:
  0.0 27.6 jit_solution(9062126845367904229)
XLA Ops:
  0.0 1.4 %shard_map.91 = (f32[4,128,256]{2,1,0:T(8,128)S(1)}, f32[2,136,256]{2,1,0:T(8,128)S(1)}, f32[2,136,256]{2,1,0:T(8,128)S(1)}, f32[3,4,256]{2,1,0:T(4,128)S(1)}) custom-call(f32[1,128,4,256]{3,2,1,0:T(4,128)} %conc.1, f32[1,4,256]{2,1,0:T(4,128)} %vel_x.1, f32[1,4,256]{2,1,0:T(4,128)} %vel_y.1, s32[4,256]{1,0:T(4,128)} %mask.1), custom_call_target="tpu_custom_call" | custom-call | tf_op jit(solution)/shard_map/pallas_call | solution.py:125
  1.4 3.0 %collective-permute-start = (f32[2,136,256]{2,1,0:T(8,128)S(1)}, f32[2,136,256]{2,1,0:T(8,128)S(1)}, u32[]{:S(2)}, u32[]{:S(2)}) collective-permute-start(f32[2,136,256]{2,1,0:T(8,128)S(1)} %get-tuple-element.12), channel_id=1, source_target_pairs={{0,4},{1,2},{2,1},{3,7},{4,0},{5,6},{6,5},{7,3},{8,12},{9,10},{10,... | collective-permute-start | bytes 835592 | tf_op jit(solution)/shard_map/ppermute | solution.py:51
  4.4 0.1 collective-permute-start.1
  4.6 0.7 %copy-done = f32[128]{0:T(128)S(1)} copy-done((f32[128]{0:T(128)S(1)}, f32[128]{0:T(128)}, u32[]{:S(2)}) %copy-start) | copy-done | bytes 536
  5.3 0.6 %copy-done.1 = f32[8]{0:T(128)S(1)} copy-done((f32[8]{0:T(128)S(1)}, f32[8]{0:T(128)}, u32[]{:S(2)}) %copy-start.1) | copy-done | bytes 56
  5.9 0.0 copy-done.3
  5.9 0.1 select_reduce_fusion.1
  6.1 0.6 %shard_map.92.refs_0_ = f32[2,128,256]{2,1,0:T(8,128)S(1)} custom-call(f32[4,128,256]{2,1,0:T(8,128)S(1)} %get-tuple-element.11.rows_ref, f32[2,136,256]{2,1,0:T(8,128)S(1)} %collective-permute-done.1.halo_ref, f32[3,4,256]{2,1,0:T(4,128)S(1)} %get-tuple-element.13.flow_ref), custom_call_target="tpu_custom_call" | custom-call | flops 1769472 | bytes 1048576 | tf_op jit(solution)/shard_map/pallas_call | solution.py:210
  6.7 0.4 %collective-permute-start.4 = (f32[2,128,256]{2,1,0:T(8,128)S(1)}, f32[2,128,256]{2,1,0:T(8,128)S(1)}, u32[]{:S(2)}, u32[]{:S(2)}) collective-permute-start(f32[2,128,256]{2,1,0:T(8,128)S(1)} %shard_map.92.refs_0_), channel_id=1, source_target_pairs={{0,1},{1,0},{2,3},{3,2},{4,5},{5,4},{6,7},{7,6},{8,16},{9,17},{10,... | collective-permute-start | bytes 786440 | tf_op jit(solution)/shard_map/ppermute | solution.py:51
  7.1 2.8 %collective-permute-start.3 = (f32[2,128,256]{2,1,0:T(8,128)S(1)}, f32[2,128,256]{2,1,0:T(8,128)S(1)}, u32[]{:S(2)}, u32[]{:S(2)}) collective-permute-start(f32[2,128,256]{2,1,0:T(8,128)S(1)} %shard_map.92.refs_0_), channel_id=1, source_target_pairs={{0,8},{1,9},{2,10},{3,11},{4,12},{5,13},{6,14},{7,15},{8,0},{9,1},... | collective-permute-start | bytes 786440 | tf_op jit(solution)/shard_map/ppermute | solution.py:51
  9.9 0.6 %shard_map.93.refs_0_ = f32[2,128,256]{2,1,0:T(8,128)S(1)} custom-call(f32[4,128,256]{2,1,0:T(8,128)S(1)} %get-tuple-element.11.rows_ref, f32[2,136,256]{2,1,0:T(8,128)S(1)} %collective-permute-done.halo_ref, f32[3,4,256]{2,1,0:T(4,128)S(1)} %get-tuple-element.13.flow_ref, f32[2,128,256]{2,1,0:T(8,128)S(1)} %shard_map.92.refs_0_), custom_call_target="tpu_custom_call" | custom-call | flops 1769472 | bytes 1048576 | tf_op jit(solution)/shard_map/pallas_call | solution.py:210
  10.5 1.5 %collective-permute-start.2 = (f32[2,128,256]{2,1,0:T(8,128)S(1)}, f32[2,128,256]{2,1,0:T(8,128)S(1)}, u32[]{:S(2)}, u32[]{:S(2)}) collective-permute-start(f32[2,128,256]{2,1,0:T(8,128)S(1)} %shard_map.93.refs_0_), channel_id=1, source_target_pairs={{0,4},{1,5},{2,6},{3,7},{4,0},{5,1},{6,2},{7,3},{8,12},{9,13},{10,... | collective-permute-start | bytes 786440 | tf_op jit(solution)/shard_map/ppermute | solution.py:51
  12.1 0.1 stack.59
  12.2 0.1 copy.23
  12.3 4.2 %collective-permute-done.3.refs_1_ = f32[2,128,256]{2,1,0:T(8,128)S(1)} collective-permute-done((f32[2,128,256]{2,1,0:T(8,128)S(1)}, f32[2,128,256]{2,1,0:T(8,128)S(1)}, u32[]{:S(2)}, u32[]{:S(2)}) %collective-permute-start.3) | collective-permute-done | bytes 262176 | tf_op jit(solution)/shard_map/ppermute | solution.py:51
  16.5 0.2 shard_map.94.refs_2_
  16.6 1.3 %collective-permute-start.7 = (f32[2,128,256]{2,1,0:T(8,128)S(1)}, f32[2,128,256]{2,1,0:T(8,128)S(1)}, u32[]{:S(2)}, u32[]{:S(2)}) collective-permute-start(f32[2,128,256]{2,1,0:T(8,128)S(1)} %shard_map.94.refs_2_), channel_id=1, source_target_pairs={{0,4},{1,5},{2,6},{3,7},{4,0},{5,1},{6,2},{7,3},{8,12},{9,13},{10,... | collective-permute-start | bytes 786440 | tf_op jit(solution)/shard_map/ppermute | solution.py:51
  17.9 0.7 %collective-permute-done.2.refs_1_ = f32[2,128,256]{2,1,0:T(8,128)S(1)} collective-permute-done((f32[2,128,256]{2,1,0:T(8,128)S(1)}, f32[2,128,256]{2,1,0:T(8,128)S(1)}, u32[]{:S(2)}, u32[]{:S(2)}) %collective-permute-start.2) | collective-permute-done | bytes 262176 | tf_op jit(solution)/shard_map/ppermute | solution.py:51
  18.6 0.2 shard_map.95
  18.8 1.1 %collective-permute-start.5 = (f32[2,128,256]{2,1,0:T(8,128)S(1)}, f32[2,128,256]{2,1,0:T(8,128)S(1)}, u32[]{:S(2)}, u32[]{:S(2)}) collective-permute-start(f32[2,128,256]{2,1,0:T(8,128)S(1)} %get-tuple-element.15), channel_id=1, source_target_pairs={{0,8},{1,9},{2,10},{3,11},{4,12},{5,13},{6,14},{7,15},{8,0},{9,1},... | collective-permute-start | bytes 786440 | tf_op jit(solution)/shard_map/ppermute | solution.py:51
  19.9 0.1 subtract_multiply_fusion
  20.1 4.3 %collective-permute-done.7.refs_3_ = f32[2,128,256]{2,1,0:T(8,128)S(1)} collective-permute-done((f32[2,128,256]{2,1,0:T(8,128)S(1)}, f32[2,128,256]{2,1,0:T(8,128)S(1)}, u32[]{:S(2)}, u32[]{:S(2)}) %collective-permute-start.7) | collective-permute-done | bytes 262176 | tf_op jit(solution)/shard_map/ppermute | solution.py:51
  24.5 1.6 %shard_map.96.refs_4_ = f32[1,128,4,256]{3,2,1,0:T(4,128)} custom-call(f32[128,128]{1,0:T(8,128)S(1)} %pad.4.table_ref, bf16[256,384]{1,0:T(8,128)(2,1)S(1)} %pad_maximum_fusion.both_ref, f32[2,128,256]{2,1,0:T(8,128)S(1)} %shard_map.92.refs_0_, f32[2,128,256]{2,1,0:T(8,128)S(1)} %collective-permute-done.3.refs_1_, ...), custom_call_target="tpu_custom_call" | custom-call | flops 100663296 | bytes 1572864 | tf_op jit(solution)/shard_map/pallas_call | solution.py:285
  26.1 1.6 %shard_map.97 = f32[1,128,4,256]{3,2,1,0:T(4,128)} custom-call(f32[128,128]{1,0:T(8,128)S(1)} %pad.4.table_ref, bf16[256,384]{1,0:T(8,128)(2,1)S(1)} %pad_maximum_fusion.both_ref, f32[2,128,256]{2,1,0:T(8,128)S(1)} %shard_map.93.refs_0_, f32[2,128,256]{2,1,0:T(8,128)S(1)} %collective-permute-done.2.refs_1_, ...), custom_call_target="tpu_custom_call", output_to_operand_aliasing={{}: (6, {})} | custom-call | flops 100663296 | bytes 1572864 | tf_op jit(solution)/shard_map/pallas_call | solution.py:285
  (23 shorter events, 0.2 us)
Async XLA Ops:
  1.4 8.5 %collective-permute-start = (f32[2,136,256]{2,1,0:T(8,128)S(1)}, f32[2,136,256]{2,1,0:T(8,128)S(1)}, u32[]{:S(2)}, u32[]{:S(2)}) collective-permute-start(f32[2,136,256]{2,1,0:T(8,128)S(1)} %get-tuple-element.12), channel_id=1, source_target_pairs={{0,4},{1,2},{2,1},{3,7},{4,0},{5,6},{6,5},{7,3},{8,12},{9,10},{10,... | collective-permute-start | bytes 835592 | tf_op jit(solution)/shard_map/ppermute | solution.py:51
  4.4 1.6 %collective-permute-start.1 = (f32[2,136,256]{2,1,0:T(8,128)S(1)}, f32[2,136,256]{2,1,0:T(8,128)S(1)}, u32[]{:S(2)}, u32[]{:S(2)}) collective-permute-start(f32[2,136,256]{2,1,0:T(8,128)S(1)} %get-tuple-element.14), channel_id=1, source_target_pairs={{0,1},{1,0},{2,3},{3,2},{4,5},{5,4},{6,7},{7,6},{8,9},{9,8},{10,11... | collective-permute-start | bytes 835592 | tf_op jit(solution)/shard_map/ppermute | solution.py:51
  4.6 0.7 %copy-start = (f32[128]{0:T(128)S(1)}, f32[128]{0:T(128)}, u32[]{:S(2)}) copy-start(f32[128]{0:T(128)} %param.13) | copy-start | bytes 1540
  5.2 0.7 %copy-start.1 = (f32[8]{0:T(128)S(1)}, f32[8]{0:T(128)}, u32[]{:S(2)}) copy-start(f32[8]{0:T(128)} %param.15) | copy-start | bytes 100
  5.2 0.7 %copy-start.2 = (s32[128]{0:T(128)S(1)}, s32[128]{0:T(128)}, u32[]{:S(2)}) copy-start(s32[128]{0:T(128)} %param.14) | copy-start | bytes 1540
  5.2 0.7 %copy-start.3 = (f32[8]{0:T(128)S(1)}, f32[8]{0:T(128)}, u32[]{:S(2)}) copy-start(f32[8]{0:T(128)} %param.17) | copy-start | bytes 100
  5.2 0.7 %copy-start.4 = (f32[8]{0:T(128)S(1)}, f32[8]{0:T(128)}, u32[]{:S(2)}) copy-start(f32[8]{0:T(128)} %param.16) | copy-start | bytes 100
  6.7 5.6 %collective-permute-start.4 = (f32[2,128,256]{2,1,0:T(8,128)S(1)}, f32[2,128,256]{2,1,0:T(8,128)S(1)}, u32[]{:S(2)}, u32[]{:S(2)}) collective-permute-start(f32[2,128,256]{2,1,0:T(8,128)S(1)} %shard_map.92.refs_0_), channel_id=1, source_target_pairs={{0,1},{1,0},{2,3},{3,2},{4,5},{5,4},{6,7},{7,6},{8,16},{9,17},{10,... | collective-permute-start | bytes 786440 | tf_op jit(solution)/shard_map/ppermute | solution.py:51
  7.1 9.3 %collective-permute-start.3 = (f32[2,128,256]{2,1,0:T(8,128)S(1)}, f32[2,128,256]{2,1,0:T(8,128)S(1)}, u32[]{:S(2)}, u32[]{:S(2)}) collective-permute-start(f32[2,128,256]{2,1,0:T(8,128)S(1)} %shard_map.92.refs_0_), channel_id=1, source_target_pairs={{0,8},{1,9},{2,10},{3,11},{4,12},{5,13},{6,14},{7,15},{8,0},{9,1},... | collective-permute-start | bytes 786440 | tf_op jit(solution)/shard_map/ppermute | solution.py:51
  10.5 8.1 %collective-permute-start.2 = (f32[2,128,256]{2,1,0:T(8,128)S(1)}, f32[2,128,256]{2,1,0:T(8,128)S(1)}, u32[]{:S(2)}, u32[]{:S(2)}) collective-permute-start(f32[2,128,256]{2,1,0:T(8,128)S(1)} %shard_map.93.refs_0_), channel_id=1, source_target_pairs={{0,4},{1,5},{2,6},{3,7},{4,0},{5,1},{6,2},{7,3},{8,12},{9,13},{10,... | collective-permute-start | bytes 786440 | tf_op jit(solution)/shard_map/ppermute | solution.py:51
  16.6 7.8 %collective-permute-start.7 = (f32[2,128,256]{2,1,0:T(8,128)S(1)}, f32[2,128,256]{2,1,0:T(8,128)S(1)}, u32[]{:S(2)}, u32[]{:S(2)}) collective-permute-start(f32[2,128,256]{2,1,0:T(8,128)S(1)} %shard_map.94.refs_2_), channel_id=1, source_target_pairs={{0,4},{1,5},{2,6},{3,7},{4,0},{5,1},{6,2},{7,3},{8,12},{9,13},{10,... | collective-permute-start | bytes 786440 | tf_op jit(solution)/shard_map/ppermute | solution.py:51
  18.8 7.2 %collective-permute-start.5 = (f32[2,128,256]{2,1,0:T(8,128)S(1)}, f32[2,128,256]{2,1,0:T(8,128)S(1)}, u32[]{:S(2)}, u32[]{:S(2)}) collective-permute-start(f32[2,128,256]{2,1,0:T(8,128)S(1)} %get-tuple-element.15), channel_id=1, source_target_pairs={{0,8},{1,9},{2,10},{3,11},{4,12},{5,13},{6,14},{7,15},{8,0},{9,1},... | collective-permute-start | bytes 786440 | tf_op jit(solution)/shard_map/ppermute | solution.py:51
  19.9 6.1 %collective-permute-start.6 = (f32[2,128,256]{2,1,0:T(8,128)S(1)}, f32[2,128,256]{2,1,0:T(8,128)S(1)}, u32[]{:S(2)}, u32[]{:S(2)}) collective-permute-start(f32[2,128,256]{2,1,0:T(8,128)S(1)} %get-tuple-element.16), channel_id=1, source_target_pairs={{0,1},{1,0},{2,3},{3,2},{4,5},{5,4},{6,7},{7,6},{8,16},{9,17},{10,... | collective-permute-start | bytes 786440 | tf_op jit(solution)/shard_map/ppermute | solution.py:51

commit v4 on v3

--- a/solution.py
+++ b/solution.py
@@ -79,93 +79,74 @@
     return exchange(value, partner)
 
 
-def load_kernel(conc, vel_x, vel_y, mask, rows, near, *refs):
-    far, (flow, mask_rows, sems) = refs[:-3], refs[-3:]
-    count, bins, _ = rows.shape
-    part = bins // len(far)
+def load_kernel(conc, vel_x, vel_y, mask, near, far, flow, mask_rows, sems):
+    _, bins, count, _ = conc.shape
 
     def body(odd):
         near_at, far_at = (0, count - EDGE) if odd else (count - EDGE, 0)
-        copies = [pltpu.make_async_copy(mask, mask_rows, sems.at[0])]
-        copies.append(pltpu.make_async_copy(vel_x.at[0], flow.at[0], sems.at[1]))
-        copies.append(pltpu.make_async_copy(vel_y.at[0], flow.at[1], sems.at[2]))
-        edges = [(near, near_at, 0, bins)] + [(ref, far_at, i * part, part) for i, ref in enumerate(far)]
-        for target, at, low, size in edges:
+        copies = []
+        for target, at in ((far, far_at), (near, near_at)):
             for r in range(EDGE):
                 copies.append(
                     pltpu.make_async_copy(
-                        conc.at[0, pl.ds(low, size), at + r, :], target.at[r, pl.ds(0, size)], sems.at[len(copies)]
+                        conc.at[0, :, at + r, :], target.at[r, pl.ds(0, bins)], sems.at[len(copies)]
                     )
                 )
-        for r in range(count):
-            copies.append(pltpu.make_async_copy(conc.at[0, :, r, :], rows.at[r], sems.at[len(copies)]))
+        for source, target in ((mask, mask_rows), (vel_x.at[0], flow.at[0]), (vel_y.at[0], flow.at[1])):
+            copies.append(pltpu.make_async_copy(source, target, sems.at[len(copies)]))
         for copy in copies:
             copy.start()
-        for copy in copies[:3]:
+        for target in (far, near):
+            for r in range(EDGE):
+                target[r, bins:, :] = jnp.zeros_like(target[r, bins:, :])
+        for copy in copies[2 * EDGE :]:
             copy.wait()
         flow[2] = mask_rows[...].astype(jnp.float32)
-        for target, at, _, size in edges:
-            end = at if at == 0 else count - 1
-            for r in range(EDGE):
-                target[r, size:, :] = jnp.zeros_like(target[r, size:, :])
+        for target, at in ((far, far_at), (near, near_at)):
+            end = 0 if at == 0 else count - 1
             for i in range(3):
-                target[0, size + i : size + i + 1, :] = flow[i, end : end + 1, :]
-        for copy in copies[3:]:
+                target[0, bins + i : bins + i + 1, :] = flow[i, end : end + 1, :]
+        for copy in copies[: 2 * EDGE]:
             copy.wait()
 
     by_parity(body)
 
 
-def load(conc, vel_x, vel_y, mask, parts):
+def load(conc, vel_x, vel_y, mask):
     _, bins, count, cols = conc.shape
-
-    def edge(size):
-        return pltpu.VMEM((EDGE, size + SUBLANES, cols), jnp.float32)
-
-    rows, near, *far, flow = pl.pallas_call(
+    assert count == 2 * EDGE
+    edge = pltpu.VMEM((EDGE, bins + SUBLANES, cols), jnp.float32)
+    return pl.pallas_call(
         load_kernel,
-        out_shape=(
-            pltpu.VMEM((count, bins, cols), jnp.float32),
-            edge(bins),
-            *[edge(bins // parts)] * parts,
-            pltpu.VMEM((3, count, cols), jnp.float32),
-        ),
+        out_shape=(edge, edge, pltpu.VMEM((3, count, cols), jnp.float32)),
         in_specs=[HBM] * 4,
-        out_specs=(VMEM,) * (3 + parts),
-        scratch_shapes=[
-            pltpu.VMEM((count, cols), jnp.int32),
-            pltpu.SemaphoreType.DMA((3 + EDGE * (1 + parts) + count,)),
-        ],
+        out_specs=(VMEM,) * 3,
+        scratch_shapes=[pltpu.VMEM((count, cols), jnp.int32), pltpu.SemaphoreType.DMA((3 + 2 * EDGE,))],
         compiler_params=PARAMS,
     )(*in_hbm(conc, vel_x, vel_y, mask))
-    return rows, near, far, flow
-
-
-def horizontal_kernel(near, low, rows_ref, halo_ref, flow_ref, *refs):
+
+
+def horizontal_kernel(near, own_ref, other_ref, halo_ref, flow_ref, *refs):
     out_ref, scale_ref = refs[-2:]
-    count, _, cols = rows_ref.shape
-    bins = out_ref.shape[1]
+    _, bins, cols = out_ref.shape
+    count = flow_ref.shape[1]
     column = lax.broadcasted_iota(jnp.int32, (1, cols), 1)
-    block = 4 * SUBLANES
+    block = 16 * SUBLANES
 
     def body(odd):
         first = odd == near
-        base = 0 if first else count - 4
-
-        def row(i):
-            if first:
-                return (halo_ref, i) if i < EDGE else (rows_ref, i - EDGE)
-            return (rows_ref, base + i) if i < 4 else (halo_ref, i - 4)
+        order = (halo_ref, own_ref, other_ref) if first else (other_ref, own_ref, halo_ref)
+        base = 2 if first else 0
 
         band = lax.axis_index("xy")
         outside = jnp.logical_and(not near, jnp.logical_or(band == 0, band == lax.axis_size("xy") - 1))
         inside = jnp.where(outside, 0.0, 1.0)
         for i in range(1, 5):
-            ref, at = row(i)
-            if ref is halo_ref:
+            if order[i // EDGE] is halo_ref:
                 aux = halo_ref[0, bins : bins + SUBLANES, :]
                 x, y, water = aux[0:1], aux[1:2], aux[2:3] * inside
             else:
+                at = i - base
                 x, y, water = (flow_ref[part, at : at + 1, :] for part in range(3))
             x, y = 0.5 * x, 0.5 * y
             east = inside if i == 3 and not first else 1.0
@@ -194,10 +175,7 @@
             )
 
         for at in range(0, bins, block):
-            cells = {}
-            for i in range(6):
-                ref, place = row(i)
-                cells[i] = ref[place, pl.ds(at if ref is halo_ref else low + at, block), :]
+            cells = {i: order[i // EDGE][i % EDGE, pl.ds(at, block), :] for i in range(6)}
             once = {i: step(cells, i) for i in range(1, 5)}
             for i in range(EDGE):
                 out_ref[i, pl.ds(at, block), :] = step(once, EDGE + i)
@@ -205,17 +183,18 @@
     by_parity(body)
 
 
-def horizontal(near, rows, halo, flow, low, size, before=()):
-    cols = rows.shape[2]
+def horizontal(near, own, other, halo, flow, before=()):
+    _, bins, cols = own.shape
+    bins -= SUBLANES
     return pl.pallas_call(
-        functools.partial(horizontal_kernel, near, low),
-        out_shape=pltpu.VMEM((EDGE, size, cols), jnp.float32),
-        in_specs=[VMEM] * 3 + [ANY] * len(before),
+        functools.partial(horizontal_kernel, near),
+        out_shape=pltpu.VMEM((EDGE, bins, cols), jnp.float32),
+        in_specs=[VMEM] * 4 + [ANY] * len(before),
         out_specs=VMEM,
         scratch_shapes=[pltpu.VMEM((4, 5, SUBLANES, cols), jnp.float32)],
-        cost_estimate=pl.CostEstimate(flops=6 * 9 * size * cols, bytes_accessed=32 * size * cols, transcendentals=0),
+        cost_estimate=pl.CostEstimate(flops=6 * 9 * bins * cols, bytes_accessed=32 * bins * cols, transcendentals=0),
         compiler_params=PARAMS,
-    )(*in_vmem(rows, halo, flow, *before))
+    )(*in_vmem(own, other, halo, flow, *before))
 
 
 def weigh(table_ref, low, terms):
@@ -250,47 +229,49 @@
     return high, (value - high.astype(jnp.float32)).astype(jnp.bfloat16)
 
 
-def collide_kernel(near, parts, table_ref, both_ref, *refs):
+def collide_kernel(chunks, table_ref, both_ref, *refs):
     out_ref, done_ref, sems = refs[-3:]
-    count = out_ref.shape[2]
+    count, cols = out_ref.shape[2:]
 
     def body(odd):
-        at = 0 if odd == near else count - EDGE
-        copies = []
-        for r in range(EDGE):
-            first, pieces = 0, []
+        copies, first = [], 0
+        for near, parts in chunks:
+            at = 0 if odd == near else count - EDGE
+            rows = [[] for _ in range(EDGE)]
             for low, columns in parts:
                 cells = refs[first : first + len(columns)]
                 first += len(columns)
-                pieces.append(weigh(table_ref, low, [(column, ref[r]) for column, ref in zip(columns, cells)]))
-            cells = jnp.concatenate(pieces, 0)
+                for r in range(EDGE):
+                    rows[r].append(weigh(table_ref, low, [(column, ref[r]) for column, ref in zip(columns, cells)]))
+            cells = jnp.concatenate([jnp.concatenate(pieces, 0) for pieces in rows], 1)
             high, low = split(cells)
-            sums = jnp.dot(
-                both_ref[...], jnp.concatenate([high, low, high], 0), preferred_element_type=jnp.float32
-            )
-            done_ref[r] = cells + cells * sums[:NB] + sums[NB:]
-            copies.append(pltpu.make_async_copy(done_ref.at[r], out_ref.at[0, :, at + r, :], sems.at[r]))
-            copies[-1].start()
+            sums = jnp.dot(both_ref[...], jnp.concatenate([high, low, high], 0), preferred_element_type=jnp.float32)
+            result = cells + cells * sums[:NB] + sums[NB:]
+            for r in range(EDGE):
+                slot = len(copies)
+                done_ref[slot] = result[:, r * cols : (r + 1) * cols]
+                copies.append(pltpu.make_async_copy(done_ref.at[slot], out_ref.at[0, :, at + r, :], sems.at[slot]))
+                copies[-1].start()
         for copy in copies:
             copy.wait()
 
     by_parity(body)
 
 
-def collide(near, table, both, parts, shape, before=None):
+def collide(table, both, chunks, shape, before=None):
     rest = () if before is None else (before,)
-    cells = [value for _, terms in parts for _, value in terms]
-    parts = [(low, [column for column, _ in terms]) for low, terms in parts]
-    cols = shape[3]
+    cells = [value for _, parts in chunks for _, terms in parts for _, value in terms]
+    chunks = [(near, [(low, [column for column, _ in terms]) for low, terms in parts]) for near, parts in chunks]
+    rows, cols = EDGE * len(chunks), shape[3]
     return pl.pallas_call(
-        functools.partial(collide_kernel, near, parts),
+        functools.partial(collide_kernel, chunks),
         out_shape=pltpu.HBM(shape, jnp.float32),
         in_specs=[VMEM] * (2 + len(cells)) + [HBM] * len(rest),
         out_specs=HBM,
         input_output_aliases={2 + len(cells): 0} if rest else {},
-        scratch_shapes=[pltpu.VMEM((EDGE, NB, cols), jnp.float32), pltpu.SemaphoreType.DMA((EDGE,))],
+        scratch_shapes=[pltpu.VMEM((rows, NB, cols), jnp.float32), pltpu.SemaphoreType.DMA((rows,))],
         cost_estimate=pl.CostEstimate(
-            flops=12 * NB * NB * EDGE * cols, bytes_accessed=24 * EDGE * NB * cols, transcendentals=0
+            flops=12 * NB * NB * rows * cols, bytes_accessed=24 * rows * NB * cols, transcendentals=0
         ),
         compiler_params=PARAMS,
     )(*in_vmem(table, both, *cells), *in_hbm(*rest))
@@ -307,21 +288,14 @@
     agg_down,
     break_rate,
 ):
-    rows, near_edge, far_edges, flow = load(conc, vel_x, vel_y, sea_mask, 1)
+    near_edge, far_edge, flow = load(conc, vel_x, vel_y, sea_mask)
+    halo_chip = swap_chip(far_edge)
     halo_core = swap_core(near_edge)
-    halo_chip = [swap_chip(edge) for edge in far_edges]
-    part = NB // 1
-    near = horizontal(True, rows, halo_core, flow, 0, NB)
-    far = []
-    for i in reversed(range(1)):
-        far.insert(0, horizontal(False, rows, halo_chip[i], flow, i * part, part, (far or [near])[:1]))
+    near = horizontal(True, near_edge, far_edge, halo_core, flow)
+    far = horizontal(False, far_edge, near_edge, halo_chip, flow, (near,))
 
     def transported(is_far, low, high):
-        if not is_far:
-            return near[:, low:high]
-        if high - low > part:
-            return jnp.concatenate(far, 1)
-        return far[low // part][:, low % part : low % part + high - low]
+        return (near, far)[is_far][:, low:high]
 
     levels = lax.axis_size("bins")
     k = lax.axis_index("bins")
@@ -413,12 +387,9 @@
                 terms = [(4, cells[0]), (11, cells[1]), (12, cells[2]), (13, swap_pair(sends[0]))]
             before = tuple(sends[:1])
             parts[is_far].append((low, terms))
-    result = None
-    for is_far in (0, 1):
-        result = collide(
-            not is_far, table, both, sorted(parts[is_far], key=lambda item: item[0]), conc.shape, result
-        )
-    return result
+    chunks = [(not is_far, sorted(parts[is_far], key=lambda item: item[0])) for is_far in (0, 1)]
+    half = collide(table, both, chunks[:1], conc.shape)
+    return collide(table, both, chunks[1:], conc.shape, half)
 
 
 def solution(mesh):

time: 27.8 us -> 27 us (0.971)
  Pallas kernels: 6.19 us -> 4.99 us
  waiting for transfers between devices: 9.2 us -> 9.5 us
    pallas_call x5, Pallas kernels: 5.81 us -> 4.61 us  [the longest x2 2.36 us: collide(): pl.pallas_call(functools.partial(collide_kernel, chunks), out_shape=pltpu...]
    ppermute x8, waiting for transfers between devices: 9.2 us -> 9.5 us  [exchange(): return lax.ppermute(value, ('bins', 'xy'), pairs)]
  transfers between devices with their start and end apart: 8 -> 8, of which waited for: 3 -> 4; matrix products, arithmetic and copies ran while one was open for 2% -> 2% of each run, Pallas kernels for 12% -> 10%
where the time goes in v4:
time: 27 us; the launch traced here: 26.8 us
  starting transfers between devices  10.4 us (39%)
  waiting for transfers between devices  9.5 us (35%)
  Pallas kernels  4.99 us (18%)
  local copies, waits for them, and re-layouts  1.51 us (6%)
  other arithmetic  0.3 us (1%)
    ppermute x8, starting transfers between devices, exchange(): return lax.ppermute(value, ('bins', 'xy'), pairs)  10.4 us
    ppermute x8, waiting for transfers between devices, exchange(): return lax.ppermute(value, ('bins', 'xy'), pairs)  9.5 us
    pallas_call x2, Pallas kernels, collide(): pl.pallas_call(functools.partial(collide_kernel, chunks), out_shape=pltpu...  2.36 us
    unnamed x10, local copies, waits for them, and re-layouts  1.33 us
    pallas_call x1, Pallas kernels, load(): pl.pallas_call(load_kernel, out_shape=(edge, edge, pltpu.VMEM((3, count,...  1.16 us
    pallas_call x2, Pallas kernels, horizontal(): pl.pallas_call(functools.partial(horizontal_kernel, near), out_shape=pltp...  1.1 us
  transfers between devices with their start and end apart: 8, of which 4 were waited for; matrix products, arithmetic and copies ran while one was open for 2% of the time, Pallas kernels for 10%

profile of v4, /device:TPU:0, one launch (start us, length us, event | category | flops | bytes accessed | tf_op | source)
XLA Modules:
  0.0 26.8 jit_solution(1537377398666809451)
XLA Ops:
  0.0 1.2 %shard_map.91 = (f32[2,136,256]{2,1,0:T(8,128)S(1)}, f32[2,136,256]{2,1,0:T(8,128)S(1)}, f32[3,4,256]{2,1,0:T(4,128)S(1)}) custom-call(f32[1,128,4,256]{3,2,1,0:T(4,128)} %conc.1, f32[1,4,256]{2,1,0:T(4,128)} %vel_x.1, f32[1,4,256]{2,1,0:T(4,128)} %vel_y.1, s32[4,256]{1,0:T(4,128)} %mask.1), custom_call_target="tpu_custom_call" | custom-call | tf_op jit(solution)/shard_map/pallas_call | solution.py:119
  1.2 3.0 %collective-permute-start = (f32[2,136,256]{2,1,0:T(8,128)S(1)}, f32[2,136,256]{2,1,0:T(8,128)S(1)}, u32[]{:S(2)}, u32[]{:S(2)}) collective-permute-start(f32[2,136,256]{2,1,0:T(8,128)S(1)} %get-tuple-element.10.other_ref.own_ref), channel_id=1, source_target_pairs={{0,4},{1,2},{2,1},{3,7},{4,0},{5,6},{6,5},{7,3},{8,12},{9,10},{10,... | collective-permute-start | bytes 835592 | tf_op jit(solution)/shard_map/ppermute | solution.py:51
  4.2 0.1 collective-permute-start.1
  4.3 0.7 %copy-done = f32[128]{0:T(128)S(1)} copy-done((f32[128]{0:T(128)S(1)}, f32[128]{0:T(128)}, u32[]{:S(2)}) %copy-start) | copy-done | bytes 536
  5.0 0.6 %copy-done.1 = f32[8]{0:T(128)S(1)} copy-done((f32[8]{0:T(128)S(1)}, f32[8]{0:T(128)}, u32[]{:S(2)}) %copy-start.1) | copy-done | bytes 56
  5.7 0.1 select_reduce_fusion.1
  5.8 0.6 %shard_map.92.refs_0_ = f32[2,128,256]{2,1,0:T(8,128)S(1)} custom-call(f32[2,136,256]{2,1,0:T(8,128)S(1)} %get-tuple-element.11.own_ref.other_ref, f32[2,136,256]{2,1,0:T(8,128)S(1)} %get-tuple-element.10.other_ref.own_ref, f32[2,136,256]{2,1,0:T(8,128)S(1)} %collective-permute-done.1.halo_ref, f32[3,4,256]{2,1,0:T(4,128)S(1)} %get-tuple-element.12.flow_ref), custom_call_target="tpu_custom_call" | custom-call | flops 1769472 | bytes 1048576 | tf_op jit(solution)/shard_map/pallas_call | solution.py:189
  6.4 0.4 %collective-permute-start.4 = (f32[2,128,256]{2,1,0:T(8,128)S(1)}, f32[2,128,256]{2,1,0:T(8,128)S(1)}, u32[]{:S(2)}, u32[]{:S(2)}) collective-permute-start(f32[2,128,256]{2,1,0:T(8,128)S(1)} %shard_map.92.refs_0_), channel_id=1, source_target_pairs={{0,1},{1,0},{2,3},{3,2},{4,5},{5,4},{6,7},{7,6},{8,16},{9,17},{10,... | collective-permute-start | bytes 786440 | tf_op jit(solution)/shard_map/ppermute | solution.py:51
  6.8 2.8 %collective-permute-start.3 = (f32[2,128,256]{2,1,0:T(8,128)S(1)}, f32[2,128,256]{2,1,0:T(8,128)S(1)}, u32[]{:S(2)}, u32[]{:S(2)}) collective-permute-start(f32[2,128,256]{2,1,0:T(8,128)S(1)} %shard_map.92.refs_0_), channel_id=1, source_target_pairs={{0,8},{1,9},{2,10},{3,11},{4,12},{5,13},{6,14},{7,15},{8,0},{9,1},... | collective-permute-start | bytes 786440 | tf_op jit(solution)/shard_map/ppermute | solution.py:51
  9.6 0.5 %shard_map.93.refs_0_ = f32[2,128,256]{2,1,0:T(8,128)S(1)} custom-call(f32[2,136,256]{2,1,0:T(8,128)S(1)} %get-tuple-element.10.other_ref.own_ref, f32[2,136,256]{2,1,0:T(8,128)S(1)} %get-tuple-element.11.own_ref.other_ref, f32[2,136,256]{2,1,0:T(8,128)S(1)} %collective-permute-done.halo_ref, f32[3,4,256]{2,1,0:T(4,128)S(1)} %get-tuple-element.12.flow_ref, ...), custom_call_target="tpu_custom_call" | custom-call | flops 1769472 | bytes 1048576 | tf_op jit(solution)/shard_map/pallas_call | solution.py:189
  10.1 1.5 %collective-permute-start.2 = (f32[2,128,256]{2,1,0:T(8,128)S(1)}, f32[2,128,256]{2,1,0:T(8,128)S(1)}, u32[]{:S(2)}, u32[]{:S(2)}) collective-permute-start(f32[2,128,256]{2,1,0:T(8,128)S(1)} %shard_map.93.refs_0_), channel_id=1, source_target_pairs={{0,4},{1,5},{2,6},{3,7},{4,0},{5,1},{6,2},{7,3},{8,12},{9,13},{10,... | collective-permute-start | bytes 786440 | tf_op jit(solution)/shard_map/ppermute | solution.py:51
  11.7 0.1 stack.59
  11.8 0.1 copy.23
  11.9 4.2 %collective-permute-done.3.refs_1_ = f32[2,128,256]{2,1,0:T(8,128)S(1)} collective-permute-done((f32[2,128,256]{2,1,0:T(8,128)S(1)}, f32[2,128,256]{2,1,0:T(8,128)S(1)}, u32[]{:S(2)}, u32[]{:S(2)}) %collective-permute-start.3) | collective-permute-done | bytes 262176 | tf_op jit(solution)/shard_map/ppermute | solution.py:51
  16.1 0.2 shard_map.94.refs_2_
  16.3 1.3 %collective-permute-start.7 = (f32[2,128,256]{2,1,0:T(8,128)S(1)}, f32[2,128,256]{2,1,0:T(8,128)S(1)}, u32[]{:S(2)}, u32[]{:S(2)}) collective-permute-start(f32[2,128,256]{2,1,0:T(8,128)S(1)} %shard_map.94.refs_2_), channel_id=1, source_target_pairs={{0,4},{1,5},{2,6},{3,7},{4,0},{5,1},{6,2},{7,3},{8,12},{9,13},{10,... | collective-permute-start | bytes 786440 | tf_op jit(solution)/shard_map/ppermute | solution.py:51
  17.6 0.6 %collective-permute-done.2.refs_1_ = f32[2,128,256]{2,1,0:T(8,128)S(1)} collective-permute-done((f32[2,128,256]{2,1,0:T(8,128)S(1)}, f32[2,128,256]{2,1,0:T(8,128)S(1)}, u32[]{:S(2)}, u32[]{:S(2)}) %collective-permute-start.2) | collective-permute-done | bytes 262176 | tf_op jit(solution)/shard_map/ppermute | solution.py:51
  18.2 0.2 shard_map.95
  18.4 1.2 %collective-permute-start.5 = (f32[2,128,256]{2,1,0:T(8,128)S(1)}, f32[2,128,256]{2,1,0:T(8,128)S(1)}, u32[]{:S(2)}, u32[]{:S(2)}) collective-permute-start(f32[2,128,256]{2,1,0:T(8,128)S(1)} %get-tuple-element.13), channel_id=1, source_target_pairs={{0,8},{1,9},{2,10},{3,11},{4,12},{5,13},{6,14},{7,15},{8,0},{9,1},... | collective-permute-start | bytes 786440 | tf_op jit(solution)/shard_map/ppermute | solution.py:51
  19.6 0.1 subtract_multiply_fusion
  19.8 4.3 %collective-permute-done.7.refs_3_ = f32[2,128,256]{2,1,0:T(8,128)S(1)} collective-permute-done((f32[2,128,256]{2,1,0:T(8,128)S(1)}, f32[2,128,256]{2,1,0:T(8,128)S(1)}, u32[]{:S(2)}, u32[]{:S(2)}) %collective-permute-start.7) | collective-permute-done | bytes 262176 | tf_op jit(solution)/shard_map/ppermute | solution.py:51
  24.1 1.2 %shard_map.96.refs_4_ = f32[1,128,4,256]{3,2,1,0:T(4,128)} custom-call(f32[128,128]{1,0:T(8,128)S(1)} %pad.4.table_ref, bf16[256,384]{1,0:T(8,128)(2,1)S(1)} %pad_maximum_fusion.both_ref, f32[2,128,256]{2,1,0:T(8,128)S(1)} %shard_map.92.refs_0_, f32[2,128,256]{2,1,0:T(8,128)S(1)} %collective-permute-done.3.refs_1_, ...), custom_call_target="tpu_custom_call" | custom-call | flops 100663296 | bytes 1572864 | tf_op jit(solution)/shard_map/pallas_call | solution.py:266
  25.3 0.3 %collective-permute-done.5.refs_2_ = f32[2,128,256]{2,1,0:T(8,128)S(1)} collective-permute-done((f32[2,128,256]{2,1,0:T(8,128)S(1)}, f32[2,128,256]{2,1,0:T(8,128)S(1)}, u32[]{:S(2)}, u32[]{:S(2)}) %collective-permute-start.5) | collective-permute-done | bytes 262176 | tf_op jit(solution)/shard_map/ppermute | solution.py:51
  25.6 1.2 %shard_map.97 = f32[1,128,4,256]{3,2,1,0:T(4,128)} custom-call(f32[128,128]{1,0:T(8,128)S(1)} %pad.4.table_ref, bf16[256,384]{1,0:T(8,128)(2,1)S(1)} %pad_maximum_fusion.both_ref, f32[2,128,256]{2,1,0:T(8,128)S(1)} %shard_map.93.refs_0_, f32[2,128,256]{2,1,0:T(8,128)S(1)} %collective-permute-done.2.refs_1_, ...), custom_call_target="tpu_custom_call", output_to_operand_aliasing={{}: (6, {})} | custom-call | flops 100663296 | bytes 1572864 | tf_op jit(solution)/shard_map/pallas_call | solution.py:266
  (23 shorter events, 0.2 us)
Async XLA Ops:
  1.2 8.4 %collective-permute-start = (f32[2,136,256]{2,1,0:T(8,128)S(1)}, f32[2,136,256]{2,1,0:T(8,128)S(1)}, u32[]{:S(2)}, u32[]{:S(2)}) collective-permute-start(f32[2,136,256]{2,1,0:T(8,128)S(1)} %get-tuple-element.10.other_ref.own_ref), channel_id=1, source_target_pairs={{0,4},{1,2},{2,1},{3,7},{4,0},{5,6},{6,5},{7,3},{8,12},{9,10},{10,... | collective-permute-start | bytes 835592 | tf_op jit(solution)/shard_map/ppermute | solution.py:51
  4.2 1.6 %collective-permute-start.1 = (f32[2,136,256]{2,1,0:T(8,128)S(1)}, f32[2,136,256]{2,1,0:T(8,128)S(1)}, u32[]{:S(2)}, u32[]{:S(2)}) collective-permute-start(f32[2,136,256]{2,1,0:T(8,128)S(1)} %get-tuple-element.11.own_ref.other_ref), channel_id=1, source_target_pairs={{0,1},{1,0},{2,3},{3,2},{4,5},{5,4},{6,7},{7,6},{8,9},{9,8},{10,11... | collective-permute-start | bytes 835592 | tf_op jit(solution)/shard_map/ppermute | solution.py:51
  4.3 0.7 %copy-start = (f32[128]{0:T(128)S(1)}, f32[128]{0:T(128)}, u32[]{:S(2)}) copy-start(f32[128]{0:T(128)} %param.13) | copy-start | bytes 1540
  5.0 0.7 %copy-start.1 = (f32[8]{0:T(128)S(1)}, f32[8]{0:T(128)}, u32[]{:S(2)}) copy-start(f32[8]{0:T(128)} %param.15) | copy-start | bytes 100
  5.0 0.7 %copy-start.2 = (s32[128]{0:T(128)S(1)}, s32[128]{0:T(128)}, u32[]{:S(2)}) copy-start(s32[128]{0:T(128)} %param.14) | copy-start | bytes 1540
  5.0 0.7 %copy-start.3 = (f32[8]{0:T(128)S(1)}, f32[8]{0:T(128)}, u32[]{:S(2)}) copy-start(f32[8]{0:T(128)} %param.17) | copy-start | bytes 100
  5.0 0.7 %copy-start.4 = (f32[8]{0:T(128)S(1)}, f32[8]{0:T(128)}, u32[]{:S(2)}) copy-start(f32[8]{0:T(128)} %param.16) | copy-start | bytes 100
  6.4 5.5 %collective-permute-start.4 = (f32[2,128,256]{2,1,0:T(8,128)S(1)}, f32[2,128,256]{2,1,0:T(8,128)S(1)}, u32[]{:S(2)}, u32[]{:S(2)}) collective-permute-start(f32[2,128,256]{2,1,0:T(8,128)S(1)} %shard_map.92.refs_0_), channel_id=1, source_target_pairs={{0,1},{1,0},{2,3},{3,2},{4,5},{5,4},{6,7},{7,6},{8,16},{9,17},{10,... | collective-permute-start | bytes 786440 | tf_op jit(solution)/shard_map/ppermute | solution.py:51
  6.8 9.3 %collective-permute-start.3 = (f32[2,128,256]{2,1,0:T(8,128)S(1)}, f32[2,128,256]{2,1,0:T(8,128)S(1)}, u32[]{:S(2)}, u32[]{:S(2)}) collective-permute-start(f32[2,128,256]{2,1,0:T(8,128)S(1)} %shard_map.92.refs_0_), channel_id=1, source_target_pairs={{0,8},{1,9},{2,10},{3,11},{4,12},{5,13},{6,14},{7,15},{8,0},{9,1},... | collective-permute-start | bytes 786440 | tf_op jit(solution)/shard_map/ppermute | solution.py:51
  10.1 8.1 %collective-permute-start.2 = (f32[2,128,256]{2,1,0:T(8,128)S(1)}, f32[2,128,256]{2,1,0:T(8,128)S(1)}, u32[]{:S(2)}, u32[]{:S(2)}) collective-permute-start(f32[2,128,256]{2,1,0:T(8,128)S(1)} %shard_map.93.refs_0_), channel_id=1, source_target_pairs={{0,4},{1,5},{2,6},{3,7},{4,0},{5,1},{6,2},{7,3},{8,12},{9,13},{10,... | collective-permute-start | bytes 786440 | tf_op jit(solution)/shard_map/ppermute | solution.py:51
  16.3 7.8 %collective-permute-start.7 = (f32[2,128,256]{2,1,0:T(8,128)S(1)}, f32[2,128,256]{2,1,0:T(8,128)S(1)}, u32[]{:S(2)}, u32[]{:S(2)}) collective-permute-start(f32[2,128,256]{2,1,0:T(8,128)S(1)} %shard_map.94.refs_2_), channel_id=1, source_target_pairs={{0,4},{1,5},{2,6},{3,7},{4,0},{5,1},{6,2},{7,3},{8,12},{9,13},{10,... | collective-permute-start | bytes 786440 | tf_op jit(solution)/shard_map/ppermute | solution.py:51
  18.4 7.2 %collective-permute-start.5 = (f32[2,128,256]{2,1,0:T(8,128)S(1)}, f32[2,128,256]{2,1,0:T(8,128)S(1)}, u32[]{:S(2)}, u32[]{:S(2)}) collective-permute-start(f32[2,128,256]{2,1,0:T(8,128)S(1)} %get-tuple-element.13), channel_id=1, source_target_pairs={{0,8},{1,9},{2,10},{3,11},{4,12},{5,13},{6,14},{7,15},{8,0},{9,1},... | collective-permute-start | bytes 786440 | tf_op jit(solution)/shard_map/ppermute | solution.py:51
  19.6 6.0 %collective-permute-start.6 = (f32[2,128,256]{2,1,0:T(8,128)S(1)}, f32[2,128,256]{2,1,0:T(8,128)S(1)}, u32[]{:S(2)}, u32[]{:S(2)}) collective-permute-start(f32[2,128,256]{2,1,0:T(8,128)S(1)} %get-tuple-element.14), channel_id=1, source_target_pairs={{0,1},{1,0},{2,3},{3,2},{4,5},{5,4},{6,7},{7,6},{8,16},{9,17},{10,... | collective-permute-start | bytes 786440 | tf_op jit(solution)/shard_map/ppermute | solution.py:51

commit v5 on v4

--- a/solution.py
+++ b/solution.py
@@ -16,7 +16,7 @@
 collide_scale = 2.0
 SUBLANES = 8
 EDGE = 2
-CHUNKS = (((0, 0, 128, False),), ((1, 0, 128, True),))
+PARTS = 1
 VMEM = pl.BlockSpec(memory_space=pltpu.VMEM)
 HBM = pl.BlockSpec(memory_space=pltpu.HBM)
 ANY = pl.BlockSpec(memory_space=pl.ANY)
@@ -60,7 +60,7 @@
 
     def partner(level, band):
         to = band + 1 if band % 2 else band - 1
-        return (level, to) if 0 <= to < bands else (level ^ 1, band)
+        return (level, to) if 0 <= to < bands else (level ^ 2, band)
 
     return exchange(value, partner)
 
@@ -79,34 +79,38 @@
     return exchange(value, partner)
 
 
-def load_kernel(conc, vel_x, vel_y, mask, near, far, flow, mask_rows, sems):
+def load_kernel(conc, vel_x, vel_y, mask, near, *refs):
+    far, (flow, mask_rows, sems) = refs[:-3], refs[-3:]
     _, bins, count, _ = conc.shape
+    part = bins // len(far)
 
     def body(odd):
         near_at, far_at = (0, count - EDGE) if odd else (count - EDGE, 0)
+        edges = [(ref, far_at, i * part, part) for i, ref in enumerate(far)] + [(near, near_at, 0, bins)]
         copies = []
-        for target, at in ((far, far_at), (near, near_at)):
+        for target, at, low, size in edges:
             for r in range(EDGE):
                 copies.append(
                     pltpu.make_async_copy(
-                        conc.at[0, :, at + r, :], target.at[r, pl.ds(0, bins)], sems.at[len(copies)]
+                        conc.at[0, pl.ds(low, size), at + r, :], target.at[r, pl.ds(0, size)], sems.at[len(copies)]
                     )
                 )
+        rows = len(copies)
         for source, target in ((mask, mask_rows), (vel_x.at[0], flow.at[0]), (vel_y.at[0], flow.at[1])):
             copies.append(pltpu.make_async_copy(source, target, sems.at[len(copies)]))
         for copy in copies:
             copy.start()
-        for target in (far, near):
+        for target, _, _, size in edges:
             for r in range(EDGE):
-                target[r, bins:, :] = jnp.zeros_like(target[r, bins:, :])
-        for copy in copies[2 * EDGE :]:
+                target[r, size:, :] = jnp.zeros_like(target[r, size:, :])
+        for copy in copies[rows:]:
             copy.wait()
         flow[2] = mask_rows[...].astype(jnp.float32)
-        for target, at in ((far, far_at), (near, near_at)):
+        for target, at, _, size in edges:
             end = 0 if at == 0 else count - 1
             for i in range(3):
-                target[0, bins + i : bins + i + 1, :] = flow[i, end : end + 1, :]
-        for copy in copies[: 2 * EDGE]:
+                target[0, size + i : size + i + 1, :] = flow[i, end : end + 1, :]
+        for copy in copies[:rows]:
             copy.wait()
 
     by_parity(body)
@@ -115,34 +119,43 @@
 def load(conc, vel_x, vel_y, mask):
     _, bins, count, cols = conc.shape
     assert count == 2 * EDGE
-    edge = pltpu.VMEM((EDGE, bins + SUBLANES, cols), jnp.float32)
-    return pl.pallas_call(
+
+    def edge(size):
+        return pltpu.VMEM((EDGE, size + SUBLANES, cols), jnp.float32)
+
+    near, *far, flow = pl.pallas_call(
         load_kernel,
-        out_shape=(edge, edge, pltpu.VMEM((3, count, cols), jnp.float32)),
+        out_shape=(edge(bins), *[edge(bins // PARTS)] * PARTS, pltpu.VMEM((3, count, cols), jnp.float32)),
         in_specs=[HBM] * 4,
-        out_specs=(VMEM,) * 3,
-        scratch_shapes=[pltpu.VMEM((count, cols), jnp.int32), pltpu.SemaphoreType.DMA((3 + 2 * EDGE,))],
+        out_specs=(VMEM,) * (2 + PARTS),
+        scratch_shapes=[
+            pltpu.VMEM((count, cols), jnp.int32),
+            pltpu.SemaphoreType.DMA((3 + EDGE * (1 + PARTS),)),
+        ],
         compiler_params=PARAMS,
     )(*in_hbm(conc, vel_x, vel_y, mask))
-
-
-def horizontal_kernel(near, own_ref, other_ref, halo_ref, flow_ref, *refs):
+    return near, far, flow
+
+
+def horizontal_kernel(near, low, near_ref, *refs):
+    far_refs, (halo_ref, flow_ref) = refs[: 1 if low is not None else PARTS], refs[1 if low is not None else PARTS :][:2]
     out_ref, scale_ref = refs[-2:]
     _, bins, cols = out_ref.shape
+    share = NB // PARTS
     count = flow_ref.shape[1]
     column = lax.broadcasted_iota(jnp.int32, (1, cols), 1)
     block = 16 * SUBLANES
 
     def body(odd):
         first = odd == near
-        order = (halo_ref, own_ref, other_ref) if first else (other_ref, own_ref, halo_ref)
+        order = ("halo", "own", "other") if first else ("other", "own", "halo")
         base = 2 if first else 0
 
         band = lax.axis_index("xy")
         outside = jnp.logical_and(not near, jnp.logical_or(band == 0, band == lax.axis_size("xy") - 1))
         inside = jnp.where(outside, 0.0, 1.0)
         for i in range(1, 5):
-            if order[i // EDGE] is halo_ref:
+            if order[i // EDGE] == "halo":
                 aux = halo_ref[0, bins : bins + SUBLANES, :]
                 x, y, water = aux[0:1], aux[1:2], aux[2:3] * inside
             else:
@@ -175,7 +188,16 @@
             )
 
         for at in range(0, bins, block):
-            cells = {i: order[i // EDGE][i % EDGE, pl.ds(at, block), :] for i in range(6)}
+            cells = {}
+            for i in range(6):
+                kind = order[i // EDGE]
+                if kind == "halo":
+                    ref, place = halo_ref, at
+                elif (kind == "own") == near:
+                    ref, place = near_ref, at + (low or 0)
+                else:
+                    ref, place = far_refs[at // share], at % share
+                cells[i] = ref[i % EDGE, pl.ds(place, block), :]
             once = {i: step(cells, i) for i in range(1, 5)}
             for i in range(EDGE):
                 out_ref[i, pl.ds(at, block), :] = step(once, EDGE + i)
@@ -183,42 +205,51 @@
     by_parity(body)
 
 
-def horizontal(near, own, other, halo, flow, before=()):
-    _, bins, cols = own.shape
+def horizontal(low, near, far, halo, flow, before=()):
+    _, bins, cols = halo.shape
     bins -= SUBLANES
     return pl.pallas_call(
-        functools.partial(horizontal_kernel, near),
+        functools.partial(horizontal_kernel, low is None, low),
         out_shape=pltpu.VMEM((EDGE, bins, cols), jnp.float32),
-        in_specs=[VMEM] * 4 + [ANY] * len(before),
+        in_specs=[VMEM] * (3 + len(far)) + [ANY] * len(before),
         out_specs=VMEM,
         scratch_shapes=[pltpu.VMEM((4, 5, SUBLANES, cols), jnp.float32)],
         cost_estimate=pl.CostEstimate(flops=6 * 9 * bins * cols, bytes_accessed=32 * bins * cols, transcendentals=0),
         compiler_params=PARAMS,
-    )(*in_vmem(own, other, halo, flow, *before))
+    )(*in_vmem(near, *far, halo, flow, *before))
 
 
 def weigh(table_ref, low, terms):
     out = None
     for column, cells in terms:
-        part = table_ref[low : low + cells.shape[0], column : column + 1] * cells
+        part = cells if column is None else table_ref[low : low + cells.shape[0], column : column + 1] * cells
         out = part if out is None else out + part
     return out
 
 
-def combine_kernel(low, sums, width, table_ref, *refs):
-    cells, outs = refs[:width], refs[len(refs) - len(sums) :]
-    for r in range(EDGE):
-        for terms, out in zip(sums, outs):
-            out[r] = weigh(table_ref, low, [(column, cells[i][r]) for i, column in enumerate(terms)])
-
-
-def combine(table, low, cells, sums, before=()):
+def combine_kernel(sums, width, table_ref, *refs):
+    outs = refs[len(refs) - len(sums) :]
+    low = 0
+    while low < NB:
+        cells, refs = refs[:width], refs[width:]
+        size = cells[0].shape[1]
+        for r in range(EDGE):
+            for terms, out in zip(sums, outs):
+                out[r, pl.ds(low, size)] = weigh(table_ref, low, [(at, cells[i][r]) for i, at in enumerate(terms)])
+        low += size
+
+
+def combine(table, parts, sums, before=()):
+    cells = [value for part in parts for value in part]
+    shape = (EDGE, NB, cells[0].shape[2])
     outs = pl.pallas_call(
-        functools.partial(combine_kernel, low, sums, len(cells)),
-        out_shape=(pltpu.VMEM(cells[0].shape, jnp.float32),) * len(sums),
+        functools.partial(combine_kernel, sums, len(parts[0])),
+        out_shape=(pltpu.VMEM(shape, jnp.float32),) * len(sums),
         in_specs=[VMEM] * (1 + len(cells)) + [ANY] * len(before),
         out_specs=(VMEM,) * len(sums),
-        cost_estimate=pl.CostEstimate(flops=6 * cells[0].size, bytes_accessed=20 * cells[0].size, transcendentals=0),
+        cost_estimate=pl.CostEstimate(
+            flops=6 * NB * EDGE * shape[2], bytes_accessed=20 * NB * EDGE * shape[2], transcendentals=0
+        ),
         compiler_params=PARAMS,
     )(*in_vmem(table, *cells, *before))
     return list(outs)
@@ -288,14 +319,15 @@
     agg_down,
     break_rate,
 ):
-    near_edge, far_edge, flow = load(conc, vel_x, vel_y, sea_mask)
-    halo_chip = swap_chip(far_edge)
+    near_edge, far_edges, flow = load(conc, vel_x, vel_y, sea_mask)
+    halo_chip = [swap_chip(edge) for edge in far_edges]
     halo_core = swap_core(near_edge)
-    near = horizontal(True, near_edge, far_edge, halo_core, flow)
-    far = horizontal(False, far_edge, near_edge, halo_chip, flow, (near,))
-
-    def transported(is_far, low, high):
-        return (near, far)[is_far][:, low:high]
+    near = horizontal(None, near_edge, far_edges, halo_core, flow)
+    part = NB // PARTS
+    far, before = [], (near,)
+    for i, edge in enumerate(far_edges):
+        far.append(horizontal(i * part, near_edge, [edge], halo_chip[i], flow, before))
+        before = (far[-1],)
 
     levels = lax.axis_size("bins")
     k = lax.axis_index("bins")
@@ -321,8 +353,8 @@
     pair_far = jnp.where(odd, fall * (keep(k - 1) + keep(k - 2)), rise * (keep(k + 1) + keep(k + 2)))
     below, above = (k >= 2).astype(jnp.float32), (k + 2 < levels).astype(jnp.float32)
     there_0, there_1 = jnp.where(high_z, below, above), jnp.where(high_z, above, below)
-    far_0 = jnp.where(high_z, up2, down2) * there_0
-    far_1 = jnp.where(high_z, down2, up2) * there_1
+    from_0 = jnp.where(high_z, up2, down2) * there_0
+    from_1 = jnp.where(high_z, down2, up2) * there_1
     pair_far = pair_far * jnp.where(odd, below, above)
     uses_0 = odd == high_z
 
@@ -337,13 +369,13 @@
     index = jnp.arange(NB)
     i, j = index[None, :], index[:, None]
     weight = 1.0 / jnp.maximum(index, 1).astype(jnp.float32)
-    pairs = jnp.where(i < j, down_rate[:, None] * up_rate[None, :], 0.0) - jnp.where(
+    matrix = jnp.where(i < j, down_rate[:, None] * up_rate[None, :], 0.0) - jnp.where(
         i > j, up_rate[:, None] * down_rate[None, :], 0.0
     )
     pieces = jnp.where(i > j, (brk_rate * weight)[None, :], 0.0) - jnp.where(
         (i == j) & (j >= 1), brk_rate[:, None], 0.0
     )
-    both = jnp.concatenate([pairs * (step_duration * collide_scale / NB), pieces * step_duration], 0)
+    both = jnp.concatenate([matrix * (step_duration * collide_scale / NB), pieces * step_duration], 0)
 
     high = lax.reduce_precision(both, 8, 7)
     low = both - high
@@ -351,45 +383,21 @@
 
     columns = [
         send_0[0], send_0[1], send_1[0], send_1[1], on_self, from_pair, there_0 + zero, there_1 + zero,
-        pair_own, jnp.where(uses_0, pair_far, zero), jnp.where(uses_0, zero, pair_far), far_0, far_1, zero + 1.0,
+        pair_own, jnp.where(uses_0, pair_far, zero), jnp.where(uses_0, zero, pair_far), from_0, from_1, zero + 1.0,
     ]
     table = jnp.pad(jnp.stack(columns, 1), ((0, 0), (0, 128 - len(columns))))
 
-    first = []
-    for group in CHUNKS:
-        for is_far, low, high, x_first in group:
-            cells = transported(is_far, low, high)
-            if x_first:
-                first.append((cells, swap_pair(cells)))
-            elif True:
-                z1 = swap_far(cells, 1)
-                first.append((cells, swap_far(cells, 0), z1))
-            else:
-                first.append((cells, swap_far(cells, 0), swap_far(cells, 1)))
-    parts = [[], []]
-    before = ()
-    for group in CHUNKS:
-        came = [first.pop(0) for _ in group]
-        if len(group) > 1:
-            came = lax.optimization_barrier(came)
-        for (is_far, low, high, x_first), cells in zip(group, came):
-            if x_first:
-                sends = combine(table, low, cells, ((0, 1), (2, 3)), before)
-                if True:
-                    r1 = swap_far(sends[1], 1)
-                    r0 = swap_far(sends[0], 0)
-                else:
-                    r0 = swap_far(sends[0], 0)
-                    r1 = swap_far(sends[1], 1)
-                terms = [(4, cells[0]), (5, cells[1]), (6, r0), (7, r1)]
-            else:
-                sends = combine(table, low, cells, ((8, 9, 10),), before)
-                terms = [(4, cells[0]), (11, cells[1]), (12, cells[2]), (13, swap_pair(sends[0]))]
-            before = tuple(sends[:1])
-            parts[is_far].append((low, terms))
-    chunks = [(not is_far, sorted(parts[is_far], key=lambda item: item[0])) for is_far in (0, 1)]
-    half = collide(table, both, chunks[:1], conc.shape)
-    return collide(table, both, chunks[1:], conc.shape, half)
+    far_1 = swap_far(near, 1)
+    far_0 = swap_far(near, 0)
+    pairs_far = [(cells, swap_pair(cells)) for cells in far]
+    (send,) = combine(table, [(near, far_0, far_1)], ((8, 9, 10),))
+    pair = swap_pair(send)
+    sends = combine(table, pairs_far, ((0, 1),), (send,))
+    sends += combine(table, pairs_far, ((2, 3), (4, 5)), (sends[0],))
+    back_1 = swap_far(sends[1], 1)
+    back_0 = swap_far(sends[0], 0)
+    half = collide(table, both, [(True, [(0, [(4, near), (11, far_0), (12, far_1), (None, pair)])])], conc.shape)
+    return collide(table, both, [(False, [(0, [(None, sends[2]), (6, back_0), (7, back_1)])])], conc.shape, half)
 
 
 def solution(mesh):

time: 27 us -> 26.6 us (0.985)
  waiting for transfers between devices: 9.5 us -> 9.19 us
    ppermute x8, waiting for transfers between devices: 9.5 us -> 9.19 us  [exchange(): return lax.ppermute(value, ('bins', 'xy'), pairs)]
    pallas_call x5 -> x6, Pallas kernels: 2.64 us -> 2.76 us  [the longest x1 1.16 us: load(): pl.pallas_call(load_kernel, out_shape=(edge(bins), *[edge(bins // PARTS)]...]
  transfers between devices with their start and end apart: 8 -> 8, of which waited for: 4 -> 5; matrix products, arithmetic and copies ran while one was open for 2% -> 2% of each run, Pallas kernels for 10% -> 10%
where the time goes in v5:
time: 26.6 us; the launch traced here: 26.4 us
  starting transfers between devices  10.3 us (39%)
  waiting for transfers between devices  9.19 us (35%)
  Pallas kernels  5.05 us (19%)
  local copies, waits for them, and re-layouts  1.51 us (6%)
  other arithmetic  0.3 us (1%)
    ppermute x8, starting transfers between devices, exchange(): return lax.ppermute(value, ('bins', 'xy'), pairs)  10.3 us
    ppermute x8, waiting for transfers between devices, exchange(): return lax.ppermute(value, ('bins', 'xy'), pairs)  9.19 us
    pallas_call x2, Pallas kernels, collide(): pl.pallas_call(functools.partial(collide_kernel, chunks), out_shape=pltpu...  2.29 us
    unnamed x10, local copies, waits for them, and re-layouts  1.33 us
    pallas_call x1, Pallas kernels, load(): pl.pallas_call(load_kernel, out_shape=(edge(bins), *[edge(bins // PARTS)]...  1.16 us
    pallas_call x2, Pallas kernels, horizontal(): pl.pallas_call(functools.partial(horizontal_kernel, low is None, low), ou...  1.08 us
  transfers between devices with their start and end apart: 8, of which 5 were waited for; matrix products, arithmetic and copies ran while one was open for 2% of the time, Pallas kernels for 10%

profile of v5, /device:TPU:0, one launch (start us, length us, event | category | flops | bytes accessed | tf_op | source)
XLA Modules:
  0.0 26.4 jit_solution(2820346132631349914)
XLA Ops:
  0.0 1.2 %shard_map.91 = (f32[2,136,256]{2,1,0:T(8,128)S(1)}, f32[2,136,256]{2,1,0:T(8,128)S(1)}, f32[3,4,256]{2,1,0:T(4,128)S(1)}) custom-call(f32[1,128,4,256]{3,2,1,0:T(4,128)} %conc.1, f32[1,4,256]{2,1,0:T(4,128)} %vel_x.1, f32[1,4,256]{2,1,0:T(4,128)} %vel_y.1, s32[4,256]{1,0:T(4,128)} %mask.1), custom_call_target="tpu_custom_call" | custom-call | tf_op jit(solution)/shard_map/pallas_call | solution.py:126
  1.2 3.1 %collective-permute-start = (f32[2,136,256]{2,1,0:T(8,128)S(1)}, f32[2,136,256]{2,1,0:T(8,128)S(1)}, u32[]{:S(2)}, u32[]{:S(2)}) collective-permute-start(f32[2,136,256]{2,1,0:T(8,128)S(1)} %get-tuple-element.11.refs_0_), channel_id=1, source_target_pairs={{0,8},{1,2},{2,1},{3,11},{4,12},{5,6},{6,5},{7,15},{8,0},{9,10},{1... | collective-permute-start | bytes 835592 | tf_op jit(solution)/shard_map/ppermute | solution.py:51
  4.3 0.7 %copy-done = f32[128]{0:T(128)S(1)} copy-done((f32[128]{0:T(128)S(1)}, f32[128]{0:T(128)}, u32[]{:S(2)}) %copy-start) | copy-done | bytes 536
  5.0 0.6 %copy-done.1 = f32[8]{0:T(128)S(1)} copy-done((f32[8]{0:T(128)S(1)}, f32[8]{0:T(128)}, u32[]{:S(2)}) %copy-start.1) | copy-done | bytes 56
  5.7 0.1 select_reduce_fusion.1
  5.8 0.5 %shard_map.92.refs_3_.refs_0_ = f32[2,128,256]{2,1,0:T(8,128)S(1)} custom-call(f32[2,136,256]{2,1,0:T(8,128)S(1)} %get-tuple-element.10.near_ref, f32[2,136,256]{2,1,0:T(8,128)S(1)} %get-tuple-element.11.refs_0_, f32[2,136,256]{2,1,0:T(8,128)S(1)} %collective-permute-done.1.refs_1_, f32[3,4,256]{2,1,0:T(4,128)S(1)} %get-tuple-element.12.refs_2_), custom_call_target="tpu_custom_call" | custom-call | flops 1769472 | bytes 1048576 | tf_op jit(solution)/shard_map/pallas_call | solution.py:211
  6.4 1.6 %collective-permute-start.3 = (f32[2,128,256]{2,1,0:T(8,128)S(1)}, f32[2,128,256]{2,1,0:T(8,128)S(1)}, u32[]{:S(2)}, u32[]{:S(2)}) collective-permute-start(f32[2,128,256]{2,1,0:T(8,128)S(1)} %shard_map.92.refs_3_.refs_0_), channel_id=1, source_target_pairs={{0,8},{1,9},{2,10},{3,11},{4,12},{5,13},{6,14},{7,15},{8,0},{9,1},... | collective-permute-start | bytes 786440 | tf_op jit(solution)/shard_map/ppermute | solution.py:51
  8.0 0.8 %collective-permute-done.refs_1_ = f32[2,136,256]{2,1,0:T(8,128)S(1)} collective-permute-done((f32[2,136,256]{2,1,0:T(8,128)S(1)}, f32[2,136,256]{2,1,0:T(8,128)S(1)}, u32[]{:S(2)}, u32[]{:S(2)}) %collective-permute-start) | collective-permute-done | bytes 278560 | tf_op jit(solution)/shard_map/ppermute | solution.py:51
  8.8 0.5 %shard_map.93.refs_0_ = f32[2,128,256]{2,1,0:T(8,128)S(1)} custom-call(f32[2,136,256]{2,1,0:T(8,128)S(1)} %get-tuple-element.10.near_ref, f32[2,136,256]{2,1,0:T(8,128)S(1)} %get-tuple-element.11.refs_0_, f32[2,136,256]{2,1,0:T(8,128)S(1)} %collective-permute-done.refs_1_, f32[3,4,256]{2,1,0:T(4,128)S(1)} %get-tuple-element.12.refs_2_, ...), custom_call_target="tpu_custom_call" | custom-call | flops 1769472 | bytes 1048576 | tf_op jit(solution)/shard_map/pallas_call | solution.py:211
  9.3 2.0 %collective-permute-start.2 = (f32[2,128,256]{2,1,0:T(8,128)S(1)}, f32[2,128,256]{2,1,0:T(8,128)S(1)}, u32[]{:S(2)}, u32[]{:S(2)}) collective-permute-start(f32[2,128,256]{2,1,0:T(8,128)S(1)} %shard_map.93.refs_0_), channel_id=1, source_target_pairs={{0,4},{1,5},{2,6},{3,7},{4,0},{5,1},{6,2},{7,3},{8,12},{9,13},{10,... | collective-permute-start | bytes 786440 | tf_op jit(solution)/shard_map/ppermute | solution.py:51
  11.4 0.1 copy.23
  11.5 3.5 %collective-permute-done.3.refs_1_ = f32[2,128,256]{2,1,0:T(8,128)S(1)} collective-permute-done((f32[2,128,256]{2,1,0:T(8,128)S(1)}, f32[2,128,256]{2,1,0:T(8,128)S(1)}, u32[]{:S(2)}, u32[]{:S(2)}) %collective-permute-start.3) | collective-permute-done | bytes 262176 | tf_op jit(solution)/shard_map/ppermute | solution.py:51
  15.1 0.2 shard_map.94.refs_2_
  15.3 1.6 %collective-permute-start.7 = (f32[2,128,256]{2,1,0:T(8,128)S(1)}, f32[2,128,256]{2,1,0:T(8,128)S(1)}, u32[]{:S(2)}, u32[]{:S(2)}) collective-permute-start(f32[2,128,256]{2,1,0:T(8,128)S(1)} %shard_map.94.refs_2_), channel_id=1, source_target_pairs={{0,4},{1,5},{2,6},{3,7},{4,0},{5,1},{6,2},{7,3},{8,12},{9,13},{10,... | collective-permute-start | bytes 786440 | tf_op jit(solution)/shard_map/ppermute | solution.py:51
  16.8 0.9 %collective-permute-done.2.refs_1_ = f32[2,128,256]{2,1,0:T(8,128)S(1)} collective-permute-done((f32[2,128,256]{2,1,0:T(8,128)S(1)}, f32[2,128,256]{2,1,0:T(8,128)S(1)}, u32[]{:S(2)}, u32[]{:S(2)}) %collective-permute-start.2) | collective-permute-done | bytes 262176 | tf_op jit(solution)/shard_map/ppermute | solution.py:51
  17.7 0.1 shard_map.95.refs_2_
  17.8 1.9 %collective-permute-start.5 = (f32[2,128,256]{2,1,0:T(8,128)S(1)}, f32[2,128,256]{2,1,0:T(8,128)S(1)}, u32[]{:S(2)}, u32[]{:S(2)}) collective-permute-start(f32[2,128,256]{2,1,0:T(8,128)S(1)} %shard_map.95.refs_2_), channel_id=1, source_target_pairs={{0,8},{1,9},{2,10},{3,11},{4,12},{5,13},{6,14},{7,15},{8,0},{9,1},... | collective-permute-start | bytes 786440 | tf_op jit(solution)/shard_map/ppermute | solution.py:51
  19.7 0.2 shard_map.96
  19.9 0.1 collective-permute-start.6
  20.0 0.1 subtract_multiply_fusion
  20.2 3.1 %collective-permute-done.7.refs_3_ = f32[2,128,256]{2,1,0:T(8,128)S(1)} collective-permute-done((f32[2,128,256]{2,1,0:T(8,128)S(1)}, f32[2,128,256]{2,1,0:T(8,128)S(1)}, u32[]{:S(2)}, u32[]{:S(2)}) %collective-permute-start.7) | collective-permute-done | bytes 262176 | tf_op jit(solution)/shard_map/ppermute | solution.py:51
  23.3 1.2 %shard_map.97.refs_3_ = f32[1,128,4,256]{3,2,1,0:T(4,128)} custom-call(f32[128,128]{1,0:T(8,128)S(1)} %pad.4.table_ref, bf16[256,384]{1,0:T(8,128)(2,1)S(1)} %pad_maximum_fusion.both_ref, f32[2,128,256]{2,1,0:T(8,128)S(1)} %shard_map.92.refs_3_.refs_0_, f32[2,128,256]{2,1,0:T(8,128)S(1)} %collective-permute-done.3.refs_1_, ...), custom_call_target="tpu_custom_call" | custom-call | flops 100663296 | bytes 1572864 | tf_op jit(solution)/shard_map/pallas_call | solution.py:297
  24.5 0.9 %collective-permute-done.5.refs_1_ = f32[2,128,256]{2,1,0:T(8,128)S(1)} collective-permute-done((f32[2,128,256]{2,1,0:T(8,128)S(1)}, f32[2,128,256]{2,1,0:T(8,128)S(1)}, u32[]{:S(2)}, u32[]{:S(2)}) %collective-permute-start.5) | collective-permute-done | bytes 262176 | tf_op jit(solution)/shard_map/ppermute | solution.py:51
  25.3 1.1 %shard_map.98 = f32[1,128,4,256]{3,2,1,0:T(4,128)} custom-call(f32[128,128]{1,0:T(8,128)S(1)} %pad.4.table_ref, bf16[256,384]{1,0:T(8,128)(2,1)S(1)} %pad_maximum_fusion.both_ref, f32[2,128,256]{2,1,0:T(8,128)S(1)} %get-tuple-element.13.refs_0_, f32[2,128,256]{2,1,0:T(8,128)S(1)} %collective-permute-done.5.refs_1_, ...), custom_call_target="tpu_custom_call", output_to_operand_aliasing={{}: (5, {})} | custom-call | flops 100663296 | bytes 1572864 | tf_op jit(solution)/shard_map/pallas_call | solution.py:297
  (24 shorter events, 0.3 us)
Async XLA Ops:
  1.2 7.6 %collective-permute-start = (f32[2,136,256]{2,1,0:T(8,128)S(1)}, f32[2,136,256]{2,1,0:T(8,128)S(1)}, u32[]{:S(2)}, u32[]{:S(2)}) collective-permute-start(f32[2,136,256]{2,1,0:T(8,128)S(1)} %get-tuple-element.11.refs_0_), channel_id=1, source_target_pairs={{0,8},{1,2},{2,1},{3,11},{4,12},{5,6},{6,5},{7,15},{8,0},{9,10},{1... | collective-permute-start | bytes 835592 | tf_op jit(solution)/shard_map/ppermute | solution.py:51
  4.3 1.6 %collective-permute-start.1 = (f32[2,136,256]{2,1,0:T(8,128)S(1)}, f32[2,136,256]{2,1,0:T(8,128)S(1)}, u32[]{:S(2)}, u32[]{:S(2)}) collective-permute-start(f32[2,136,256]{2,1,0:T(8,128)S(1)} %get-tuple-element.10.near_ref), channel_id=1, source_target_pairs={{0,1},{1,0},{2,3},{3,2},{4,5},{5,4},{6,7},{7,6},{8,9},{9,8},{10,11... | collective-permute-start | bytes 835592 | tf_op jit(solution)/shard_map/ppermute | solution.py:51
  4.3 0.7 %copy-start = (f32[128]{0:T(128)S(1)}, f32[128]{0:T(128)}, u32[]{:S(2)}) copy-start(f32[128]{0:T(128)} %param.13) | copy-start | bytes 1540
  5.0 0.7 %copy-start.1 = (f32[8]{0:T(128)S(1)}, f32[8]{0:T(128)}, u32[]{:S(2)}) copy-start(f32[8]{0:T(128)} %param.15) | copy-start | bytes 100
  5.0 0.7 %copy-start.2 = (s32[128]{0:T(128)S(1)}, s32[128]{0:T(128)}, u32[]{:S(2)}) copy-start(s32[128]{0:T(128)} %param.14) | copy-start | bytes 1540
  5.0 0.7 %copy-start.3 = (f32[8]{0:T(128)S(1)}, f32[8]{0:T(128)}, u32[]{:S(2)}) copy-start(f32[8]{0:T(128)} %param.17) | copy-start | bytes 100
  5.0 0.7 %copy-start.4 = (f32[8]{0:T(128)S(1)}, f32[8]{0:T(128)}, u32[]{:S(2)}) copy-start(f32[8]{0:T(128)} %param.16) | copy-start | bytes 100
  6.4 8.7 %collective-permute-start.3 = (f32[2,128,256]{2,1,0:T(8,128)S(1)}, f32[2,128,256]{2,1,0:T(8,128)S(1)}, u32[]{:S(2)}, u32[]{:S(2)}) collective-permute-start(f32[2,128,256]{2,1,0:T(8,128)S(1)} %shard_map.92.refs_3_.refs_0_), channel_id=1, source_target_pairs={{0,8},{1,9},{2,10},{3,11},{4,12},{5,13},{6,14},{7,15},{8,0},{9,1},... | collective-permute-start | bytes 786440 | tf_op jit(solution)/shard_map/ppermute | solution.py:51
  8.0 7.1 %collective-permute-start.4 = (f32[2,128,256]{2,1,0:T(8,128)S(1)}, f32[2,128,256]{2,1,0:T(8,128)S(1)}, u32[]{:S(2)}, u32[]{:S(2)}) collective-permute-start(f32[2,128,256]{2,1,0:T(8,128)S(1)} %shard_map.92.refs_3_.refs_0_), channel_id=1, source_target_pairs={{0,1},{1,0},{2,3},{3,2},{4,5},{5,4},{6,7},{7,6},{8,16},{9,17},{10,... | collective-permute-start | bytes 786440 | tf_op jit(solution)/shard_map/ppermute | solution.py:51
  9.3 8.4 %collective-permute-start.2 = (f32[2,128,256]{2,1,0:T(8,128)S(1)}, f32[2,128,256]{2,1,0:T(8,128)S(1)}, u32[]{:S(2)}, u32[]{:S(2)}) collective-permute-start(f32[2,128,256]{2,1,0:T(8,128)S(1)} %shard_map.93.refs_0_), channel_id=1, source_target_pairs={{0,4},{1,5},{2,6},{3,7},{4,0},{5,1},{6,2},{7,3},{8,12},{9,13},{10,... | collective-permute-start | bytes 786440 | tf_op jit(solution)/shard_map/ppermute | solution.py:51
  15.3 8.0 %collective-permute-start.7 = (f32[2,128,256]{2,1,0:T(8,128)S(1)}, f32[2,128,256]{2,1,0:T(8,128)S(1)}, u32[]{:S(2)}, u32[]{:S(2)}) collective-permute-start(f32[2,128,256]{2,1,0:T(8,128)S(1)} %shard_map.94.refs_2_), channel_id=1, source_target_pairs={{0,4},{1,5},{2,6},{3,7},{4,0},{5,1},{6,2},{7,3},{8,12},{9,13},{10,... | collective-permute-start | bytes 786440 | tf_op jit(solution)/shard_map/ppermute | solution.py:51
  17.8 7.5 %collective-permute-start.5 = (f32[2,128,256]{2,1,0:T(8,128)S(1)}, f32[2,128,256]{2,1,0:T(8,128)S(1)}, u32[]{:S(2)}, u32[]{:S(2)}) collective-permute-start(f32[2,128,256]{2,1,0:T(8,128)S(1)} %shard_map.95.refs_2_), channel_id=1, source_target_pairs={{0,8},{1,9},{2,10},{3,11},{4,12},{5,13},{6,14},{7,15},{8,0},{9,1},... | collective-permute-start | bytes 786440 | tf_op jit(solution)/shard_map/ppermute | solution.py:51
  19.9 5.4 %collective-permute-start.6 = (f32[2,128,256]{2,1,0:T(8,128)S(1)}, f32[2,128,256]{2,1,0:T(8,128)S(1)}, u32[]{:S(2)}, u32[]{:S(2)}) collective-permute-start(f32[2,128,256]{2,1,0:T(8,128)S(1)} %get-tuple-element.14), channel_id=1, source_target_pairs={{0,1},{1,0},{2,3},{3,2},{4,5},{5,4},{6,7},{7,6},{8,16},{9,17},{10,... | collective-permute-start | bytes 786440 | tf_op jit(solution)/shard_map/ppermute | solution.py:51

commit v6 on v5

--- a/solution.py
+++ b/solution.py
@@ -222,7 +222,7 @@
 def weigh(table_ref, low, terms):
     out = None
     for column, cells in terms:
-        part = cells if column is None else table_ref[low : low + cells.shape[0], column : column + 1] * cells
+        part = cells if column is None else column * cells if not isinstance(column, int) else table_ref[low : low + cells.shape[0], column : column + 1] * cells
         out = part if out is None else out + part
     return out
 
@@ -264,6 +264,11 @@
     out_ref, done_ref, sems = refs[-3:]
     count, cols = out_ref.shape[2:]
 
+    levels, k = lax.axis_size("bins"), lax.axis_index("bins")
+    below, above = jnp.where(k >= 2, 1.0, 0.0), jnp.where(k + 2 < levels, 1.0, 0.0)
+    high_z = (k // 2) % 2 == 1
+    there = {"there_0": jnp.where(high_z, below, above), "there_1": jnp.where(high_z, above, below)}
+
     def body(odd):
         copies, first = [], 0
         for near, parts in chunks:
@@ -273,7 +278,9 @@
                 cells = refs[first : first + len(columns)]
                 first += len(columns)
                 for r in range(EDGE):
-                    rows[r].append(weigh(table_ref, low, [(column, ref[r]) for column, ref in zip(columns, cells)]))
+                    rows[r].append(
+                        weigh(table_ref, low, [(there.get(column, column), ref[r]) for column, ref in zip(columns, cells)])
+                    )
             cells = jnp.concatenate([jnp.concatenate(pieces, 0) for pieces in rows], 1)
             high, low = split(cells)
             sums = jnp.dot(both_ref[...], jnp.concatenate([high, low, high], 0), preferred_element_type=jnp.float32)
@@ -397,7 +404,7 @@
     back_1 = swap_far(sends[1], 1)
     back_0 = swap_far(sends[0], 0)
     half = collide(table, both, [(True, [(0, [(4, near), (11, far_0), (12, far_1), (None, pair)])])], conc.shape)
-    return collide(table, both, [(False, [(0, [(None, sends[2]), (6, back_0), (7, back_1)])])], conc.shape, half)
+    return collide(table, both, [(False, [(0, [(None, sends[2]), ("there_0", back_0), ("there_1", back_1)])])], conc.shape, half)
 
 
 def solution(mesh):

time: 26.6 us -> 26.6 us (level)
  no operation moved by 1% of the time
where the time goes in v6:
time: 26.6 us; the launch traced here: 26.4 us
  starting transfers between devices  10.3 us (39%)
  waiting for transfers between devices  9.19 us (35%)
  Pallas kernels  4.97 us (19%)
  local copies, waits for them, and re-layouts  1.51 us (6%)
  other arithmetic  0.3 us (1%)
    ppermute x8, starting transfers between devices, exchange(): return lax.ppermute(value, ('bins', 'xy'), pairs)  10.3 us
    ppermute x8, waiting for transfers between devices, exchange(): return lax.ppermute(value, ('bins', 'xy'), pairs)  9.19 us
    pallas_call x2, Pallas kernels, collide(): pl.pallas_call(functools.partial(collide_kernel, chunks), out_shape=pltpu...  2.21 us
    unnamed x10, local copies, waits for them, and re-layouts  1.33 us
    pallas_call x1, Pallas kernels, load(): pl.pallas_call(load_kernel, out_shape=(edge(bins), *[edge(bins // PARTS)]...  1.16 us
    pallas_call x2, Pallas kernels, horizontal(): pl.pallas_call(functools.partial(horizontal_kernel, low is None, low), ou...  1.08 us
  transfers between devices with their start and end apart: 8, of which 5 were waited for; matrix products, arithmetic and copies ran while one was open for 2% of the time, Pallas kernels for 10%

profile of v6, /device:TPU:0, one launch (start us, length us, event | category | flops | bytes accessed | tf_op | source)
XLA Modules:
  0.0 26.4 jit_solution(340668797036744265)
XLA Ops:
  0.0 1.2 %shard_map.91 = (f32[2,136,256]{2,1,0:T(8,128)S(1)}, f32[2,136,256]{2,1,0:T(8,128)S(1)}, f32[3,4,256]{2,1,0:T(4,128)S(1)}) custom-call(f32[1,128,4,256]{3,2,1,0:T(4,128)} %conc.1, f32[1,4,256]{2,1,0:T(4,128)} %vel_x.1, f32[1,4,256]{2,1,0:T(4,128)} %vel_y.1, s32[4,256]{1,0:T(4,128)} %mask.1), custom_call_target="tpu_custom_call" | custom-call | tf_op jit(solution)/shard_map/pallas_call | solution.py:126
  1.2 3.1 %collective-permute-start = (f32[2,136,256]{2,1,0:T(8,128)S(1)}, f32[2,136,256]{2,1,0:T(8,128)S(1)}, u32[]{:S(2)}, u32[]{:S(2)}) collective-permute-start(f32[2,136,256]{2,1,0:T(8,128)S(1)} %get-tuple-element.11.refs_0_), channel_id=1, source_target_pairs={{0,8},{1,2},{2,1},{3,11},{4,12},{5,6},{6,5},{7,15},{8,0},{9,10},{1... | collective-permute-start | bytes 835592 | tf_op jit(solution)/shard_map/ppermute | solution.py:51
  4.3 0.7 %copy-done = f32[128]{0:T(128)S(1)} copy-done((f32[128]{0:T(128)S(1)}, f32[128]{0:T(128)}, u32[]{:S(2)}) %copy-start) | copy-done | bytes 536
  5.0 0.6 %copy-done.1 = f32[8]{0:T(128)S(1)} copy-done((f32[8]{0:T(128)S(1)}, f32[8]{0:T(128)}, u32[]{:S(2)}) %copy-start.1) | copy-done | bytes 56
  5.7 0.1 select_reduce_fusion.1
  5.8 0.5 %shard_map.92.refs_3_.refs_0_ = f32[2,128,256]{2,1,0:T(8,128)S(1)} custom-call(f32[2,136,256]{2,1,0:T(8,128)S(1)} %get-tuple-element.10.near_ref, f32[2,136,256]{2,1,0:T(8,128)S(1)} %get-tuple-element.11.refs_0_, f32[2,136,256]{2,1,0:T(8,128)S(1)} %collective-permute-done.1.refs_1_, f32[3,4,256]{2,1,0:T(4,128)S(1)} %get-tuple-element.12.refs_2_), custom_call_target="tpu_custom_call" | custom-call | flops 1769472 | bytes 1048576 | tf_op jit(solution)/shard_map/pallas_call | solution.py:211
  6.4 1.6 %collective-permute-start.3 = (f32[2,128,256]{2,1,0:T(8,128)S(1)}, f32[2,128,256]{2,1,0:T(8,128)S(1)}, u32[]{:S(2)}, u32[]{:S(2)}) collective-permute-start(f32[2,128,256]{2,1,0:T(8,128)S(1)} %shard_map.92.refs_3_.refs_0_), channel_id=1, source_target_pairs={{0,8},{1,9},{2,10},{3,11},{4,12},{5,13},{6,14},{7,15},{8,0},{9,1},... | collective-permute-start | bytes 786440 | tf_op jit(solution)/shard_map/ppermute | solution.py:51
  8.0 0.8 %collective-permute-done.refs_1_ = f32[2,136,256]{2,1,0:T(8,128)S(1)} collective-permute-done((f32[2,136,256]{2,1,0:T(8,128)S(1)}, f32[2,136,256]{2,1,0:T(8,128)S(1)}, u32[]{:S(2)}, u32[]{:S(2)}) %collective-permute-start) | collective-permute-done | bytes 278560 | tf_op jit(solution)/shard_map/ppermute | solution.py:51
  8.8 0.5 %shard_map.93.refs_0_ = f32[2,128,256]{2,1,0:T(8,128)S(1)} custom-call(f32[2,136,256]{2,1,0:T(8,128)S(1)} %get-tuple-element.10.near_ref, f32[2,136,256]{2,1,0:T(8,128)S(1)} %get-tuple-element.11.refs_0_, f32[2,136,256]{2,1,0:T(8,128)S(1)} %collective-permute-done.refs_1_, f32[3,4,256]{2,1,0:T(4,128)S(1)} %get-tuple-element.12.refs_2_, ...), custom_call_target="tpu_custom_call" | custom-call | flops 1769472 | bytes 1048576 | tf_op jit(solution)/shard_map/pallas_call | solution.py:211
  9.3 2.0 %collective-permute-start.2 = (f32[2,128,256]{2,1,0:T(8,128)S(1)}, f32[2,128,256]{2,1,0:T(8,128)S(1)}, u32[]{:S(2)}, u32[]{:S(2)}) collective-permute-start(f32[2,128,256]{2,1,0:T(8,128)S(1)} %shard_map.93.refs_0_), channel_id=1, source_target_pairs={{0,4},{1,5},{2,6},{3,7},{4,0},{5,1},{6,2},{7,3},{8,12},{9,13},{10,... | collective-permute-start | bytes 786440 | tf_op jit(solution)/shard_map/ppermute | solution.py:51
  11.4 0.1 copy.23
  11.5 3.5 %collective-permute-done.3.refs_1_ = f32[2,128,256]{2,1,0:T(8,128)S(1)} collective-permute-done((f32[2,128,256]{2,1,0:T(8,128)S(1)}, f32[2,128,256]{2,1,0:T(8,128)S(1)}, u32[]{:S(2)}, u32[]{:S(2)}) %collective-permute-start.3) | collective-permute-done | bytes 262176 | tf_op jit(solution)/shard_map/ppermute | solution.py:51
  15.1 0.2 shard_map.94.refs_2_
  15.3 1.6 %collective-permute-start.7 = (f32[2,128,256]{2,1,0:T(8,128)S(1)}, f32[2,128,256]{2,1,0:T(8,128)S(1)}, u32[]{:S(2)}, u32[]{:S(2)}) collective-permute-start(f32[2,128,256]{2,1,0:T(8,128)S(1)} %shard_map.94.refs_2_), channel_id=1, source_target_pairs={{0,4},{1,5},{2,6},{3,7},{4,0},{5,1},{6,2},{7,3},{8,12},{9,13},{10,... | collective-permute-start | bytes 786440 | tf_op jit(solution)/shard_map/ppermute | solution.py:51
  16.8 0.9 %collective-permute-done.2.refs_1_ = f32[2,128,256]{2,1,0:T(8,128)S(1)} collective-permute-done((f32[2,128,256]{2,1,0:T(8,128)S(1)}, f32[2,128,256]{2,1,0:T(8,128)S(1)}, u32[]{:S(2)}, u32[]{:S(2)}) %collective-permute-start.2) | collective-permute-done | bytes 262176 | tf_op jit(solution)/shard_map/ppermute | solution.py:51
  17.7 0.1 shard_map.95.refs_2_
  17.8 1.9 %collective-permute-start.5 = (f32[2,128,256]{2,1,0:T(8,128)S(1)}, f32[2,128,256]{2,1,0:T(8,128)S(1)}, u32[]{:S(2)}, u32[]{:S(2)}) collective-permute-start(f32[2,128,256]{2,1,0:T(8,128)S(1)} %shard_map.95.refs_2_), channel_id=1, source_target_pairs={{0,8},{1,9},{2,10},{3,11},{4,12},{5,13},{6,14},{7,15},{8,0},{9,1},... | collective-permute-start | bytes 786440 | tf_op jit(solution)/shard_map/ppermute | solution.py:51
  19.7 0.2 shard_map.96
  19.9 0.1 collective-permute-start.6
  20.0 0.1 subtract_multiply_fusion
  20.2 3.1 %collective-permute-done.7.refs_3_ = f32[2,128,256]{2,1,0:T(8,128)S(1)} collective-permute-done((f32[2,128,256]{2,1,0:T(8,128)S(1)}, f32[2,128,256]{2,1,0:T(8,128)S(1)}, u32[]{:S(2)}, u32[]{:S(2)}) %collective-permute-start.7) | collective-permute-done | bytes 262176 | tf_op jit(solution)/shard_map/ppermute | solution.py:51
  23.3 1.2 %shard_map.97.refs_3_ = f32[1,128,4,256]{3,2,1,0:T(4,128)} custom-call(f32[128,128]{1,0:T(8,128)S(1)} %pad.4.table_ref, bf16[256,384]{1,0:T(8,128)(2,1)S(1)} %pad_maximum_fusion.both_ref, f32[2,128,256]{2,1,0:T(8,128)S(1)} %shard_map.92.refs_3_.refs_0_, f32[2,128,256]{2,1,0:T(8,128)S(1)} %collective-permute-done.3.refs_1_, ...), custom_call_target="tpu_custom_call" | custom-call | flops 100663296 | bytes 1572864 | tf_op jit(solution)/shard_map/pallas_call | solution.py:304
  24.5 0.9 %collective-permute-done.5.refs_1_ = f32[2,128,256]{2,1,0:T(8,128)S(1)} collective-permute-done((f32[2,128,256]{2,1,0:T(8,128)S(1)}, f32[2,128,256]{2,1,0:T(8,128)S(1)}, u32[]{:S(2)}, u32[]{:S(2)}) %collective-permute-start.5) | collective-permute-done | bytes 262176 | tf_op jit(solution)/shard_map/ppermute | solution.py:51
  25.3 1.1 %shard_map.98 = f32[1,128,4,256]{3,2,1,0:T(4,128)} custom-call(f32[128,128]{1,0:T(8,128)S(1)} %pad.4.table_ref, bf16[256,384]{1,0:T(8,128)(2,1)S(1)} %pad_maximum_fusion.both_ref, f32[2,128,256]{2,1,0:T(8,128)S(1)} %get-tuple-element.13.refs_0_, f32[2,128,256]{2,1,0:T(8,128)S(1)} %collective-permute-done.5.refs_1_, ...), custom_call_target="tpu_custom_call", output_to_operand_aliasing={{}: (5, {})} | custom-call | flops 100663296 | bytes 1572864 | tf_op jit(solution)/shard_map/pallas_call | solution.py:304
  (24 shorter events, 0.3 us)
Async XLA Ops:
  1.2 7.6 %collective-permute-start = (f32[2,136,256]{2,1,0:T(8,128)S(1)}, f32[2,136,256]{2,1,0:T(8,128)S(1)}, u32[]{:S(2)}, u32[]{:S(2)}) collective-permute-start(f32[2,136,256]{2,1,0:T(8,128)S(1)} %get-tuple-element.11.refs_0_), channel_id=1, source_target_pairs={{0,8},{1,2},{2,1},{3,11},{4,12},{5,6},{6,5},{7,15},{8,0},{9,10},{1... | collective-permute-start | bytes 835592 | tf_op jit(solution)/shard_map/ppermute | solution.py:51
  4.3 1.6 %collective-permute-start.1 = (f32[2,136,256]{2,1,0:T(8,128)S(1)}, f32[2,136,256]{2,1,0:T(8,128)S(1)}, u32[]{:S(2)}, u32[]{:S(2)}) collective-permute-start(f32[2,136,256]{2,1,0:T(8,128)S(1)} %get-tuple-element.10.near_ref), channel_id=1, source_target_pairs={{0,1},{1,0},{2,3},{3,2},{4,5},{5,4},{6,7},{7,6},{8,9},{9,8},{10,11... | collective-permute-start | bytes 835592 | tf_op jit(solution)/shard_map/ppermute | solution.py:51
  4.3 0.7 %copy-start = (f32[128]{0:T(128)S(1)}, f32[128]{0:T(128)}, u32[]{:S(2)}) copy-start(f32[128]{0:T(128)} %param.13) | copy-start | bytes 1540
  5.0 0.7 %copy-start.1 = (f32[8]{0:T(128)S(1)}, f32[8]{0:T(128)}, u32[]{:S(2)}) copy-start(f32[8]{0:T(128)} %param.15) | copy-start | bytes 100
  5.0 0.7 %copy-start.2 = (s32[128]{0:T(128)S(1)}, s32[128]{0:T(128)}, u32[]{:S(2)}) copy-start(s32[128]{0:T(128)} %param.14) | copy-start | bytes 1540
  5.0 0.7 %copy-start.3 = (f32[8]{0:T(128)S(1)}, f32[8]{0:T(128)}, u32[]{:S(2)}) copy-start(f32[8]{0:T(128)} %param.17) | copy-start | bytes 100
  5.0 0.7 %copy-start.4 = (f32[8]{0:T(128)S(1)}, f32[8]{0:T(128)}, u32[]{:S(2)}) copy-start(f32[8]{0:T(128)} %param.16) | copy-start | bytes 100
  6.4 8.7 %collective-permute-start.3 = (f32[2,128,256]{2,1,0:T(8,128)S(1)}, f32[2,128,256]{2,1,0:T(8,128)S(1)}, u32[]{:S(2)}, u32[]{:S(2)}) collective-permute-start(f32[2,128,256]{2,1,0:T(8,128)S(1)} %shard_map.92.refs_3_.refs_0_), channel_id=1, source_target_pairs={{0,8},{1,9},{2,10},{3,11},{4,12},{5,13},{6,14},{7,15},{8,0},{9,1},... | collective-permute-start | bytes 786440 | tf_op jit(solution)/shard_map/ppermute | solution.py:51
  8.0 7.1 %collective-permute-start.4 = (f32[2,128,256]{2,1,0:T(8,128)S(1)}, f32[2,128,256]{2,1,0:T(8,128)S(1)}, u32[]{:S(2)}, u32[]{:S(2)}) collective-permute-start(f32[2,128,256]{2,1,0:T(8,128)S(1)} %shard_map.92.refs_3_.refs_0_), channel_id=1, source_target_pairs={{0,1},{1,0},{2,3},{3,2},{4,5},{5,4},{6,7},{7,6},{8,16},{9,17},{10,... | collective-permute-start | bytes 786440 | tf_op jit(solution)/shard_map/ppermute | solution.py:51
  9.3 8.4 %collective-permute-start.2 = (f32[2,128,256]{2,1,0:T(8,128)S(1)}, f32[2,128,256]{2,1,0:T(8,128)S(1)}, u32[]{:S(2)}, u32[]{:S(2)}) collective-permute-start(f32[2,128,256]{2,1,0:T(8,128)S(1)} %shard_map.93.refs_0_), channel_id=1, source_target_pairs={{0,4},{1,5},{2,6},{3,7},{4,0},{5,1},{6,2},{7,3},{8,12},{9,13},{10,... | collective-permute-start | bytes 786440 | tf_op jit(solution)/shard_map/ppermute | solution.py:51
  15.3 8.0 %collective-permute-start.7 = (f32[2,128,256]{2,1,0:T(8,128)S(1)}, f32[2,128,256]{2,1,0:T(8,128)S(1)}, u32[]{:S(2)}, u32[]{:S(2)}) collective-permute-start(f32[2,128,256]{2,1,0:T(8,128)S(1)} %shard_map.94.refs_2_), channel_id=1, source_target_pairs={{0,4},{1,5},{2,6},{3,7},{4,0},{5,1},{6,2},{7,3},{8,12},{9,13},{10,... | collective-permute-start | bytes 786440 | tf_op jit(solution)/shard_map/ppermute | solution.py:51
  17.8 7.5 %collective-permute-start.5 = (f32[2,128,256]{2,1,0:T(8,128)S(1)}, f32[2,128,256]{2,1,0:T(8,128)S(1)}, u32[]{:S(2)}, u32[]{:S(2)}) collective-permute-start(f32[2,128,256]{2,1,0:T(8,128)S(1)} %shard_map.95.refs_2_), channel_id=1, source_target_pairs={{0,8},{1,9},{2,10},{3,11},{4,12},{5,13},{6,14},{7,15},{8,0},{9,1},... | collective-permute-start | bytes 786440 | tf_op jit(solution)/shard_map/ppermute | solution.py:51
  19.9 5.4 %collective-permute-start.6 = (f32[2,128,256]{2,1,0:T(8,128)S(1)}, f32[2,128,256]{2,1,0:T(8,128)S(1)}, u32[]{:S(2)}, u32[]{:S(2)}) collective-permute-start(f32[2,128,256]{2,1,0:T(8,128)S(1)} %get-tuple-element.14), channel_id=1, source_target_pairs={{0,1},{1,0},{2,3},{3,2},{4,5},{5,4},{6,7},{7,6},{8,16},{9,17},{10,... | collective-permute-start | bytes 786440 | tf_op jit(solution)/shard_map/ppermute | solution.py:51

commit v7 on v6

--- a/solution.py
+++ b/solution.py
@@ -101,15 +101,14 @@
         for copy in copies:
             copy.start()
         for target, _, _, size in edges:
-            for r in range(EDGE):
-                target[r, size:, :] = jnp.zeros_like(target[r, size:, :])
+            target[1, size:, :] = jnp.zeros_like(target[1, size:, :])
         for copy in copies[rows:]:
             copy.wait()
         flow[2] = mask_rows[...].astype(jnp.float32)
         for target, at, _, size in edges:
             end = 0 if at == 0 else count - 1
-            for i in range(3):
-                target[0, size + i : size + i + 1, :] = flow[i, end : end + 1, :]
+            ends = [flow[i, end : end + 1, :] for i in range(3)]
+            target[0, size:, :] = jnp.concatenate(ends + [jnp.zeros((SUBLANES - 3, ends[0].shape[1]), jnp.float32)], 0)
         for copy in copies[:rows]:
             copy.wait()
 

time: 26.6 us -> 26.6 us (level)
  no operation moved by 1% of the time
where the time goes in v7:
time: 26.6 us; the launch traced here: 26.4 us
  starting transfers between devices  10.3 us (39%)
  waiting for transfers between devices  9.19 us (35%)
  Pallas kernels  4.97 us (19%)
  local copies, waits for them, and re-layouts  1.51 us (6%)
  other arithmetic  0.3 us (1%)
    ppermute x8, starting transfers between devices, exchange(): return lax.ppermute(value, ('bins', 'xy'), pairs)  10.3 us
    ppermute x8, waiting for transfers between devices, exchange(): return lax.ppermute(value, ('bins', 'xy'), pairs)  9.19 us
    pallas_call x2, Pallas kernels, collide(): pl.pallas_call(functools.partial(collide_kernel, chunks), out_shape=pltpu...  2.21 us
    unnamed x10, local copies, waits for them, and re-layouts  1.33 us
    pallas_call x1, Pallas kernels, load(): pl.pallas_call(load_kernel, out_shape=(edge(bins), *[edge(bins // PARTS)]...  1.16 us
    pallas_call x2, Pallas kernels, horizontal(): pl.pallas_call(functools.partial(horizontal_kernel, low is None, low), ou...  1.08 us
  transfers between devices with their start and end apart: 8, of which 5 were waited for; matrix products, arithmetic and copies ran while one was open for 2% of the time, Pallas kernels for 10%

profile of v7, /device:TPU:0, one launch (start us, length us, event | category | flops | bytes accessed | tf_op | source)
XLA Modules:
  0.0 26.4 jit_solution(1114299279661858749)
XLA Ops:
  0.0 1.2 %shard_map.91 = (f32[2,136,256]{2,1,0:T(8,128)S(1)}, f32[2,136,256]{2,1,0:T(8,128)S(1)}, f32[3,4,256]{2,1,0:T(4,128)S(1)}) custom-call(f32[1,128,4,256]{3,2,1,0:T(4,128)} %conc.1, f32[1,4,256]{2,1,0:T(4,128)} %vel_x.1, f32[1,4,256]{2,1,0:T(4,128)} %vel_y.1, s32[4,256]{1,0:T(4,128)} %mask.1), custom_call_target="tpu_custom_call" | custom-call | tf_op jit(solution)/shard_map/pallas_call | solution.py:125
  1.2 3.1 %collective-permute-start = (f32[2,136,256]{2,1,0:T(8,128)S(1)}, f32[2,136,256]{2,1,0:T(8,128)S(1)}, u32[]{:S(2)}, u32[]{:S(2)}) collective-permute-start(f32[2,136,256]{2,1,0:T(8,128)S(1)} %get-tuple-element.11.refs_0_), channel_id=1, source_target_pairs={{0,8},{1,2},{2,1},{3,11},{4,12},{5,6},{6,5},{7,15},{8,0},{9,10},{1... | collective-permute-start | bytes 835592 | tf_op jit(solution)/shard_map/ppermute | solution.py:51
  4.3 0.7 %copy-done = f32[128]{0:T(128)S(1)} copy-done((f32[128]{0:T(128)S(1)}, f32[128]{0:T(128)}, u32[]{:S(2)}) %copy-start) | copy-done | bytes 536
  5.0 0.6 %copy-done.1 = f32[8]{0:T(128)S(1)} copy-done((f32[8]{0:T(128)S(1)}, f32[8]{0:T(128)}, u32[]{:S(2)}) %copy-start.1) | copy-done | bytes 56
  5.7 0.1 select_reduce_fusion.1
  5.8 0.5 %shard_map.92.refs_3_.refs_0_ = f32[2,128,256]{2,1,0:T(8,128)S(1)} custom-call(f32[2,136,256]{2,1,0:T(8,128)S(1)} %get-tuple-element.10.near_ref, f32[2,136,256]{2,1,0:T(8,128)S(1)} %get-tuple-element.11.refs_0_, f32[2,136,256]{2,1,0:T(8,128)S(1)} %collective-permute-done.1.refs_1_, f32[3,4,256]{2,1,0:T(4,128)S(1)} %get-tuple-element.12.refs_2_), custom_call_target="tpu_custom_call" | custom-call | flops 1769472 | bytes 1048576 | tf_op jit(solution)/shard_map/pallas_call | solution.py:210
  6.4 1.6 %collective-permute-start.3 = (f32[2,128,256]{2,1,0:T(8,128)S(1)}, f32[2,128,256]{2,1,0:T(8,128)S(1)}, u32[]{:S(2)}, u32[]{:S(2)}) collective-permute-start(f32[2,128,256]{2,1,0:T(8,128)S(1)} %shard_map.92.refs_3_.refs_0_), channel_id=1, source_target_pairs={{0,8},{1,9},{2,10},{3,11},{4,12},{5,13},{6,14},{7,15},{8,0},{9,1},... | collective-permute-start | bytes 786440 | tf_op jit(solution)/shard_map/ppermute | solution.py:51
  8.0 0.8 %collective-permute-done.refs_1_ = f32[2,136,256]{2,1,0:T(8,128)S(1)} collective-permute-done((f32[2,136,256]{2,1,0:T(8,128)S(1)}, f32[2,136,256]{2,1,0:T(8,128)S(1)}, u32[]{:S(2)}, u32[]{:S(2)}) %collective-permute-start) | collective-permute-done | bytes 278560 | tf_op jit(solution)/shard_map/ppermute | solution.py:51
  8.8 0.5 %shard_map.93.refs_0_ = f32[2,128,256]{2,1,0:T(8,128)S(1)} custom-call(f32[2,136,256]{2,1,0:T(8,128)S(1)} %get-tuple-element.10.near_ref, f32[2,136,256]{2,1,0:T(8,128)S(1)} %get-tuple-element.11.refs_0_, f32[2,136,256]{2,1,0:T(8,128)S(1)} %collective-permute-done.refs_1_, f32[3,4,256]{2,1,0:T(4,128)S(1)} %get-tuple-element.12.refs_2_, ...), custom_call_target="tpu_custom_call" | custom-call | flops 1769472 | bytes 1048576 | tf_op jit(solution)/shard_map/pallas_call | solution.py:210
  9.3 2.0 %collective-permute-start.2 = (f32[2,128,256]{2,1,0:T(8,128)S(1)}, f32[2,128,256]{2,1,0:T(8,128)S(1)}, u32[]{:S(2)}, u32[]{:S(2)}) collective-permute-start(f32[2,128,256]{2,1,0:T(8,128)S(1)} %shard_map.93.refs_0_), channel_id=1, source_target_pairs={{0,4},{1,5},{2,6},{3,7},{4,0},{5,1},{6,2},{7,3},{8,12},{9,13},{10,... | collective-permute-start | bytes 786440 | tf_op jit(solution)/shard_map/ppermute | solution.py:51
  11.4 0.1 copy.23
  11.5 3.5 %collective-permute-done.3.refs_1_ = f32[2,128,256]{2,1,0:T(8,128)S(1)} collective-permute-done((f32[2,128,256]{2,1,0:T(8,128)S(1)}, f32[2,128,256]{2,1,0:T(8,128)S(1)}, u32[]{:S(2)}, u32[]{:S(2)}) %collective-permute-start.3) | collective-permute-done | bytes 262176 | tf_op jit(solution)/shard_map/ppermute | solution.py:51
  15.1 0.2 shard_map.94.refs_2_
  15.3 1.6 %collective-permute-start.7 = (f32[2,128,256]{2,1,0:T(8,128)S(1)}, f32[2,128,256]{2,1,0:T(8,128)S(1)}, u32[]{:S(2)}, u32[]{:S(2)}) collective-permute-start(f32[2,128,256]{2,1,0:T(8,128)S(1)} %shard_map.94.refs_2_), channel_id=1, source_target_pairs={{0,4},{1,5},{2,6},{3,7},{4,0},{5,1},{6,2},{7,3},{8,12},{9,13},{10,... | collective-permute-start | bytes 786440 | tf_op jit(solution)/shard_map/ppermute | solution.py:51
  16.8 0.9 %collective-permute-done.2.refs_1_ = f32[2,128,256]{2,1,0:T(8,128)S(1)} collective-permute-done((f32[2,128,256]{2,1,0:T(8,128)S(1)}, f32[2,128,256]{2,1,0:T(8,128)S(1)}, u32[]{:S(2)}, u32[]{:S(2)}) %collective-permute-start.2) | collective-permute-done | bytes 262176 | tf_op jit(solution)/shard_map/ppermute | solution.py:51
  17.7 0.1 shard_map.95.refs_2_
  17.8 1.9 %collective-permute-start.5 = (f32[2,128,256]{2,1,0:T(8,128)S(1)}, f32[2,128,256]{2,1,0:T(8,128)S(1)}, u32[]{:S(2)}, u32[]{:S(2)}) collective-permute-start(f32[2,128,256]{2,1,0:T(8,128)S(1)} %shard_map.95.refs_2_), channel_id=1, source_target_pairs={{0,8},{1,9},{2,10},{3,11},{4,12},{5,13},{6,14},{7,15},{8,0},{9,1},... | collective-permute-start | bytes 786440 | tf_op jit(solution)/shard_map/ppermute | solution.py:51
  19.7 0.2 shard_map.96
  19.9 0.1 collective-permute-start.6
  20.0 0.1 subtract_multiply_fusion
  20.2 3.1 %collective-permute-done.7.refs_3_ = f32[2,128,256]{2,1,0:T(8,128)S(1)} collective-permute-done((f32[2,128,256]{2,1,0:T(8,128)S(1)}, f32[2,128,256]{2,1,0:T(8,128)S(1)}, u32[]{:S(2)}, u32[]{:S(2)}) %collective-permute-start.7) | collective-permute-done | bytes 262176 | tf_op jit(solution)/shard_map/ppermute | solution.py:51
  23.3 1.2 %shard_map.97.refs_3_ = f32[1,128,4,256]{3,2,1,0:T(4,128)} custom-call(f32[128,128]{1,0:T(8,128)S(1)} %pad.4.table_ref, bf16[256,384]{1,0:T(8,128)(2,1)S(1)} %pad_maximum_fusion.both_ref, f32[2,128,256]{2,1,0:T(8,128)S(1)} %shard_map.92.refs_3_.refs_0_, f32[2,128,256]{2,1,0:T(8,128)S(1)} %collective-permute-done.3.refs_1_, ...), custom_call_target="tpu_custom_call" | custom-call | flops 100663296 | bytes 1572864 | tf_op jit(solution)/shard_map/pallas_call | solution.py:303
  24.5 0.9 %collective-permute-done.5.refs_1_ = f32[2,128,256]{2,1,0:T(8,128)S(1)} collective-permute-done((f32[2,128,256]{2,1,0:T(8,128)S(1)}, f32[2,128,256]{2,1,0:T(8,128)S(1)}, u32[]{:S(2)}, u32[]{:S(2)}) %collective-permute-start.5) | collective-permute-done | bytes 262176 | tf_op jit(solution)/shard_map/ppermute | solution.py:51
  25.3 1.1 %shard_map.98 = f32[1,128,4,256]{3,2,1,0:T(4,128)} custom-call(f32[128,128]{1,0:T(8,128)S(1)} %pad.4.table_ref, bf16[256,384]{1,0:T(8,128)(2,1)S(1)} %pad_maximum_fusion.both_ref, f32[2,128,256]{2,1,0:T(8,128)S(1)} %get-tuple-element.13.refs_0_, f32[2,128,256]{2,1,0:T(8,128)S(1)} %collective-permute-done.5.refs_1_, ...), custom_call_target="tpu_custom_call", output_to_operand_aliasing={{}: (5, {})} | custom-call | flops 100663296 | bytes 1572864 | tf_op jit(solution)/shard_map/pallas_call | solution.py:303
  (24 shorter events, 0.3 us)
Async XLA Ops:
  1.2 7.6 %collective-permute-start = (f32[2,136,256]{2,1,0:T(8,128)S(1)}, f32[2,136,256]{2,1,0:T(8,128)S(1)}, u32[]{:S(2)}, u32[]{:S(2)}) collective-permute-start(f32[2,136,256]{2,1,0:T(8,128)S(1)} %get-tuple-element.11.refs_0_), channel_id=1, source_target_pairs={{0,8},{1,2},{2,1},{3,11},{4,12},{5,6},{6,5},{7,15},{8,0},{9,10},{1... | collective-permute-start | bytes 835592 | tf_op jit(solution)/shard_map/ppermute | solution.py:51
  4.3 1.6 %collective-permute-start.1 = (f32[2,136,256]{2,1,0:T(8,128)S(1)}, f32[2,136,256]{2,1,0:T(8,128)S(1)}, u32[]{:S(2)}, u32[]{:S(2)}) collective-permute-start(f32[2,136,256]{2,1,0:T(8,128)S(1)} %get-tuple-element.10.near_ref), channel_id=1, source_target_pairs={{0,1},{1,0},{2,3},{3,2},{4,5},{5,4},{6,7},{7,6},{8,9},{9,8},{10,11... | collective-permute-start | bytes 835592 | tf_op jit(solution)/shard_map/ppermute | solution.py:51
  4.3 0.7 %copy-start = (f32[128]{0:T(128)S(1)}, f32[128]{0:T(128)}, u32[]{:S(2)}) copy-start(f32[128]{0:T(128)} %param.13) | copy-start | bytes 1540
  5.0 0.7 %copy-start.1 = (f32[8]{0:T(128)S(1)}, f32[8]{0:T(128)}, u32[]{:S(2)}) copy-start(f32[8]{0:T(128)} %param.15) | copy-start | bytes 100
  5.0 0.7 %copy-start.2 = (s32[128]{0:T(128)S(1)}, s32[128]{0:T(128)}, u32[]{:S(2)}) copy-start(s32[128]{0:T(128)} %param.14) | copy-start | bytes 1540
  5.0 0.7 %copy-start.3 = (f32[8]{0:T(128)S(1)}, f32[8]{0:T(128)}, u32[]{:S(2)}) copy-start(f32[8]{0:T(128)} %param.17) | copy-start | bytes 100
  5.0 0.7 %copy-start.4 = (f32[8]{0:T(128)S(1)}, f32[8]{0:T(128)}, u32[]{:S(2)}) copy-start(f32[8]{0:T(128)} %param.16) | copy-start | bytes 100
  6.4 8.7 %collective-permute-start.3 = (f32[2,128,256]{2,1,0:T(8,128)S(1)}, f32[2,128,256]{2,1,0:T(8,128)S(1)}, u32[]{:S(2)}, u32[]{:S(2)}) collective-permute-start(f32[2,128,256]{2,1,0:T(8,128)S(1)} %shard_map.92.refs_3_.refs_0_), channel_id=1, source_target_pairs={{0,8},{1,9},{2,10},{3,11},{4,12},{5,13},{6,14},{7,15},{8,0},{9,1},... | collective-permute-start | bytes 786440 | tf_op jit(solution)/shard_map/ppermute | solution.py:51
  8.0 7.1 %collective-permute-start.4 = (f32[2,128,256]{2,1,0:T(8,128)S(1)}, f32[2,128,256]{2,1,0:T(8,128)S(1)}, u32[]{:S(2)}, u32[]{:S(2)}) collective-permute-start(f32[2,128,256]{2,1,0:T(8,128)S(1)} %shard_map.92.refs_3_.refs_0_), channel_id=1, source_target_pairs={{0,1},{1,0},{2,3},{3,2},{4,5},{5,4},{6,7},{7,6},{8,16},{9,17},{10,... | collective-permute-start | bytes 786440 | tf_op jit(solution)/shard_map/ppermute | solution.py:51
  9.3 8.4 %collective-permute-start.2 = (f32[2,128,256]{2,1,0:T(8,128)S(1)}, f32[2,128,256]{2,1,0:T(8,128)S(1)}, u32[]{:S(2)}, u32[]{:S(2)}) collective-permute-start(f32[2,128,256]{2,1,0:T(8,128)S(1)} %shard_map.93.refs_0_), channel_id=1, source_target_pairs={{0,4},{1,5},{2,6},{3,7},{4,0},{5,1},{6,2},{7,3},{8,12},{9,13},{10,... | collective-permute-start | bytes 786440 | tf_op jit(solution)/shard_map/ppermute | solution.py:51
  15.3 8.0 %collective-permute-start.7 = (f32[2,128,256]{2,1,0:T(8,128)S(1)}, f32[2,128,256]{2,1,0:T(8,128)S(1)}, u32[]{:S(2)}, u32[]{:S(2)}) collective-permute-start(f32[2,128,256]{2,1,0:T(8,128)S(1)} %shard_map.94.refs_2_), channel_id=1, source_target_pairs={{0,4},{1,5},{2,6},{3,7},{4,0},{5,1},{6,2},{7,3},{8,12},{9,13},{10,... | collective-permute-start | bytes 786440 | tf_op jit(solution)/shard_map/ppermute | solution.py:51
  17.8 7.5 %collective-permute-start.5 = (f32[2,128,256]{2,1,0:T(8,128)S(1)}, f32[2,128,256]{2,1,0:T(8,128)S(1)}, u32[]{:S(2)}, u32[]{:S(2)}) collective-permute-start(f32[2,128,256]{2,1,0:T(8,128)S(1)} %shard_map.95.refs_2_), channel_id=1, source_target_pairs={{0,8},{1,9},{2,10},{3,11},{4,12},{5,13},{6,14},{7,15},{8,0},{9,1},... | collective-permute-start | bytes 786440 | tf_op jit(solution)/shard_map/ppermute | solution.py:51
  19.9 5.4 %collective-permute-start.6 = (f32[2,128,256]{2,1,0:T(8,128)S(1)}, f32[2,128,256]{2,1,0:T(8,128)S(1)}, u32[]{:S(2)}, u32[]{:S(2)}) collective-permute-start(f32[2,128,256]{2,1,0:T(8,128)S(1)} %get-tuple-element.14), channel_id=1, source_target_pairs={{0,1},{1,0},{2,3},{3,2},{4,5},{5,4},{6,7},{7,6},{8,16},{9,17},{10,... | collective-permute-start | bytes 786440 | tf_op jit(solution)/shard_map/ppermute | solution.py:51
